TPU v7x, 128 devices: a whole 4x4x4 slice. The times are simulated.
128 devices in a mesh: lat: 8 (over y_lo, z), lon: 16 (over x, y_hi, core).
Axes of the slice: x: 4, y: 4 (y_hi: 2, y_lo: 2; y = y_hi * 2 + y_lo), z: 4, core: 2. Of those that a mesh axis runs over, the one named last changes fastest.
Arguments:
- queries: bfloat16 [2, 384, 384, 512], P(None, 'lat', 'lon'), may hold values from -160 to 160
- key_tokens: bfloat16 [2, 384, 384, 512], P(None, 'lat', 'lon'), may hold values from -6 to 6
- value_tokens: bfloat16 [2, 384, 384, 512], P(None, 'lat', 'lon'), may hold values from -6 to 6
- out_grad: bfloat16 [2, 384, 384, 512], P(None, 'lat', 'lon'), may hold values from -6 to 6
- land_mask: int32 [384, 384], P('lat', 'lon'), may hold values 0 or 1
- land_embed: float32 [512], replicated, may hold values from -4 to 4
- rel_table: float32 [8, 759], replicated, may hold values from -4 to 4
Outputs:
- attended: bfloat16 [2, 384, 384, 512], P(None, 'lat', 'lon')
- grad_queries: bfloat16 [2, 384, 384, 512], P(None, 'lat', 'lon')
- grad_keys: bfloat16 [2, 384, 384, 512], P(None, 'lat', 'lon')
- grad_values: bfloat16 [2, 384, 384, 512], P(None, 'lat', 'lon')
All inputs are finite; a program needn't handle non-finite values. No bound on the sum of `land_mask` on one device may be relied on, other than what follows from the above.
Results may differ from a plain program's by a relative error of at most 0.034.
The roundings to bfloat16 on the way count: a program that leaves them out, or rounds other values in their place, can miss the bound.
Values may be sent and summed in bfloat16 or wider, within the bound.
A program may use at most 256 MiB of HBM per device.

v0:
```python
import jax
import jax.numpy as jnp
from jax import lax
from jax.sharding import PartitionSpec as P


def shifted(block, axis, distance):
    devices = range(lax.axis_size(axis))
    route = [((i - distance) % len(devices), i) for i in devices]
    return lax.ppermute(block, axis, route)


def one_hot_offsets(length, count, offset):
    pos = jnp.arange(length)
    diff = pos[:, None] - pos[None, :] + offset
    return (jnp.arange(count)[:, None, None] == diff[None]).astype(jnp.float32)


def relative_bias(rel_table):
    heads = rel_table.shape[0]
    table = rel_table.reshape(heads, 3, 11, 23)
    best = lax.Precision.HIGHEST
    first = jnp.einsum("hxyz,zab->hxyab", table, one_hot_offsets(12, 23, 11), precision=best)
    second = jnp.einsum("hxyab,ycd->hxcdab", first, one_hot_offsets(6, 11, 5), precision=best)
    third = jnp.einsum("hxcdab,xef->hefcdab", second, one_hot_offsets(2, 3, 1), precision=best)
    return third.transpose(0, 1, 3, 5, 2, 4, 6).reshape(heads, 144, 144)


def attend(query, keyed, valued, grad_out, bias, keep):
    count, tokens, width = query.shape
    heads = bias.shape[0]
    size = width // heads
    scale = float(size) ** (-0.5)
    q_heads = query.reshape(count, tokens, heads, size)
    k_heads = keyed.reshape(count, tokens, heads, size)
    v_heads = valued.reshape(count, tokens, heads, size)
    g_heads = grad_out.reshape(count, tokens, heads, size)
    f32 = jnp.float32
    scores = (
        jnp.einsum("wihc,wjhc->whij", q_heads, k_heads, preferred_element_type=f32) * scale
        + bias[None]
    )
    scores = jnp.where(keep[:, None], scores, -jnp.inf)
    peak = jnp.max(scores, axis=-1, keepdims=True)
    expo = jnp.exp(scores - peak)
    probs = expo / jnp.sum(expo, axis=-1, keepdims=True)
    probs_low = probs.astype(jnp.bfloat16)
    attended = jnp.einsum("whij,wjhc->wihc", probs_low, v_heads, preferred_element_type=f32).astype(
        jnp.bfloat16
    )
    grad_probs = jnp.einsum("wihc,wjhc->whij", g_heads, v_heads, preferred_element_type=f32)
    delta = jnp.einsum("wihc,wihc->whi", g_heads.astype(f32), attended.astype(f32))
    grad_scores = (probs * (grad_probs - delta[..., None])).astype(jnp.bfloat16)
    grad_query = (
        jnp.einsum("whij,wjhc->wihc", grad_scores, k_heads, preferred_element_type=f32) * scale
    ).astype(jnp.bfloat16)
    grad_key = (
        jnp.einsum("whij,wihc->wjhc", grad_scores, q_heads, preferred_element_type=f32) * scale
    ).astype(jnp.bfloat16)
    grad_value = jnp.einsum(
        "whij,wihc->wjhc", probs_low, g_heads, preferred_element_type=f32
    ).astype(jnp.bfloat16)
    shape = (count, tokens, width)
    return (
        attended.reshape(shape),
        grad_query.reshape(shape),
        grad_key.reshape(shape),
        grad_value.reshape(shape),
    )


def window_pass(arrays, first_row, total_rows, bias):
    lev, rows, cols, width = arrays[0].shape
    bands = rows // 6
    groups = cols // 12

    def to_windows(array):
        return (
            array.reshape(lev, bands, 6, groups, 12, width)
            .transpose(1, 3, 0, 2, 4, 5)
            .reshape(bands * groups, lev * 72, width)
        )

    def from_windows(array):
        return (
            array.reshape(bands, groups, lev, 6, 12, width)
            .transpose(2, 0, 3, 1, 4, 5)
            .reshape(lev, rows, cols, width)
        )

    parts = [to_windows(array) for array in arrays]
    row_of = jnp.arange(72 * lev) // 12 % 6
    band_of = jnp.arange(bands * groups) // groups
    global_row = first_row + band_of[:, None] * 6 + row_of[None, :]
    region = (global_row < 0) | (global_row >= total_rows)
    keep = region[:, :, None] == region[:, None, :]
    outputs = attend(parts[0], parts[1], parts[2], parts[3], bias, keep)
    return tuple((from_windows(output) for output in outputs))


def shards(queries, key_tokens, value_tokens, out_grad, land_mask, land_embed, rel_table):
    lev, rows, cols, width = queries.shape
    keyed = (
        key_tokens.astype(jnp.float32)
        + land_mask.astype(jnp.float32)[None, :, :, None] * land_embed
    ).astype(jnp.bfloat16)
    arrays = (queries, keyed, value_tokens, out_grad)
    bias = relative_bias(rel_table)
    total_rows = lax.axis_size("lat") * rows
    anchor = lax.axis_index("lat") * rows
    below = shifted((queries[:, :3], keyed[:, :3], value_tokens[:, :3], out_grad[:, :3]), "lat", -1)
    tall = [jnp.concatenate([whole, extra], axis=1) for whole, extra in zip(arrays, below)]
    beside = shifted(
        (tall[0][:, :, :6], tall[1][:, :, :6], tall[2][:, :, :6], tall[3][:, :, :6]), "lon", -1
    )
    extended = tuple(
        (
            jnp.concatenate([whole[:, 3:, 6:], extra[:, 3:]], axis=2)
            for whole, extra in zip(tall, beside)
        )
    )
    results = window_pass(extended, anchor + 3, total_rows, bias)
    side_back = shifted(
        (
            results[0][:, :, cols - 6 :],
            results[1][:, :, cols - 6 :],
            results[2][:, :, cols - 6 :],
            results[3][:, :, cols - 6 :],
        ),
        "lon",
        1,
    )
    widened = [
        jnp.concatenate([extra, whole[:, :, : cols - 6]], axis=2)
        for whole, extra in zip(results, side_back)
    ]
    rows_returned = shifted(
        (
            widened[0][:, rows - 3 :],
            widened[1][:, rows - 3 :],
            widened[2][:, rows - 3 :],
            widened[3][:, rows - 3 :],
        ),
        "lat",
        1,
    )
    final = [
        jnp.concatenate([extra, whole[:, : rows - 3]], axis=1)
        for whole, extra in zip(widened, rows_returned)
    ]
    return (final[0], final[1], final[2], final[3])


def solution(mesh):
    in_specs = (
        P(None, "lat", "lon", None),
        P(None, "lat", "lon", None),
        P(None, "lat", "lon", None),
        P(None, "lat", "lon", None),
        P("lat", "lon"),
        P(),
        P(),
    )
    out_specs = (
        P(None, "lat", "lon", None),
        P(None, "lat", "lon", None),
        P(None, "lat", "lon", None),
        P(None, "lat", "lon", None),
    )
    return jax.shard_map(shards, mesh=mesh, in_specs=in_specs, out_specs=out_specs, check_vma=False)
```

profile of v0, /device:TPU:17, one launch (start us, length us, event | category | flops | bytes accessed | tf_op | source)
XLA Modules:
  0.0 394.7 jit_solution(11088004703701836908)
XLA Ops:
  1.8 4.5 %collective-permute-start.8 = (bf16[2,3,24,512]{3,1,2,0:T(4,128)(2,1)S(1)}, bf16[2,3,24,512]{3,1,2,0:T(4,128)(2,1)S(1)}, u32[]{:S(2)}, u32[]{:S(2)}) collective-permute-start(bf16[2,3,24,512]{3,1,2,0:T(4,128)(2,1)S(1)} %copy.136), channel_id=1, source_target_pairs={{16,0},{32,16},{48,32},{64,48},{80,64},{96,80},{112,96},{0,112},{1... | collective-permute-start | bytes 442376 | tf_op jit(solution)/shard_map/ppermute | solution.py:10
  22.9 10.3 %convolution_bitcast_fusion.1 = f32[8,3,6,6,12,12]{5,3,4,1,0,2:T(8,128)S(1)} fusion(f32[8,3,11,12,12,1]{2,4,1,0,3,5:T(8,128)S(1)} %convolution_bitcast_fusion.2, s32[6,6]{1,0:T(8,128)S(1)} %subtract_add_fusion.1), kind=kOutput, calls=%fused_computation.22 | convolution fusion | flops 16423308 | bytes 649872 | tf_op jit(solution)/shard_map/hxyab,ycd->hxcdab/dot_general | solution.py:24
  33.2 14.4 %convolution_bitcast_fusion = f32[8,2,6,12,2,6,12]{6,4,3,5,2,0,1:T(2,128)} fusion(f32[8,3,6,6,12,12]{5,3,4,1,0,2:T(8,128)S(1)} %convolution_bitcast_fusion.1, s32[2,2]{1,0:T(2,128)S(1)} %subtract_add_fusion.2), kind=kOutput, calls=%fused_computation.14 | convolution fusion | flops 5971980 | bytes 1161232 | tf_op jit(solution)/shard_map/hxcdab,xef->hefcdab/dot_general | solution.py:25
  58.0 15.4 %copy.122 = f32[8,2,6,12,2,6,12]{3,2,1,6,5,4,0:T(8,128)} copy(f32[8,2,6,12,2,6,12]{6,4,3,5,2,0,1:T(2,128)} %convolution_bitcast_fusion) | data formatting | bytes 1327104 | tf_op jit(solution)/shard_map/add | solution.py:40
  73.4 6.6 %reshape.198 = f32[8,144,144]{1,2,0:T(8,128)S(1)} reshape(f32[8,2,6,12,2,6,12]{3,2,1,6,5,4,0:T(8,128)} %copy.122) | data formatting | bytes 1327104 | tf_op jit(solution)/shard_map/add | solution.py:40
  105.3 4.9 %reshape_reshape.26 = bf16[16,144,8,64]{3,2,0,1:T(8,128)(2,1)} reshape(bf16[8,2,2,6,12,512]{5,1,0,4,3,2:T(2,128)(2,1)S(1)} %copy.71) | data formatting | bytes 4718592 | tf_op jit(solution)/shard_map/reshape;reshape | solution.py:35
  110.2 8.5 %copy.73 = bf16[16,144,8,64]{1,3,2,0:T(8,128)(2,1)} copy(bf16[16,144,8,64]{3,2,0,1:T(8,128)(2,1)} %reshape_reshape.26) | data formatting | bytes 4718592 | tf_op jit(solution)/shard_map/reshape;reshape | solution.py:35
  123.8 4.7 %reshape_reshape.25 = bf16[16,144,8,64]{3,2,0,1:T(8,128)(2,1)} reshape(bf16[8,2,2,6,12,512]{5,1,0,4,3,2:T(2,128)(2,1)S(1)} %copy.68) | data formatting | bytes 4718592 | tf_op jit(solution)/shard_map/reshape;reshape | solution.py:34
  128.5 8.5 %copy.72 = bf16[16,144,8,64]{1,3,2,0:T(8,128)(2,1)} copy(bf16[16,144,8,64]{3,2,0,1:T(8,128)(2,1)} %reshape_reshape.25) | data formatting | bytes 4718592 | tf_op jit(solution)/shard_map/reshape;reshape | solution.py:34
  142.1 4.7 %reshape_reshape.28 = bf16[16,144,8,64]{3,2,0,1:T(8,128)(2,1)} reshape(bf16[8,2,2,6,12,512]{5,1,0,4,3,2:T(2,128)(2,1)S(1)} %copy.85) | data formatting | bytes 4718592 | tf_op jit(solution)/shard_map/reshape;reshape | solution.py:37
  146.8 8.5 %copy.86 = bf16[16,144,8,64]{1,3,2,0:T(8,128)(2,1)} copy(bf16[16,144,8,64]{3,2,0,1:T(8,128)(2,1)} %reshape_reshape.28) | data formatting | bytes 4718592 | tf_op jit(solution)/shard_map/reshape;reshape | solution.py:37
  155.4 7.4 %bitcast_convert_fusion = f32[16,8,144,64]{3,1,0,2:T(8,128)} fusion(bf16[16,144,8,64]{3,2,0,1:T(8,128)(2,1)} %reshape_reshape.28), kind=kLoop, calls=%fused_computation.17 | loop fusion | flops 1179648 | bytes 7077888
  169.4 4.7 %reshape_reshape.24 = bf16[16,144,8,64]{3,2,0,1:T(8,128)(2,1)} reshape(bf16[8,2,2,6,12,512]{5,1,0,4,3,2:T(2,128)(2,1)S(1)} %copy.64) | data formatting | bytes 4718592 | tf_op jit(solution)/shard_map/reshape;reshape | solution.py:36
  174.0 8.3 %copy.78 = bf16[16,144,8,64]{1,3,2,0:T(8,128)(2,1)} copy(bf16[16,144,8,64]{3,2,0,1:T(8,128)(2,1)} %reshape_reshape.24) | data formatting | bytes 4718592 | tf_op jit(solution)/shard_map/reshape;reshape | solution.py:36
  182.4 11.2 %copy.116 = f32[16,8,144,64]{2,3,1,0:T(8,128)} copy(f32[16,8,144,64]{3,1,0,2:T(8,128)} %bitcast_convert_fusion) | data formatting | bytes 9437184
  193.6 13.4 %fusion.35 = (f32[16,8,144]{2,1,0:T(8,128)S(1)}, f32[16,8,144,144]{2,3,1,0:T(8,128)}) fusion(f32[8,144,144]{1,2,0:T(8,128)S(1)} %reshape.198, pred[16,144,144]{1,2,0:T(8,128)(4,1)S(1)} %copy-done.16, bf16[16,144,8,64]{1,3,2,0:T(8,128)(2,1)} %copy.72, bf16[16,144,8,64]{1,3,2,0:T(8,128)(2,1)} %copy.73), kind=kOutput, calls=%fused_computation.85 | convolution fusion | flops 353009792 | bytes 16404480 | tf_op jit(solution)/shard_map/sub | solution.py:45
  207.1 7.8 %fusion.6 = bf16[16,8,144,144]{2,3,1,0:T(8,128)(2,1)S(1)} fusion(f32[16,8,144,144]{2,3,1,0:T(8,128)} %get-tuple-element.13, f32[16,8,144]{2,1,0:T(8,128)S(1)} %get-tuple-element.12), kind=kLoop, calls=%fused_computation.13 | loop fusion | flops 5308416 | bytes 15998976 | tf_op jit(solution)/shard_map/convert_element_type | solution.py:47
  214.9 11.5 %multiply_reduce_fusion = (f32[16,8,144]{2,1,0:T(8,128)S(1)}, bf16[16,8,64,144]{3,2,1,0:T(8,128)(2,1)}) fusion(f32[16,8,144,64]{2,3,1,0:T(8,128)} %copy.116, bf16[16,144,8,64]{1,3,2,0:T(8,128)(2,1)} %copy.78, bf16[16,8,144,144]{2,3,1,0:T(8,128)(2,1)S(1)} %fusion.6), kind=kOutput, calls=%fused_computation.10 | convolution fusion | flops 344438784 | bytes 14819328 | tf_op jit(solution)/shard_map/whij,wjhc->wihc/dot_general | solution.py:48
  226.4 13.9 %multiply_convert_fusion = bf16[16,8,144,144]{2,3,1,0:T(8,128)(2,1)} fusion(f32[16,8,144]{2,1,0:T(8,128)S(1)} %get-tuple-element.14, bf16[16,144,8,64]{1,3,2,0:T(8,128)(2,1)} %copy.86, bf16[16,144,8,64]{1,3,2,0:T(8,128)(2,1)} %copy.78, f32[16,8,144,144]{2,3,1,0:T(8,128)} %get-tuple-element.13, f32[16,8,144]{2,1,0:T(8,128)S(1)} %get-tuple-element.12), kind=kOutput, calls=%fused_computation.1 | convolution fusion | flops 350355456 | bytes 20791296 | tf_op jit(solution)/shard_map/wihc,wjhc->whij/dot_general | solution.py:51
  240.4 10.1 %fusion.10 = bf16[16,144,8,64]{1,3,2,0:T(8,128)(2,1)} fusion(bf16[16,144,8,64]{1,3,2,0:T(8,128)(2,1)} %copy.72, bf16[16,8,144,144]{2,3,1,0:T(8,128)(2,1)} %multiply_convert_fusion), kind=kOutput, calls=%fused_computation.20 | convolution fusion | flops 342097920 | bytes 10027008 | tf_op jit(solution)/shard_map/whij,wihc->wjhc/dot_general | solution.py:58
  250.5 8.3 %fusion.9 = bf16[16,144,8,64]{1,3,2,0:T(8,128)(2,1)} fusion(bf16[16,144,8,64]{1,3,2,0:T(8,128)(2,1)} %copy.73, bf16[16,8,144,144]{2,3,1,0:T(8,128)(2,1)} %multiply_convert_fusion), kind=kOutput, calls=%fused_computation.19 | convolution fusion | flops 342097920 | bytes 10027008 | tf_op jit(solution)/shard_map/whij,wjhc->wihc/dot_general | solution.py:55
  258.8 8.4 %copy.80 = bf16[16,144,8,64]{3,2,0,1:T(8,128)(2,1)} copy(bf16[16,144,8,64]{1,3,2,0:T(8,128)(2,1)} %bitcast.99) | data formatting | bytes 4718592 | tf_op jit(solution)/shard_map/convert_element_type | solution.py:48
  267.1 7.0 %reshape_reshape.27 = bf16[8,2,2,6,12,512]{5,1,0,4,3,2:T(2,128)(2,1)S(1)} reshape(bf16[16,144,8,64]{3,2,0,1:T(8,128)(2,1)} %copy.80) | data formatting | bytes 4718592 | tf_op jit(solution)/shard_map/reshape;reshape | solution.py:86
  277.9 8.4 %copy.91 = bf16[16,144,8,64]{3,2,0,1:T(8,128)(2,1)} copy(bf16[16,144,8,64]{1,3,2,0:T(8,128)(2,1)} %fusion.9) | data formatting | bytes 4718592 | tf_op jit(solution)/shard_map/convert_element_type | solution.py:56
  286.3 7.1 %reshape_reshape.29 = bf16[8,2,2,6,12,512]{5,1,0,4,3,2:T(2,128)(2,1)S(1)} reshape(bf16[16,144,8,64]{3,2,0,1:T(8,128)(2,1)} %copy.91) | data formatting | bytes 4718592 | tf_op jit(solution)/shard_map/reshape;reshape | solution.py:86
  297.3 8.4 %copy.95 = bf16[16,144,8,64]{3,2,0,1:T(8,128)(2,1)} copy(bf16[16,144,8,64]{1,3,2,0:T(8,128)(2,1)} %fusion.10) | data formatting | bytes 4718592 | tf_op jit(solution)/shard_map/convert_element_type | solution.py:59
  305.6 7.0 %reshape_reshape.30 = bf16[8,2,2,6,12,512]{5,1,0,4,3,2:T(2,128)(2,1)S(1)} reshape(bf16[16,144,8,64]{3,2,0,1:T(8,128)(2,1)} %copy.95) | data formatting | bytes 4718592 | tf_op jit(solution)/shard_map/reshape;reshape | solution.py:86
  325.9 10.2 %convert_bitcast_fusion = bf16[16,144,8,64]{1,3,2,0:T(8,128)(2,1)} fusion(bf16[16,144,8,64]{1,3,2,0:T(8,128)(2,1)} %copy.86, bf16[16,8,144,144]{2,3,1,0:T(8,128)(2,1)} %copy-done), kind=kOutput, calls=%fused_computation.21 | convolution fusion | flops 340918272 | bytes 10027008 | tf_op jit(solution)/shard_map/whij,wihc->wjhc/dot_general | solution.py:60
  336.1 8.4 %copy.99 = bf16[16,144,8,64]{3,2,0,1:T(8,128)(2,1)} copy(bf16[16,144,8,64]{1,3,2,0:T(8,128)(2,1)} %convert_bitcast_fusion) | data formatting | bytes 4718592 | tf_op jit(solution)/shard_map/convert_element_type | solution.py:62
  344.4 7.0 %reshape_reshape.31 = bf16[8,2,2,6,12,512]{5,1,0,4,3,2:T(2,128)(2,1)S(1)} reshape(bf16[16,144,8,64]{3,2,0,1:T(8,128)(2,1)} %copy.99) | data formatting | bytes 4718592 | tf_op jit(solution)/shard_map/reshape;reshape | solution.py:86
  366.4 6.2 %collective-permute-done.7 = bf16[2,3,24,512]{3,0,2,1:T(2,128)(2,1)S(1)} collective-permute-done((bf16[2,3,24,512]{3,0,2,1:T(2,128)(2,1)S(1)}, bf16[2,3,24,512]{3,0,2,1:T(2,128)(2,1)S(1)}, u32[]{:S(2)}, u32[]{:S(2)}) %collective-permute-start.7) | collective-permute-done | bytes 147488 | tf_op jit(solution)/shard_map/ppermute | solution.py:10
  372.6 4.4 %fusion.14 = bf16[2,48,24,512]{3,0,2,1:T(2,128)(2,1)S(1)} fusion(bf16[2,48,18,512]{3,0,2,1:T(2,128)(2,1)S(1)} %slice.141, bf16[2,48,6,512]{3,0,2,1:T(2,128)(2,1)} %collective-permute-done.6, bf16[2,3,24,512]{3,0,2,1:T(2,128)(2,1)S(1)} %collective-permute-done.7), kind=kLoop, calls=%fused_computation.33 | loop fusion | flops 2359296 | bytes 4866048 | tf_op jit(solution)/shard_map/concatenate | solution.py:148
  (140 shorter events, 123.1 us)
Async XLA Ops:
  0.6 10.9 %copy-start.13 = (bf16[2,48,24,512]{3,2,1,0:T(8,128)(2,1)S(1)}, bf16[2,48,24,512]{3,2,1,0:T(8,128)(2,1)}, u32[]{:S(2)}) copy-start(bf16[2,48,24,512]{3,2,1,0:T(8,128)(2,1)} %param.8) | copy-start | bytes 7077892
  1.8 51.1 %collective-permute-start.8 = (bf16[2,3,24,512]{3,1,2,0:T(4,128)(2,1)S(1)}, bf16[2,3,24,512]{3,1,2,0:T(4,128)(2,1)S(1)}, u32[]{:S(2)}, u32[]{:S(2)}) collective-permute-start(bf16[2,3,24,512]{3,1,2,0:T(4,128)(2,1)S(1)} %copy.136), channel_id=1, source_target_pairs={{16,0},{32,16},{48,32},{64,48},{80,64},{96,80},{112,96},{0,112},{1... | collective-permute-start | bytes 442376 | tf_op jit(solution)/shard_map/ppermute | solution.py:10
  8.1 74.7 %collective-permute-start = (bf16[2,3,24,512]{3,1,2,0:T(4,128)(2,1)}, bf16[2,3,24,512]{3,1,2,0:T(4,128)(2,1)}, u32[]{:S(2)}, u32[]{:S(2)}) collective-permute-start(bf16[2,3,24,512]{3,1,2,0:T(4,128)(2,1)} %copy.134), channel_id=1, source_target_pairs={{16,0},{32,16},{48,32},{64,48},{80,64},{96,80},{112,96},{0,112},{1... | collective-permute-start | bytes 442376 | tf_op jit(solution)/shard_map/ppermute | solution.py:10
  9.9 40.2 %collective-permute-start.2 = (bf16[2,3,24,512]{3,1,2,0:T(4,128)(2,1)}, bf16[2,3,24,512]{3,1,2,0:T(4,128)(2,1)S(1)}, u32[]{:S(2)}, u32[]{:S(2)}) collective-permute-start(bf16[2,3,24,512]{3,1,2,0:T(4,128)(2,1)} %copy.135), channel_id=1, source_target_pairs={{16,0},{32,16},{48,32},{64,48},{80,64},{96,80},{112,96},{0,112},{1... | collective-permute-start | bytes 442376 | tf_op jit(solution)/shard_map/ppermute | solution.py:10
  12.7 3.2 copy-start.11
  12.8 35.0 %collective-permute-start.4 = (bf16[2,3,24,512]{3,1,2,0:T(4,128)(2,1)S(1)}, bf16[2,3,24,512]{3,1,2,0:T(4,128)(2,1)S(1)}, u32[]{:S(2)}, u32[]{:S(2)}) collective-permute-start(bf16[2,3,24,512]{3,1,2,0:T(4,128)(2,1)S(1)} %slice.136), channel_id=1, source_target_pairs={{16,0},{32,16},{48,32},{64,48},{80,64},{96,80},{112,96},{0,112},{1... | collective-permute-start | bytes 442376 | tf_op jit(solution)/shard_map/ppermute | solution.py:10
  15.9 2.2 copy-start.12
  33.2 14.5 %copy-start.17 = (s32[144]{0:T(256)S(1)}, s32[144]{0:T(256)}, u32[]{:S(2)}) copy-start(s32[144]{0:T(256)} %and_select_fusion) | copy-start | bytes 1732
  33.2 14.4 %copy-start.18 = (s32[16]{0:T(128)S(1)}, s32[16]{0:T(128)}, u32[]{:S(2)}) copy-start(s32[16]{0:T(128)} %fusion.32) | copy-start | bytes 196
  47.7 7.9 %copy-start.14 = (bf16[2,3,24,512]{3,1,2,0:T(4,128)(2,1)}, bf16[2,3,24,512]{3,1,2,0:T(4,128)(2,1)S(1)}, u32[]{:S(2)}) copy-start(bf16[2,3,24,512]{3,1,2,0:T(4,128)(2,1)S(1)} %collective-permute-done.4) | copy-start | bytes 442372
  48.7 44.2 %collective-permute-start.5 = (bf16[2,51,6,512]{3,1,2,0:T(8,128)(2,1)}, bf16[2,51,6,512]{3,1,2,0:T(8,128)(2,1)}, u32[]{:S(2)}, u32[]{:S(2)}) collective-permute-start(bf16[2,51,6,512]{3,1,2,0:T(8,128)(2,1)} %pad_maximum_fusion.8), channel_id=1, source_target_pairs={{1,0},{2,1},{3,2},{4,3},{5,4},{6,5},{7,6},{8,7},{9,8},{10,9},{11,1... | collective-permute-start | bytes 1880072 | tf_op jit(solution)/shard_map/ppermute | solution.py:10
  52.9 41.3 %collective-permute-start.3 = (bf16[2,51,6,512]{3,1,2,0:T(8,128)(2,1)}, bf16[2,51,6,512]{3,1,2,0:T(8,128)(2,1)}, u32[]{:S(2)}, u32[]{:S(2)}) collective-permute-start(bf16[2,51,6,512]{3,1,2,0:T(8,128)(2,1)} %slice.134), channel_id=1, source_target_pairs={{1,0},{2,1},{3,2},{4,3},{5,4},{6,5},{7,6},{8,7},{9,8},{10,9},{11,1... | collective-permute-start | bytes 1880072 | tf_op jit(solution)/shard_map/ppermute | solution.py:10
  55.7 41.6 %collective-permute-start.9 = (bf16[2,51,6,512]{3,1,2,0:T(8,128)(2,1)}, bf16[2,51,6,512]{3,1,2,0:T(8,128)(2,1)}, u32[]{:S(2)}, u32[]{:S(2)}) collective-permute-start(bf16[2,51,6,512]{3,1,2,0:T(8,128)(2,1)} %slice.144), channel_id=1, source_target_pairs={{1,0},{2,1},{3,2},{4,3},{5,4},{6,5},{7,6},{8,7},{9,8},{10,9},{11,1... | collective-permute-start | bytes 1880072 | tf_op jit(solution)/shard_map/ppermute | solution.py:10
  80.1 2.7 copy-start.7
  82.7 4.3 %copy-start.8 = (bf16[2,51,24,512]{3,1,2,0:T(8,128)(2,1)S(1)}, bf16[2,51,24,512]{3,1,2,0:T(8,128)(2,1)}, u32[]{:S(2)}) copy-start(bf16[2,51,24,512]{3,1,2,0:T(8,128)(2,1)} %constant_dynamic-update-slice_fusion.4) | copy-start | bytes 7520260
  84.9 6.9 %copy-start.15 = (bf16[2,3,24,512]{3,1,2,0:T(4,128)(2,1)S(1)}, bf16[2,3,24,512]{3,1,2,0:T(4,128)(2,1)}, u32[]{:S(2)}) copy-start(bf16[2,3,24,512]{3,1,2,0:T(4,128)(2,1)} %copy-done.14) | copy-start | bytes 442372
  87.9 74.8 %collective-permute-start.1 = (bf16[2,51,6,512]{3,1,2,0:T(8,128)(2,1)}, bf16[2,51,6,512]{3,1,2,0:T(8,128)(2,1)}, u32[]{:S(2)}, u32[]{:S(2)}) collective-permute-start(bf16[2,51,6,512]{3,1,2,0:T(8,128)(2,1)} %slice.130), channel_id=1, source_target_pairs={{1,0},{2,1},{3,2},{4,3},{5,4},{6,5},{7,6},{8,7},{9,8},{10,9},{11,1... | collective-permute-start | bytes 1880072 | tf_op jit(solution)/shard_map/ppermute | solution.py:10
  110.2 8.5 %copy-start.5 = (bf16[2,48,24,512]{3,1,2,0:T(8,128)(2,1)S(1)}, bf16[2,48,24,512]{3,1,2,0:T(8,128)(2,1)}, u32[]{:S(2)}) copy-start(bf16[2,48,24,512]{3,1,2,0:T(8,128)(2,1)} %pad_maximum_fusion.5) | copy-start | bytes 7077892
  128.5 8.5 %copy-start.6 = (bf16[2,48,24,512]{3,1,2,0:T(8,128)(2,1)S(1)}, bf16[2,48,24,512]{3,1,2,0:T(8,128)(2,1)}, u32[]{:S(2)}) copy-start(bf16[2,48,24,512]{3,1,2,0:T(8,128)(2,1)} %pad_maximum_fusion.7) | copy-start | bytes 7077892
  155.4 8.6 %copy-start.9 = (bf16[2,48,18,512]{3,1,2,0:T(8,128)(2,1)S(1)}, bf16[2,48,18,512]{3,1,2,0:T(8,128)(2,1)}, u32[]{:S(2)}) copy-start(bf16[2,48,18,512]{3,1,2,0:T(8,128)(2,1)} %slice.129) | copy-start | bytes 5308420
  182.4 11.3 %copy-start.16 = (pred[16,144,144]{1,2,0:T(8,128)(4,1)S(1)}, pred[16,144,144]{1,2,0:T(8,128)(4,1)}, u32[]{:S(2)}) copy-start(pred[16,144,144]{1,2,0:T(8,128)(4,1)} %broadcast_compare_fusion) | copy-start | bytes 995332
  214.9 11.6 %copy-start = (bf16[16,8,144,144]{2,3,1,0:T(8,128)(2,1)}, bf16[16,8,144,144]{2,3,1,0:T(8,128)(2,1)S(1)}, u32[]{:S(2)}) copy-start(bf16[16,8,144,144]{2,3,1,0:T(8,128)(2,1)S(1)} %fusion.6) | copy-start | bytes 15925252
  322.3 37.3 %collective-permute-start.6 = (bf16[2,48,6,512]{3,0,2,1:T(2,128)(2,1)}, bf16[2,48,6,512]{3,0,2,1:T(2,128)(2,1)}, u32[]{:S(2)}, u32[]{:S(2)}) collective-permute-start(bf16[2,48,6,512]{3,0,2,1:T(2,128)(2,1)} %slice.140), channel_id=1, source_target_pairs={{15,0},{0,1},{1,2},{2,3},{3,4},{4,5},{5,6},{6,7},{7,8},{8,9},{9,10... | collective-permute-start | bytes 1769480 | tf_op jit(solution)/shard_map/ppermute | solution.py:10
  322.7 39.6 %collective-permute-start.10 = (bf16[2,48,6,512]{3,0,2,1:T(2,128)(2,1)}, bf16[2,48,6,512]{3,0,2,1:T(2,128)(2,1)S(1)}, u32[]{:S(2)}, u32[]{:S(2)}) collective-permute-start(bf16[2,48,6,512]{3,0,2,1:T(2,128)(2,1)} %slice.146), channel_id=1, source_target_pairs={{15,0},{0,1},{1,2},{2,3},{3,4},{4,5},{5,6},{6,7},{7,8},{8,9},{9,10... | collective-permute-start | bytes 1769480 | tf_op jit(solution)/shard_map/ppermute | solution.py:10
  322.7 41.5 %collective-permute-start.12 = (bf16[2,48,6,512]{3,0,2,1:T(2,128)(2,1)}, bf16[2,48,6,512]{3,0,2,1:T(2,128)(2,1)S(1)}, u32[]{:S(2)}, u32[]{:S(2)}) collective-permute-start(bf16[2,48,6,512]{3,0,2,1:T(2,128)(2,1)} %slice.148), channel_id=1, source_target_pairs={{15,0},{0,1},{1,2},{2,3},{3,4},{4,5},{5,6},{6,7},{7,8},{8,9},{9,10... | collective-permute-start | bytes 1769480 | tf_op jit(solution)/shard_map/ppermute | solution.py:10
  354.3 2.9 copy-start.2
  354.3 11.5 %collective-permute-start.14 = (bf16[2,48,6,512]{3,0,2,1:T(2,128)(2,1)S(1)}, bf16[2,48,6,512]{3,0,2,1:T(2,128)(2,1)S(1)}, u32[]{:S(2)}, u32[]{:S(2)}) collective-permute-start(bf16[2,48,6,512]{3,0,2,1:T(2,128)(2,1)S(1)} %slice.150), channel_id=1, source_target_pairs={{15,0},{0,1},{1,2},{2,3},{3,4},{4,5},{5,6},{6,7},{7,8},{8,9},{9,10... | collective-permute-start | bytes 1769480 | tf_op jit(solution)/shard_map/ppermute | solution.py:10
  355.9 2.5 copy-start.1
  360.6 12.0 %collective-permute-start.7 = (bf16[2,3,24,512]{3,0,2,1:T(2,128)(2,1)S(1)}, bf16[2,3,24,512]{3,0,2,1:T(2,128)(2,1)S(1)}, u32[]{:S(2)}, u32[]{:S(2)}) collective-permute-start(bf16[2,3,24,512]{3,0,2,1:T(2,128)(2,1)S(1)} %pad_maximum_fusion.12), channel_id=1, source_target_pairs={{112,0},{0,16},{16,32},{32,48},{48,64},{64,80},{80,96},{96,112},{1... | collective-permute-start | bytes 442376 | tf_op jit(solution)/shard_map/ppermute | solution.py:10
  362.5 14.5 %collective-permute-start.11 = (bf16[2,3,24,512]{3,0,2,1:T(2,128)(2,1)S(1)}, bf16[2,3,24,512]{3,0,2,1:T(2,128)(2,1)S(1)}, u32[]{:S(2)}, u32[]{:S(2)}) collective-permute-start(bf16[2,3,24,512]{3,0,2,1:T(2,128)(2,1)S(1)} %pad_maximum_fusion.11), channel_id=1, source_target_pairs={{112,0},{0,16},{16,32},{32,48},{48,64},{64,80},{80,96},{96,112},{1... | collective-permute-start | bytes 442376 | tf_op jit(solution)/shard_map/ppermute | solution.py:10
  364.4 16.0 %collective-permute-start.13 = (bf16[2,3,24,512]{3,0,2,1:T(2,128)(2,1)S(1)}, bf16[2,3,24,512]{3,0,2,1:T(2,128)(2,1)S(1)}, u32[]{:S(2)}, u32[]{:S(2)}) collective-permute-start(bf16[2,3,24,512]{3,0,2,1:T(2,128)(2,1)S(1)} %pad_maximum_fusion.10), channel_id=1, source_target_pairs={{112,0},{0,16},{16,32},{32,48},{48,64},{64,80},{80,96},{96,112},{1... | collective-permute-start | bytes 442376 | tf_op jit(solution)/shard_map/ppermute | solution.py:10
  366.0 23.2 %collective-permute-start.15 = (bf16[2,3,24,512]{3,0,2,1:T(2,128)(2,1)S(1)}, bf16[2,3,24,512]{3,0,2,1:T(2,128)(2,1)S(1)}, u32[]{:S(2)}, u32[]{:S(2)}) collective-permute-start(bf16[2,3,24,512]{3,0,2,1:T(2,128)(2,1)S(1)} %pad_maximum_fusion.9), channel_id=1, source_target_pairs={{112,0},{0,16},{16,32},{32,48},{48,64},{64,80},{80,96},{96,112},{1... | collective-permute-start | bytes 442376 | tf_op jit(solution)/shard_map/ppermute | solution.py:10
  (3 other events, 5.5 us)
where the time goes:
time: 401 us; the launch traced here: 395 us
  local copies, waits for them, and re-layouts  231 us (58%)
  matrix products  93.4 us (23%)
  other arithmetic  42.5 us (11%)
  starting transfers between devices  20.1 us (5%)
  waiting for transfers between devices  6.27 us (2%)
    unnamed x49, local copies, waits for them, and re-layouts  28.2 us
    another operation x4, local copies, waits for them, and re-layouts, from_windows(): array.reshape(bands, groups, lev, 6, 12, width).transpose(2, 0, 3, 1, 4, 5)  28.1 us
    add x2, local copies, waits for them, and re-layouts, attend(): jnp.einsum('wihc,wjhc->whij', q_heads, k_heads, preferred_element_type=f32)  22.1 us
    ppermute x16, starting transfers between devices, shifted(): return lax.ppermute(block, axis, route)  20.1 us
    concatenate x4, other arithmetic, shards(): jnp.concatenate([extra, whole[:, :rows - 3]], axis=1)  14.6 us
    dot_general x1, matrix products, relative_bias(): jnp.einsum('hxcdab,xef->hefcdab', second, one_hot_offsets(2, 3, 1), preci...  14.4 us
    dot_general x1, matrix products, attend(): jnp.einsum('wihc,wjhc->whij', g_heads, v_heads, preferred_element_type=f32)  13.9 us
    sub x1, matrix products, attend(): expo = jnp.exp(scores - peak)  13.4 us
  transfers between devices with their start and end apart: 16, of which 1 were waited for; matrix products, arithmetic and copies ran while one was open for 51% of the time, Pallas kernels for 0%

commit v1 on v0

v1 whole, which is shorter than its diff:
```python
import functools

import jax
import jax.numpy as jnp
import numpy as np
from jax import lax
from jax.experimental import pallas as pl
from jax.experimental.pallas import tpu as pltpu
from jax.sharding import PartitionSpec as P

F32 = jnp.float32
BF16 = jnp.bfloat16
HALF = 36
STRIP = 72
WIN = 144
GROUP = 256
MIB = 1 << 20
VMEM_BYTES = 60 * MIB


def strip_matrix(strips):
    out = np.zeros((len(strips), 2, 2, 3, 6, 2, 2, 3, 24), np.float32)
    for place, strip in enumerate(strips):
        for part in range(2):
            for lev in range(2):
                for row in range(3):
                    for col in range(6):
                        out[place, part, lev, row, col, part, lev, row, 6 * strip + col] = 1
    return out.reshape(len(strips) * STRIP, 2 * WIN)


def far_matrix(strip, tile):
    full = strip_matrix([strip]).reshape(STRIP, 2, 2, 3, 3, 8)
    return full[:, :, :, :, tile].reshape(STRIP, 96)


def run_bases():
    run = np.arange(24)
    half, part, lev, row = run // 12, run // 6 % 2, run // 3 % 2, run % 3
    return lev * 253 + (row + 3 * (1 - part)) * 23 + 6 * half


def dot(a, b, ca=1, cb=0):
    return lax.dot_general(a, b, (((ca,), (cb,)), ((), ())), preferred_element_type=F32)


def keyed_rows(key, mask, embed):
    wide = jnp.concatenate([mask] * 4, axis=-1)
    return (key + (wide * embed)[None]).astype(BF16).astype(F32)


def side_spec(shape):
    return pl.BlockSpec((1, *shape), lambda s, core: (core[0],) + (0,) * len(shape))


def fixed_spec(shape):
    return pl.BlockSpec(shape, lambda s, core: (0,) * len(shape))


def params():
    return pltpu.CompilerParams(vmem_limit_bytes=VMEM_BYTES)


def rows_body(q0, q1, k0, k1, v0, v1, g0, g1, m0, m1, embed, top, bottom):
    for index, pair in enumerate(((q0, q1), (k0, k1), (v0, v1), (g0, g1))):
        for source, mask, out in zip(pair, (m0, m1), (top, bottom)):
            if index == 1:
                keyed = keyed_rows(source[:, 0].astype(F32), mask[0], embed[...])
                out[index] = keyed.astype(BF16)
            else:
                out[index] = source[:, 0]


def edge_rows(arrays, mask, embed):
    operands, specs = [], []
    for array in arrays:
        array = array.reshape(2, 16, STRIP, 512)
        operands += [array, array]
        specs += [
            pl.BlockSpec((2, 1, STRIP, 512), lambda s: (0, 0, 0, 0)),
            pl.BlockSpec((2, 1, STRIP, 512), lambda s: (0, 15, 0, 0)),
        ]
    mask = mask.reshape(16, STRIP, 128)
    return pl.pallas_call(
        rows_body,
        grid=(1,),
        in_specs=specs
        + [
            pl.BlockSpec((1, STRIP, 128), lambda s: (0, 0, 0)),
            pl.BlockSpec((1, STRIP, 128), lambda s: (15, 0, 0)),
            pl.BlockSpec((1, 512), lambda s: (0, 0)),
        ],
        out_specs=[pl.BlockSpec((4, 2, STRIP, 512), lambda s: (0, 0, 0, 0))] * 2,
        out_shape=[jax.ShapeDtypeStruct((4, 2, STRIP, 512), BF16)] * 2,
        compiler_params=params(),
        cost_estimate=pl.CostEstimate(flops=0, bytes_accessed=5 * MIB, transcendentals=0),
        name="edge_rows",
    )(*operands, mask, mask, embed)


def strips_body(flip, core, q, k, v, g, mask, embed, perm, out, held, packed, came, gone):
    tile = 2 * jnp.where(flip, 1 - core[0], core[0])
    arrivals = []
    for index, source in enumerate((q, k, v, g)):
        copy = pltpu.make_async_copy(source.at[:, :, tile], held.at[index], came.at[index])
        copy.start()
        arrivals.append(copy)
    departures = []
    for index in range(4):
        arrivals[index].wait()
        for band in range(1, 8):
            opening = held[index, :, 6 * band : 6 * band + 3].astype(F32)
            closing = held[index, :, 6 * band - 3 : 6 * band].astype(F32)
            if index == 1:
                opening = keyed_rows(opening, mask[6 * band : 6 * band + 3, 0], embed[...])
                closing = keyed_rows(closing, mask[6 * band - 3 : 6 * band, 0], embed[...])
            tokens = jnp.concatenate([opening.reshape(48, 512), closing.reshape(48, 512)], axis=0)
            strip = dot(perm[0], tokens.astype(BF16))
            if index == 0:
                strip = strip * 0.125
            packed[index, band - 1] = strip.astype(BF16)
        copy = pltpu.make_async_copy(packed.at[index], out.at[index], gone.at[index])
        copy.start()
        departures.append(copy)
    for copy in departures:
        copy.wait()


def pack_strips(arrays, mask, embed, perm, core, flip):
    tiles = [array.reshape(2, 48, 3, 8, 512) for array in arrays]

    def mask_pick(s, core):
        return (0, 2 * jnp.where(flip, 1 - core[0], core[0]), 0, 0)

    anywhere = pl.BlockSpec(memory_space=pl.ANY)
    return pl.pallas_call(
        functools.partial(strips_body, flip),
        grid_spec=pltpu.PrefetchScalarGridSpec(
            num_scalar_prefetch=1,
            grid=(1,),
            in_specs=[anywhere] * 4
            + [
                pl.BlockSpec((48, 1, 8, 128), mask_pick),
                fixed_spec((1, 512)),
                side_spec((STRIP, 96)),
            ],
            out_specs=anywhere,
            scratch_shapes=[
                pltpu.VMEM((4, 2, 48, 8, 512), BF16),
                pltpu.VMEM((4, 7, STRIP, 512), BF16),
                pltpu.SemaphoreType.DMA((4,)),
                pltpu.SemaphoreType.DMA((4,)),
            ],
        ),
        out_shape=jax.ShapeDtypeStruct((4, 7, STRIP, 512), BF16),
        compiler_params=params(),
        cost_estimate=pl.CostEstimate(
            flops=2 * 28 * STRIP * 96 * 512, bytes_accessed=6 * MIB, transcendentals=0
        ),
        name="pack_near" if flip else "pack_far",
    )(core, *tiles, mask.reshape(48, 3, 8, 128), embed, perm)


def corners_body(core, top, bottom, below, above, perm, far, near, mid):
    for index in range(4):
        for place, (first, second) in enumerate(((top, above), (below, bottom))):
            first = first[index].astype(F32)
            second = second[index].astype(F32)
            tokens = jnp.concatenate([first[0], first[1], second[0], second[1]], axis=0)
            strips = dot(perm[0], tokens.astype(BF16))
            if index == 0:
                strips = strips * 0.125
            far[index, place] = strips[:STRIP].astype(BF16)
            near[index, place] = strips[STRIP : 2 * STRIP].astype(BF16)
            mid[index, place] = strips[2 * STRIP :].astype(BF16)


def pack_corners(top, bottom, below, above, perm, core):
    sizes = (STRIP, STRIP, WIN)
    return pl.pallas_call(
        corners_body,
        grid_spec=pltpu.PrefetchScalarGridSpec(
            num_scalar_prefetch=1,
            grid=(1,),
            in_specs=[fixed_spec((4, 2, STRIP, 512))] * 4 + [side_spec((2 * WIN, 2 * WIN))],
            out_specs=[fixed_spec((4, 2, size, 512)) for size in sizes],
        ),
        out_shape=[jax.ShapeDtypeStruct((4, 2, size, 512), BF16) for size in sizes],
        compiler_params=params(),
        cost_estimate=pl.CostEstimate(
            flops=2 * 8 * 288 * 288 * 512, bytes_accessed=5 * MIB, transcendentals=0
        ),
        name="pack_corners",
    )(core, top, bottom, below, above, perm)


def windows(win, slots, bias, scores, grads, low, dlow, store):
    lane = lax.broadcasted_iota(jnp.int32, (1, GROUP), 1) // 64

    def spread(x):
        return jnp.concatenate(
            [x * jnp.where(lane == h, 1.0, 0.0).astype(BF16) for h in range(4)], axis=0
        )

    def by_head(wide):
        total = None
        for h in range(4):
            piece = jnp.where(lane == h, wide[WIN * h : WIN * (h + 1)], 0.0)
            total = piece if total is None else total + piece
        return total

    jobs = []
    for slot in range(slots):
        for group in range(2):
            cols = slice(GROUP * group, GROUP * (group + 1))
            q, k, v, g = (win[slot, index, :, cols] for index in range(4))
            q_wide, g_wide = spread(q), spread(g)
            place = 2 * slot + group
            scores[place] = dot(k, q_wide, 1, 1)
            grads[place] = dot(v, g_wide, 1, 1)
            jobs.append((slot, group, place, cols, k, v, q_wide, g_wide))
    for slot, group, place, cols, k, v, q_wide, g_wide in jobs:
        for start in range(0, 576, 128):
            part = slice(start, min(start + 128, 576))
            s = scores[place, :, part] + bias[0, group, :, part]
            e = jnp.exp(s - jnp.max(s, axis=0, keepdims=True))
            p = e * (1.0 / jnp.sum(e, axis=0, keepdims=True))
            gp = grads[place, :, part]
            delta = jnp.sum(p * gp, axis=0, keepdims=True)
            low[place, :, part] = p.astype(BF16)
            dlow[place, :, part] = (p * (gp - delta)).astype(BF16)
        p_low, d_low = low[place], dlow[place]
        store(slot, 0, cols, by_head(dot(p_low, v, 0, 0)))
        store(slot, 1, cols, by_head(dot(d_low, k, 0, 0)) * 0.125)
        store(slot, 2, cols, dot(d_low, q_wide))
        store(slot, 3, cols, dot(p_low, g_wide))


def place_pair(win, slot, own, halo, own_left):
    def put(left, right):
        for index in range(4):
            both = jnp.concatenate(
                [left[index, 0].astype(F32), right[index, 0].astype(F32)], axis=0
            )
            win[slot, index] = both.astype(BF16)

    @pl.when(own_left)
    def _():
        put(own, halo)

    @pl.when(jnp.logical_not(own_left))
    def _():
        put(halo, own)


def inner_body(core, q0, q1, k0, k1, v0, v1, g0, g1, m0, m1, embed, perm, mid_c, own, own_c, halo, halo_c, bias, back, *rest):
    outs, (win, result, ready, gone), work = rest[:4], rest[4:8], rest[8:]
    s = pl.program_id(0)
    left = core[0] == 0
    corner = s < 2

    @pl.when(corner)
    def _():
        for index in range(4):
            win[0, index] = mid_c[index, 0]
        place_pair(win, 1, own_c, halo_c, left)

    @pl.when(jnp.logical_not(corner))
    def _():
        for index, pair in enumerate(((q0, q1), (k0, k1), (v0, v1), (g0, g1))):
            first, second = (source[:, 0].astype(F32) for source in pair)
            if index == 1:
                first = keyed_rows(first, m0[0], embed[...])
                second = keyed_rows(second, m1[0], embed[...])
            tokens = jnp.concatenate([first[0], first[1], second[0], second[1]], axis=0)
            packed = dot(perm[...], tokens.astype(BF16))
            if index == 0:
                packed = packed * 0.125
            win[0, index] = packed.astype(BF16)
        place_pair(win, 1, own, halo, left)

    starts = (pl.multiple_of(WIN * core[0], 16), pl.multiple_of(WIN * (1 - core[0]), 16))

    def keep(slot, index, cols, value):
        result[index, pl.ds(starts[slot], WIN), cols] = value.astype(BF16)

    windows(win, 2, bias, *work, keep)

    def leave(slot, first, second):
        copies = []
        for index, out in enumerate(outs):
            for part, block in enumerate((first, second)):
                copies.append(
                    pltpu.make_async_copy(
                        ready.at[slot, index, part], out.at[:, block], gone.at[slot, index, part]
                    )
                )
        return copies

    slot = jnp.where(corner, 0, (s + 1) % 2)

    @pl.when(s >= 3)
    def _():
        for copy in leave(slot, 0, 15):
            copy.wait()

    used = pl.ds(pl.multiple_of(64 * core[0], 16), 224)
    for index in range(4):
        full = dot(back[0], result[index, used]).reshape(2, 2, STRIP, 512).astype(BF16)

        @pl.when(s != 1)
        def _():
            ready[slot, index, 0] = full[0]

        @pl.when(s != 0)
        def _():
            ready[slot, index, 1] = full[1]

    @pl.when(s > 0)
    def _():
        first = jnp.where(corner, 0, 2 * (s - 1))
        second = jnp.where(corner, 15, 2 * (s - 1) - 1)
        for copy in leave(slot, first, second):
            copy.start()

    @pl.when(s == 8)
    def _():
        for copy in leave(0, 0, 15) + leave(1, 0, 15):
            copy.wait()


def work_scratch(places):
    return [
        pltpu.VMEM((places, WIN, 576), F32),
        pltpu.VMEM((places, WIN, 576), F32),
        pltpu.VMEM((places, WIN, 576), BF16),
        pltpu.VMEM((places, WIN, 576), BF16),
    ]


def window_cost(count, moved):
    return pl.CostEstimate(
        flops=count * 6 * 2 * WIN * WIN * 512 * 4,
        bytes_accessed=moved,
        transcendentals=count * 8 * WIN * WIN,
    )


def inner(arrays, mask, embed, perm, mid_c, own, own_c, halo, halo_c, bias, back, core):
    operands, specs = [], []
    block = (2, 1, STRIP, 512)
    mask = mask.reshape(16, STRIP, 128)

    def opening(s):
        return jnp.maximum(2 * (s - 1), 2)

    def closing(s):
        return opening(s) - 1

    for array in arrays:
        array = array.reshape(2, 16, STRIP, 512)
        operands += [array, array]
        specs += [
            pl.BlockSpec(block, lambda s, core: (0, opening(s), 0, 0)),
            pl.BlockSpec(block, lambda s, core: (0, closing(s), 0, 0)),
        ]

    def band(size):
        return pl.BlockSpec((4, 1, size, 512), lambda s, core: (0, jnp.maximum(s - 2, 0), 0, 0))

    def corner(size):
        return pl.BlockSpec((4, 1, size, 512), lambda s, core: (0, jnp.minimum(s, 1), 0, 0))

    anywhere = pl.BlockSpec(memory_space=pl.ANY)
    return pl.pallas_call(
        inner_body,
        grid_spec=pltpu.PrefetchScalarGridSpec(
            num_scalar_prefetch=1,
            grid=(9,),
            in_specs=specs
            + [
                pl.BlockSpec((1, STRIP, 128), lambda s, core: (opening(s), 0, 0)),
                pl.BlockSpec((1, STRIP, 128), lambda s, core: (closing(s), 0, 0)),
                fixed_spec((1, 512)),
                fixed_spec((WIN, 2 * WIN)),
                corner(WIN),
                band(STRIP),
                corner(STRIP),
                band(STRIP),
                corner(STRIP),
                pl.BlockSpec(
                    (1, 2, WIN, 576), lambda s, core: (jnp.where(s < 2, s + 1, 0), 0, 0, 0)
                ),
                side_spec((2 * WIN, 224)),
            ],
            out_specs=[anywhere] * 4,
            scratch_shapes=[
                pltpu.VMEM((2, 4, WIN, 512), BF16),
                pltpu.VMEM((4, 2 * WIN, 512), BF16),
                pltpu.VMEM((2, 4, 2, 2, STRIP, 512), BF16),
                pltpu.SemaphoreType.DMA((2, 4, 2)),
            ]
            + work_scratch(4),
        ),
        out_shape=[jax.ShapeDtypeStruct((2, 16, STRIP, 512), BF16)] * 4,
        compiler_params=params(),
        cost_estimate=window_cost(18, 24 * MIB),
        name="inner_windows",
    )(core, *operands, mask, mask, embed, perm, mid_c, own, own_c, halo, halo_c, bias, back)


def outer_body(core, own, own_c, halo, halo_c, bias, back, p0, p1, p2, p3, o0, o1, o2, o3, win, result, tiles, came, gone, *work):
    s = pl.program_id(0)
    left = core[0] == 1
    tile = 2 * core[0]
    outs = (o0, o1, o2, o3)

    def arrivals():
        return [
            pltpu.make_async_copy(out.at[:, :, tile], tiles.at[index], came.at[index])
            for index, out in enumerate(outs)
        ]

    @pl.when(s == 0)
    def _():
        for copy in arrivals():
            copy.start()

    @pl.when(s < 7)
    def _():
        place_pair(win, 0, own, halo, left)

    @pl.when(s >= 7)
    def _():
        place_pair(win, 0, own_c, halo_c, left)

    def keep(slot, index, cols, value):
        result[index, :, cols] = value.astype(BF16)

    windows(win, 1, bias, *work, keep)

    @pl.when(s == 0)
    def _():
        for copy in arrivals():
            copy.wait()

    used = pl.ds(pl.multiple_of(64 * (1 - core[0]), 16), 80)

    def leave(step, index, row, count):
        span = pl.ds(row, count)
        return pltpu.make_async_copy(
            tiles.at[index, :, span], outs[index].at[:, span, tile], gone.at[step, index]
        )

    for index in range(4):
        full = dot(back[0], result[index, used]).reshape(2, 2, 3, 8, 512)

        def add(part, row, index=index, full=full):
            span = pl.ds(row, 3)
            total = tiles[index, :, span].astype(F32) + full[part]
            tiles[index, :, span] = total.astype(BF16)

        @pl.when(s < 7)
        def _():
            add(0, 6 * s + 6)
            add(1, 6 * s + 3)
            leave(s, index, 6 * s + 3, 6).start()

        @pl.when(s == 7)
        def _():
            add(0, 0)
            leave(7, index, 0, 3).start()

        @pl.when(s == 8)
        def _():
            add(1, 45)
            leave(8, index, 45, 3).start()

    @pl.when(s == 8)
    def _():
        for index in range(4):
            for step in range(7):
                leave(step, index, 6 * step + 3, 6).wait()
            leave(7, index, 0, 3).wait()
            leave(8, index, 45, 3).wait()


def outer(partial, own, own_c, halo, halo_c, bias, back, core):
    def band(size):
        return pl.BlockSpec((4, 1, size, 512), lambda s, core: (0, jnp.minimum(s, 6), 0, 0))

    def corner(size):
        return pl.BlockSpec((4, 1, size, 512), lambda s, core: (0, jnp.maximum(s - 7, 0), 0, 0))

    anywhere = pl.BlockSpec(memory_space=pl.ANY)
    shape = (2, 48, 3, 8, 512)
    return pl.pallas_call(
        outer_body,
        grid_spec=pltpu.PrefetchScalarGridSpec(
            num_scalar_prefetch=1,
            grid=(9,),
            in_specs=[
                band(STRIP),
                corner(STRIP),
                band(STRIP),
                corner(STRIP),
                pl.BlockSpec(
                    (1, 2, WIN, 576), lambda s, core: (jnp.maximum(s - 6, 0), 0, 0, 0)
                ),
                side_spec((96, 80)),
            ]
            + [anywhere] * 4,
            out_specs=[anywhere] * 4,
            scratch_shapes=[
                pltpu.VMEM((1, 4, WIN, 512), BF16),
                pltpu.VMEM((4, WIN, 512), BF16),
                pltpu.VMEM((4, 2, 48, 8, 512), BF16),
                pltpu.SemaphoreType.DMA((4,)),
                pltpu.SemaphoreType.DMA((9, 4)),
            ]
            + work_scratch(2),
        ),
        out_shape=[jax.ShapeDtypeStruct(shape, BF16)] * 4,
        input_output_aliases={7 + index: index for index in range(4)},
        compiler_params=params(),
        cost_estimate=window_cost(9, 12 * MIB),
        name="outer_windows",
    )(core, own, own_c, halo, halo_c, bias, back, *[x.reshape(shape) for x in partial])


def bias_body(flags, table, hot, squeeze, out, wide, part, whole):
    variant = pl.program_id(0)

    @pl.when(variant == 0)
    def _():
        for head in range(8):
            line = jnp.broadcast_to(table[head : head + 1], (8, 768))
            line = pltpu.roll(line, 0, 1, stride=1, stride_axis=0)
            for run, base in enumerate(run_bases()):
                turn = int(base - 379) % 768
                turned = pltpu.roll(line, turn, 1)
                wide[head // 4, 8 * run : 8 * run + 8, 384 * (head % 4) : 384 * (head % 4) + 384] = turned[:, :384]
        for group in range(2):
            total = None
            for _ in range(3):
                part[...] = wide[group].astype(BF16)
                wide[group] = wide[group] - part[...].astype(F32)
                spread = dot(part[...], hot[...]).astype(BF16)
                piece = dot(squeeze[...], spread)
                total = piece if total is None else total + piece
            whole[group] = total

    @pl.when((variant == 0) | (flags[variant] == 0))
    def _():
        out[0] = whole[...]

    @pl.when((variant > 0) & (flags[variant] != 0))
    def _():
        upper = lax.broadcasted_iota(jnp.int32, (WIN, 576), 0) % STRIP < HALF
        upper_i = lax.broadcasted_iota(jnp.int32, (WIN, 576), 1) % STRIP < HALF
        for group in range(2):
            out[0, group] = jnp.where(upper == upper_i, whole[group], -jnp.inf)


def window_bias(rel_table, flags):
    tokens = (run_bases()[:, None] + np.arange(6)).reshape(WIN)
    hot = np.zeros((4, 384, 4, WIN), np.float32)
    for head in range(4):
        hot[head, tokens, head, np.arange(WIN)] = 1
    squeeze = np.zeros((24, 6, 24, 8), np.float32)
    for run in range(24):
        squeeze[run, np.arange(6), run, np.arange(6)] = 1
    hot = jnp.asarray(hot.reshape(4 * 384, 4 * WIN), BF16)
    squeeze = jnp.asarray(squeeze.reshape(WIN, 192), BF16)
    table = jnp.pad(rel_table, ((0, 0), (0, 768 - rel_table.shape[1])))
    return pl.pallas_call(
        bias_body,
        grid_spec=pltpu.PrefetchScalarGridSpec(
            num_scalar_prefetch=1,
            grid=(3,),
            in_specs=[
                pl.BlockSpec((8, 768), lambda v, flags: (0, 0)),
                pl.BlockSpec((4 * 384, 576), lambda v, flags: (0, 0)),
                pl.BlockSpec((WIN, 192), lambda v, flags: (0, 0)),
            ],
            out_specs=pl.BlockSpec((1, 2, WIN, 576), lambda v, flags: (v, 0, 0, 0)),
            scratch_shapes=[
                pltpu.VMEM((2, 192, 4 * 384), F32),
                pltpu.VMEM((192, 4 * 384), BF16),
                pltpu.VMEM((2, WIN, 576), F32),
            ],
        ),
        out_shape=jax.ShapeDtypeStruct((3, 2, WIN, 576), F32),
        compiler_params=pltpu.CompilerParams(vmem_limit_bytes=VMEM_BYTES),
        cost_estimate=pl.CostEstimate(
            flops=6 * 2 * 192 * 1536 * 576, bytes_accessed=4 * MIB, transcendentals=0
        ),
        name="window_bias",
    )(flags, table, hot, squeeze)


def side_tables():
    far_strip, near_strip = (0, 3), (3, 0)
    far, near, whole, near_back, far_back = [], [], [], [], []
    for side in range(2):
        far.append(far_matrix(far_strip[side], 2 * side))
        near.append(far_matrix(near_strip[side], 2 - 2 * side))
        whole.append(strip_matrix([far_strip[side], near_strip[side], 1, 2]))
        own = strip_matrix([near_strip[side]]).T
        middle = strip_matrix([1, 2]).T
        pad = np.zeros((2 * WIN, 8), np.float32)
        pad_far = np.zeros((96, 8), np.float32)
        if side == 0:
            near_back.append(np.concatenate([middle, own, pad], axis=1))
            far_back.append(np.concatenate([pad_far, far[0].T], axis=1))
        else:
            near_back.append(np.concatenate([pad, own, middle], axis=1))
            far_back.append(np.concatenate([far[1].T, pad_far], axis=1))
    stacked = (far, near, whole, near_back, far_back)
    return [jnp.asarray(np.stack(table), BF16) for table in stacked]


def after(value, earlier):
    return lax.optimization_barrier((value, earlier))[0]


def shards(queries, key_tokens, value_tokens, out_grad, land_mask, land_embed, rel_table):
    lev, rows, cols, width = queries.shape
    lat = lax.axis_index("lat")
    core = jnp.reshape(lax.axis_index("lon") % 2, (1,))
    bands = lax.axis_size("lat")
    sectors = lax.axis_size("lon")
    arrays = (queries, key_tokens, value_tokens, out_grad)
    mask = jnp.broadcast_to(
        land_mask.astype(F32).reshape(rows // 3, STRIP, 1), (rows // 3, STRIP, 128)
    )
    embed = land_embed.reshape(1, width)
    far_perm, near_perm, all_perm, near_back, far_back = side_tables()
    mid_perm = jnp.asarray(strip_matrix([1, 2]), BF16)

    to_far = [((2 * k + 1) % sectors, (2 * k + 2) % sectors) for k in range(sectors // 2)]
    to_far += [(b, a) for a, b in to_far]
    to_near = [(i, i ^ 1) for i in range(sectors)]

    top, bottom = edge_rows(arrays, mask, embed)
    below = lax.ppermute(top, "lat", [(i, i - 1) for i in range(1, bands)])
    above = lax.ppermute(bottom, "lat", [(i, i + 1) for i in range(bands - 1)])

    far = pack_strips(arrays, mask, after(embed, top), far_perm, core, False)
    far_halo = lax.ppermute(far, "lon", to_far)
    near = pack_strips(arrays, mask, after(embed, far), near_perm, core, True)
    near_halo = lax.ppermute(near, "lon", to_near)

    flags = jnp.stack([0 * lat, lat == 0, lat == bands - 1]).astype(jnp.int32)
    bias = window_bias(after(rel_table, near), flags)

    far_c, near_c, mid_c = pack_corners(top, bottom, below, above, all_perm, core)
    far_halo_c = lax.ppermute(far_c, "lon", to_far)
    near_halo_c = lax.ppermute(near_c, "lon", to_near)

    partial = inner(
        arrays, mask, embed, mid_perm, mid_c, near, near_c, near_halo, near_halo_c, bias,
        near_back, core,
    )
    final = outer(partial, far, far_c, far_halo, far_halo_c, bias, far_back, core)
    return tuple(x.reshape(queries.shape) for x in final)


def solution(mesh):
    tokens = P(None, "lat", "lon", None)
    return jax.shard_map(
        shards,
        mesh=mesh,
        in_specs=(tokens, tokens, tokens, tokens, P("lat", "lon"), P(), P()),
        out_specs=(tokens,) * 4,
        check_vma=False,
    )
```

time: 401 us -> 141 us (0.35)
  the two profiles are of different devices: /device:TPU:17 before, /device:TPU:8 now
where the time goes in v1:
time: 141 us; the launch traced here: 140 us
  Pallas kernels  85.6 us (61%)
  waiting for transfers between devices  30.5 us (22%)
  starting transfers between devices  16.8 us (12%)
  local copies, waits for them, and re-layouts  4.63 us (3%)
    pallas_call x1, Pallas kernels, inner(): pl.pallas_call(inner_body, grid_spec=pltpu.PrefetchScalarGridSpec(num_sca...  40.2 us
    ppermute x1, waiting for transfers between devices, shards(): above = lax.ppermute(bottom, 'lat', [(i, i + 1) for i in range(bands - 1)])  29.8 us
    pallas_call x1, Pallas kernels, outer(): pl.pallas_call(outer_body, grid_spec=pltpu.PrefetchScalarGridSpec(num_sca...  21.7 us
    pallas_call x2, Pallas kernels, pack_strips(): pl.pallas_call(functools.partial(strips_body, flip), grid_spec=pltpu.Pref...  8.48 us
    pallas_call x1, Pallas kernels, window_bias(): pl.pallas_call(bias_body, grid_spec=pltpu.PrefetchScalarGridSpec(num_scal...  8.26 us
    ppermute x1, starting transfers between devices, shards(): far_halo = lax.ppermute(far, 'lon', to_far)  4.47 us
    pallas_call x1, Pallas kernels, pack_corners(): pl.pallas_call(corners_body, grid_spec=pltpu.PrefetchScalarGridSpec(num_s...  4.44 us
    ppermute x1, starting transfers between devices, shards(): far_halo_c = lax.ppermute(far_c, 'lon', to_far)  4.25 us
  transfers between devices with their start and end apart: 6, of which 2 were waited for; matrix products, arithmetic and copies ran while one was open for 1% of the time, Pallas kernels for 38%

profile of v1, /device:TPU:8, one launch (start us, length us, event | category | flops | bytes accessed | tf_op | source)
XLA Modules:
  0.0 139.7 jit_solution(10258505245017133164)
XLA Ops:
  0.6 0.7 fusion
  1.4 0.1 copy.25
  1.4 0.1 broadcast_in_dim.13
  1.5 0.1 copy.24
  1.6 1.1 broadcast_in_dim.14.m0.m1
  2.7 2.4 %edge_rows.1 = (bf16[4,2,72,512]{3,2,1,0:T(8,128)(2,1)}, bf16[4,2,72,512]{3,2,1,0:T(8,128)(2,1)}) custom-call(bf16[2,16,72,512]{3,2,1,0:T(8,128)(2,1)} %bitcast.22, bf16[2,16,72,512]{3,2,1,0:T(8,128)(2,1)} %bitcast.23, bf16[2,16,72,512]{3,2,1,0:T(8,128)(2,1)} %bitcast.28, bf16[2,16,72,512]{3,2,1,0:T(8,128)(2,1)} %bitcast.29, ...), custom_call_target="tpu_custom_call" | custom-call | bytes 5242880 | tf_op jit(solution)/shard_map/edge_rows/pallas_call | solution.py:84
  5.1 1.0 broadcast_in_dim.12.mask
  6.1 4.1 %pack_far.1.own = bf16[4,7,72,512]{3,2,1,0:T(8,128)(2,1)} custom-call(s32[1]{0:T(128)} %bitcast.core, bf16[2,48,3,8,512]{4,3,2,1,0:T(8,128)(2,1)} %bitcast.24, bf16[2,48,3,8,512]{4,3,2,1,0:T(8,128)(2,1)} %bitcast.30, bf16[2,48,3,8,512]{4,3,2,1,0:T(8,128)(2,1)} %bitcast.36, bf16[2,48,3,8,512]{4,3,2,1,0:T(8,128)(2,1)} %bitcast.42, ...), custom_call_target="tpu_custom_call" | custom-call | flops 198180864 | bytes 6291456 | tf_op jit(solution)/shard_map/pack_far/pallas_call | solution.py:136
  10.3 0.0 copy-start.4
  10.3 0.0 copy-start.3
  10.3 4.3 %pack_near.1.own = bf16[4,7,72,512]{3,2,1,0:T(8,128)(2,1)} custom-call(s32[1]{0:T(128)} %bitcast.core, bf16[2,48,3,8,512]{4,3,2,1,0:T(8,128)(2,1)} %bitcast.25, bf16[2,48,3,8,512]{4,3,2,1,0:T(8,128)(2,1)} %bitcast.31, bf16[2,48,3,8,512]{4,3,2,1,0:T(8,128)(2,1)} %bitcast.37, bf16[2,48,3,8,512]{4,3,2,1,0:T(8,128)(2,1)} %bitcast.43, ...), custom_call_target="tpu_custom_call" | custom-call | flops 198180864 | bytes 6291456 | tf_op jit(solution)/shard_map/pack_near/pallas_call | solution.py:136
  14.7 0.0 copy-start.6
  14.7 0.1 collective-permute-start.4
  14.8 3.8 %collective-permute-start.1 = (bf16[4,2,72,512]{3,2,1,0:T(8,128)(2,1)S(1)}, bf16[4,2,72,512]{3,2,1,0:T(8,128)(2,1)S(1)}, u32[]{:S(2)}, u32[]{:S(2)}) collective-permute-start(bf16[4,2,72,512]{3,2,1,0:T(8,128)(2,1)S(1)} %copy-done.4), channel_id=1, source_target_pairs={{0,16},{16,32},{32,48},{48,64},{64,80},{80,96},{96,112},{1,17},{17... | collective-permute-start | bytes 1769480 | tf_op jit(solution)/shard_map/ppermute | solution.py:647
  18.6 4.1 %collective-permute-start = (bf16[4,2,72,512]{3,2,1,0:T(8,128)(2,1)S(1)}, bf16[4,2,72,512]{3,2,1,0:T(8,128)(2,1)}, u32[]{:S(2)}, u32[]{:S(2)}) collective-permute-start(bf16[4,2,72,512]{3,2,1,0:T(8,128)(2,1)S(1)} %copy-done.3), channel_id=1, source_target_pairs={{16,0},{32,16},{48,32},{64,48},{80,64},{96,80},{112,96},{17,1},{33... | collective-permute-start | bytes 1769480 | tf_op jit(solution)/shard_map/ppermute | solution.py:646
  22.8 4.5 %collective-permute-start.2 = (bf16[4,7,72,512]{3,2,1,0:T(8,128)(2,1)S(1)}, bf16[4,7,72,512]{3,2,1,0:T(8,128)(2,1)}, u32[]{:S(2)}, u32[]{:S(2)}) collective-permute-start(bf16[4,7,72,512]{3,2,1,0:T(8,128)(2,1)S(1)} %copy-done), channel_id=1, source_target_pairs={{1,2},{3,4},{5,6},{7,8},{9,10},{11,12},{13,14},{15,0},{2,1},{4,3},... | collective-permute-start | bytes 6193160 | tf_op jit(solution)/shard_map/ppermute | solution.py:650
  27.2 29.8 %collective-permute-done.1.above = bf16[4,2,72,512]{3,2,1,0:T(8,128)(2,1)S(1)} collective-permute-done((bf16[4,2,72,512]{3,2,1,0:T(8,128)(2,1)S(1)}, bf16[4,2,72,512]{3,2,1,0:T(8,128)(2,1)S(1)}, u32[]{:S(2)}, u32[]{:S(2)}) %collective-permute-start.1) | collective-permute-done | bytes 589856 | tf_op jit(solution)/shard_map/ppermute | solution.py:647
  57.0 0.8 copy-done.5
  57.9 0.7 collective-permute-done.below
  58.5 4.4 %pack_corners.1 = (bf16[4,2,72,512]{3,2,1,0:T(8,128)(2,1)}, bf16[4,2,72,512]{3,2,1,0:T(8,128)(2,1)}, bf16[4,2,144,512]{3,2,1,0:T(8,128)(2,1)}) custom-call(s32[1]{0:T(128)} %bitcast.core, bf16[4,2,72,512]{3,2,1,0:T(8,128)(2,1)} %get-tuple-element.20.top, bf16[4,2,72,512]{3,2,1,0:T(8,128)(2,1)} %get-tuple-element.22.bottom, ...), custom_call_target="tpu_custom_call" | custom-call | flops 679477248 | bytes 5242880 | tf_op jit(solution)/shard_map/pack_corners/pallas_call | solution.py:180
  63.0 0.0 collective-permute-start.5
  63.0 0.6 pad.4.table
  63.6 0.6 add_convert_fusion.flags
  64.2 8.3 %window_bias.1.bias = f32[3,2,144,576]{3,2,1,0:T(8,128)} custom-call(s32[3]{0:T(128)} %add_convert_fusion.flags, f32[8,768]{1,0:T(8,128)} %pad.4.table, bf16[1536,576]{1,0:T(8,128)(2,1)} %constant.52.clone.hot, bf16[144,192]{1,0:T(8,128)(2,1)} %constant.53.clone.squeeze), custom_call_target="tpu_custom_call" | custom-call | flops 2038431744 | bytes 4194304 | tf_op jit(solution)/shard_map/window_bias/pallas_call | solution.py:576
  72.5 4.3 %collective-permute-start.3 = (bf16[4,2,72,512]{3,2,1,0:T(8,128)(2,1)S(1)}, bf16[4,2,72,512]{3,2,1,0:T(8,128)(2,1)S(1)}, u32[]{:S(2)}, u32[]{:S(2)}) collective-permute-start(bf16[4,2,72,512]{3,2,1,0:T(8,128)(2,1)S(1)} %copy-done.1), channel_id=1, source_target_pairs={{1,2},{3,4},{5,6},{7,8},{9,10},{11,12},{13,14},{15,0},{2,1},{4,3},... | collective-permute-start | bytes 1769480 | tf_op jit(solution)/shard_map/ppermute | solution.py:658
  76.7 0.0 collective-permute-done.5.halo_c
  76.7 0.0 collective-permute-done.4.halo
  76.7 40.2 %inner_windows.1 = (bf16[2,16,72,512]{3,2,1,0:T(8,128)(2,1)}, bf16[2,16,72,512]{3,2,1,0:T(8,128)(2,1)}, bf16[2,16,72,512]{3,2,1,0:T(8,128)(2,1)}, bf16[2,16,72,512]{3,2,1,0:T(8,128)(2,1)}) custom-call(s32[1]{0:T(128)} %bitcast.core, bf16[2,16,72,512]{3,2,1,0:T(8,128)(2,1)} %bitcast.26, bf16[2,16,72,512]{3,2,1,0:T(8,128)(2,1)} %bitcast.27, ...), custom_call_target="tpu_custom_call" | custom-call | flops 9172942848 | bytes 25165824 | tf_op jit(solution)/shard_map/inner_windows/pallas_call | solution.py:375
  117.0 0.0 collective-permute-done.3.halo_c
  117.0 0.0 collective-permute-done.2.halo
  117.0 0.8 copy-done.2
  117.8 21.7 %outer_windows.1 = (bf16[2,48,3,8,512]{4,3,2,1,0:T(8,128)(2,1)}, bf16[2,48,3,8,512]{4,3,2,1,0:T(8,128)(2,1)}, bf16[2,48,3,8,512]{4,3,2,1,0:T(8,128)(2,1)}, bf16[2,48,3,8,512]{4,3,2,1,0:T(8,128)(2,1)}) custom-call(s32[1]{0:T(128)} %bitcast.core, ...), custom_call_target="tpu_custom_call", output_to_operand_aliasing={{0}: (7, {}), {1}: (8, {}), {2}: (9, {}), {3}: (10, {})} | custom-call | flops 4586471424 | bytes 12582912 | tf_op jit(solution)/shard_map/outer_windows/pallas_call | solution.py:497
  (9 shorter events, 0.0 us)
Async XLA Ops:
  10.3 4.5 %copy-start.4 = (bf16[4,2,72,512]{3,2,1,0:T(8,128)(2,1)S(1)}, bf16[4,2,72,512]{3,2,1,0:T(8,128)(2,1)}, u32[]{:S(2)}) copy-start(bf16[4,2,72,512]{3,2,1,0:T(8,128)(2,1)} %get-tuple-element.22.bottom) | copy-start | bytes 1769476
  10.3 8.3 %copy-start.3 = (bf16[4,2,72,512]{3,2,1,0:T(8,128)(2,1)S(1)}, bf16[4,2,72,512]{3,2,1,0:T(8,128)(2,1)}, u32[]{:S(2)}) copy-start(bf16[4,2,72,512]{3,2,1,0:T(8,128)(2,1)} %get-tuple-element.20.top) | copy-start | bytes 1769476
  10.3 12.5 %copy-start = (bf16[4,7,72,512]{3,2,1,0:T(8,128)(2,1)S(1)}, bf16[4,7,72,512]{3,2,1,0:T(8,128)(2,1)}, u32[]{:S(2)}) copy-start(bf16[4,7,72,512]{3,2,1,0:T(8,128)(2,1)} %pack_far.1.own) | copy-start | bytes 6193156
  14.7 48.3 %copy-start.6 = (f32[8,759]{1,0:T(8,128)S(1)}, f32[8,759]{1,0:T(8,128)}, u32[]{:S(2)}) copy-start(f32[8,759]{1,0:T(8,128)} %param.21) | copy-start | bytes 72868
  14.7 62.0 %collective-permute-start.4 = (bf16[4,7,72,512]{3,2,1,0:T(8,128)(2,1)}, bf16[4,7,72,512]{3,2,1,0:T(8,128)(2,1)}, u32[]{:S(2)}, u32[]{:S(2)}) collective-permute-start(bf16[4,7,72,512]{3,2,1,0:T(8,128)(2,1)} %pack_near.1.own), channel_id=1, source_target_pairs={{0,1},{1,0},{2,3},{3,2},{4,5},{5,4},{6,7},{7,6},{8,9},{9,8},{10,11... | collective-permute-start | bytes 6193160 | tf_op jit(solution)/shard_map/ppermute | solution.py:652
  14.8 42.2 %collective-permute-start.1 = (bf16[4,2,72,512]{3,2,1,0:T(8,128)(2,1)S(1)}, bf16[4,2,72,512]{3,2,1,0:T(8,128)(2,1)S(1)}, u32[]{:S(2)}, u32[]{:S(2)}) collective-permute-start(bf16[4,2,72,512]{3,2,1,0:T(8,128)(2,1)S(1)} %copy-done.4), channel_id=1, source_target_pairs={{0,16},{16,32},{32,48},{48,64},{64,80},{80,96},{96,112},{1,17},{17... | collective-permute-start | bytes 1769480 | tf_op jit(solution)/shard_map/ppermute | solution.py:647
  18.6 39.9 %collective-permute-start = (bf16[4,2,72,512]{3,2,1,0:T(8,128)(2,1)S(1)}, bf16[4,2,72,512]{3,2,1,0:T(8,128)(2,1)}, u32[]{:S(2)}, u32[]{:S(2)}) collective-permute-start(bf16[4,2,72,512]{3,2,1,0:T(8,128)(2,1)S(1)} %copy-done.3), channel_id=1, source_target_pairs={{16,0},{32,16},{48,32},{64,48},{80,64},{96,80},{112,96},{17,1},{33... | collective-permute-start | bytes 1769480 | tf_op jit(solution)/shard_map/ppermute | solution.py:646
  22.8 94.2 %collective-permute-start.2 = (bf16[4,7,72,512]{3,2,1,0:T(8,128)(2,1)S(1)}, bf16[4,7,72,512]{3,2,1,0:T(8,128)(2,1)}, u32[]{:S(2)}, u32[]{:S(2)}) collective-permute-start(bf16[4,7,72,512]{3,2,1,0:T(8,128)(2,1)S(1)} %copy-done), channel_id=1, source_target_pairs={{1,2},{3,4},{5,6},{7,8},{9,10},{11,12},{13,14},{15,0},{2,1},{4,3},... | collective-permute-start | bytes 6193160 | tf_op jit(solution)/shard_map/ppermute | solution.py:650
  57.0 0.8 copy-start.5
  63.0 13.7 %collective-permute-start.5 = (bf16[4,2,72,512]{3,2,1,0:T(8,128)(2,1)}, bf16[4,2,72,512]{3,2,1,0:T(8,128)(2,1)}, u32[]{:S(2)}, u32[]{:S(2)}) collective-permute-start(bf16[4,2,72,512]{3,2,1,0:T(8,128)(2,1)} %get-tuple-element.27.own_c), channel_id=1, source_target_pairs={{0,1},{1,0},{2,3},{3,2},{4,5},{5,4},{6,7},{7,6},{8,9},{9,8},{10,11... | collective-permute-start | bytes 1769480 | tf_op jit(solution)/shard_map/ppermute | solution.py:659
  64.2 8.3 %copy-start.1 = (bf16[4,2,72,512]{3,2,1,0:T(8,128)(2,1)S(1)}, bf16[4,2,72,512]{3,2,1,0:T(8,128)(2,1)}, u32[]{:S(2)}) copy-start(bf16[4,2,72,512]{3,2,1,0:T(8,128)(2,1)} %get-tuple-element.23.own_c) | copy-start | bytes 1769476
  72.5 44.5 %collective-permute-start.3 = (bf16[4,2,72,512]{3,2,1,0:T(8,128)(2,1)S(1)}, bf16[4,2,72,512]{3,2,1,0:T(8,128)(2,1)S(1)}, u32[]{:S(2)}, u32[]{:S(2)}) collective-permute-start(bf16[4,2,72,512]{3,2,1,0:T(8,128)(2,1)S(1)} %copy-done.1), channel_id=1, source_target_pairs={{1,2},{3,4},{5,6},{7,8},{9,10},{11,12},{13,14},{15,0},{2,1},{4,3},... | collective-permute-start | bytes 1769480 | tf_op jit(solution)/shard_map/ppermute | solution.py:658
  117.0 0.8 copy-start.2

commit v2 on v1

v2 whole, which is shorter than its diff:
```python
import functools

import jax
import jax.numpy as jnp
import numpy as np
from jax import lax
from jax.experimental import pallas as pl
from jax.experimental.pallas import tpu as pltpu
from jax.sharding import PartitionSpec as P

F32 = jnp.float32
BF16 = jnp.bfloat16
HALF = 36
STRIP = 72
WIN = 144
GROUP = 256
MIB = 1 << 20
VMEM_BYTES = 60 * MIB


def strip_matrix(strips):
    out = np.zeros((len(strips), 2, 2, 3, 6, 2, 2, 3, 24), np.float32)
    for place, strip in enumerate(strips):
        for part in range(2):
            for lev in range(2):
                for row in range(3):
                    for col in range(6):
                        out[place, part, lev, row, col, part, lev, row, 6 * strip + col] = 1
    return out.reshape(len(strips) * STRIP, 2 * WIN)


def far_matrix(strip, tile):
    full = strip_matrix([strip]).reshape(STRIP, 2, 2, 3, 3, 8)
    return full[:, :, :, :, tile].reshape(STRIP, 96)


def run_bases():
    run = np.arange(24)
    half, part, lev, row = run // 12, run // 6 % 2, run // 3 % 2, run % 3
    return lev * 253 + (row + 3 * (1 - part)) * 23 + 6 * half


def dot(a, b, ca=1, cb=0):
    return lax.dot_general(a, b, (((ca,), (cb,)), ((), ())), preferred_element_type=F32)


def keyed_rows(key, mask, embed):
    wide = jnp.concatenate([mask] * 4, axis=-1)
    return (key + (wide * embed)[None]).astype(BF16).astype(F32)


def side_spec(shape):
    return pl.BlockSpec((1, *shape), lambda s, core: (core[0],) + (0,) * len(shape))


def fixed_spec(shape):
    return pl.BlockSpec(shape, lambda s, core: (0,) * len(shape))


def params():
    return pltpu.CompilerParams(vmem_limit_bytes=VMEM_BYTES)


def edges_body(core, q, k, v, g, mask, embed, far_perm, near_perm, far, near, top, bottom, held, packed, rows, came, gone, rows_came, rows_gone):
    sources = (q, k, v, g)
    tiles = (2 * core[0], 2 - 2 * core[0])

    def fetch(side, index):
        return pltpu.make_async_copy(
            sources[index].at[:, :, tiles[side]], held.at[side, index], came.at[side, index]
        )

    def send_off(side, index):
        return pltpu.make_async_copy(
            packed.at[side, index], (far, near)[side].at[index], gone.at[side, index]
        )

    ends = ((top, 0), (bottom, 45))

    def end_rows(end, index):
        out, row = ends[end]
        if index == 1:
            return pltpu.make_async_copy(rows.at[end], out.at[1], rows_gone.at[end, 1])
        return pltpu.make_async_copy(
            sources[index].at[:, row : row + 3], out.at[index], rows_gone.at[end, index]
        )

    def key_rows(end):
        row = ends[end][1]
        return pltpu.make_async_copy(k.at[:, row : row + 3], rows.at[end], rows_came.at[end])

    for index in range(4):
        fetch(0, index).start()
    for end in range(2):
        key_rows(end).start()
    for index in range(4):
        fetch(1, index).start()
    for end in range(2):
        for index in (0, 2, 3):
            end_rows(end, index).start()
    for side in range(2):
        perm = (far_perm, near_perm)[side]
        for index in range(4):
            fetch(side, index).wait()
            for band in range(1, 8):
                lower, upper = 6 * band, 6 * band - 3
                opening = held[side, index, :, lower : lower + 3].astype(F32)
                closing = held[side, index, :, upper : upper + 3].astype(F32)
                if index == 1:
                    opening = keyed_rows(
                        opening, mask[lower : lower + 3, pl.ds(tiles[side], 1)][:, 0], embed[...]
                    )
                    closing = keyed_rows(
                        closing, mask[upper : upper + 3, pl.ds(tiles[side], 1)][:, 0], embed[...]
                    )
                tokens = jnp.concatenate(
                    [opening.reshape(48, 512), closing.reshape(48, 512)], axis=0
                )
                strip = dot(perm[0], tokens.astype(BF16))
                if index == 0:
                    strip = strip * 0.125
                packed[side, index, band - 1] = strip.astype(BF16)
            send_off(side, index).start()
        if side == 0:
            for end in range(2):
                key_rows(end).wait()
                row = ends[end][1]
                keyed = keyed_rows(rows[end].astype(F32), mask[row : row + 3], embed[...])
                rows[end] = keyed.astype(BF16)
                end_rows(end, 1).start()
    for index in range(4):
        for side in range(2):
            send_off(side, index).wait()
        for end in range(2):
            end_rows(end, index).wait()


def pack_edges(arrays, mask, embed, far_perm, near_perm, core):
    tiles = [array.reshape(2, 48, 3, 8, 512) for array in arrays]
    anywhere = pl.BlockSpec(memory_space=pl.ANY)
    strips = jax.ShapeDtypeStruct((4, 7, STRIP, 512), BF16)
    ends = jax.ShapeDtypeStruct((4, 2, 3, 3, 8, 512), BF16)
    return pl.pallas_call(
        edges_body,
        grid_spec=pltpu.PrefetchScalarGridSpec(
            num_scalar_prefetch=1,
            grid=(1,),
            in_specs=[anywhere] * 4
            + [
                fixed_spec((48, 3, 8, 128)),
                fixed_spec((1, 512)),
                side_spec((STRIP, 96)),
                side_spec((STRIP, 96)),
            ],
            out_specs=[anywhere] * 4,
            scratch_shapes=[
                pltpu.VMEM((2, 4, 2, 48, 8, 512), BF16),
                pltpu.VMEM((2, 4, 7, STRIP, 512), BF16),
                pltpu.VMEM((2, 2, 3, 3, 8, 512), BF16),
                pltpu.SemaphoreType.DMA((2, 4)),
                pltpu.SemaphoreType.DMA((2, 4)),
                pltpu.SemaphoreType.DMA((2,)),
                pltpu.SemaphoreType.DMA((2, 4)),
            ],
        ),
        out_shape=[strips, strips, ends, ends],
        compiler_params=params(),
        cost_estimate=pl.CostEstimate(
            flops=2 * 56 * STRIP * 96 * 512, bytes_accessed=16 * MIB, transcendentals=0
        ),
        name="pack_edges",
    )(core, *tiles, mask.reshape(48, 3, 8, 128), embed, far_perm, near_perm)


def corners_body(core, top, bottom, below, above, perm, far, near, mid):
    for index in range(4):
        for place, (first, second) in enumerate(((top, above), (below, bottom))):
            first = first[index].astype(F32)
            second = second[index].astype(F32)
            tokens = jnp.concatenate([first[0], first[1], second[0], second[1]], axis=0)
            strips = dot(perm[0], tokens.astype(BF16))
            if index == 0:
                strips = strips * 0.125
            far[index, place] = strips[:STRIP].astype(BF16)
            near[index, place] = strips[STRIP : 2 * STRIP].astype(BF16)
            mid[index, place] = strips[2 * STRIP :].astype(BF16)


def pack_corners(top, bottom, below, above, perm, core):
    sizes = (STRIP, STRIP, WIN)
    return pl.pallas_call(
        corners_body,
        grid_spec=pltpu.PrefetchScalarGridSpec(
            num_scalar_prefetch=1,
            grid=(1,),
            in_specs=[fixed_spec((4, 2, STRIP, 512))] * 4 + [side_spec((2 * WIN, 2 * WIN))],
            out_specs=[fixed_spec((4, 2, size, 512)) for size in sizes],
        ),
        out_shape=[jax.ShapeDtypeStruct((4, 2, size, 512), BF16) for size in sizes],
        compiler_params=params(),
        cost_estimate=pl.CostEstimate(
            flops=2 * 8 * 288 * 288 * 512, bytes_accessed=5 * MIB, transcendentals=0
        ),
        name="pack_corners",
    )(core, top, bottom, below, above, perm)


def windows(win, slots, bias, scores, grads, low, dlow, store):
    lane = lax.broadcasted_iota(jnp.int32, (1, GROUP), 1) // 64

    def spread(x):
        return jnp.concatenate(
            [x * jnp.where(lane == h, 1.0, 0.0).astype(BF16) for h in range(4)], axis=0
        )

    def by_head(wide):
        total = None
        for h in range(4):
            piece = jnp.where(lane == h, wide[WIN * h : WIN * (h + 1)], 0.0)
            total = piece if total is None else total + piece
        return total

    jobs = []
    for slot in range(slots):
        for group in range(2):
            cols = slice(GROUP * group, GROUP * (group + 1))
            q, k, v, g = (win[slot, index, :, cols] for index in range(4))
            q_wide, g_wide = spread(q), spread(g)
            place = 2 * slot + group
            scores[place] = dot(k, q_wide, 1, 1)
            grads[place] = dot(v, g_wide, 1, 1)
            jobs.append((slot, group, place, cols, k, v, q_wide, g_wide))
    for slot, group, place, cols, k, v, q_wide, g_wide in jobs:
        for start in range(0, 576, 128):
            part = slice(start, min(start + 128, 576))
            s = scores[place, :, part] + bias[0, group, :, part]
            e = jnp.exp(s - jnp.max(s, axis=0, keepdims=True))
            p = e * (1.0 / jnp.sum(e, axis=0, keepdims=True))
            gp = grads[place, :, part]
            delta = jnp.sum(p * gp, axis=0, keepdims=True)
            low[place, :, part] = p.astype(BF16)
            dlow[place, :, part] = (p * (gp - delta)).astype(BF16)
        p_low, d_low = low[place], dlow[place]
        store(slot, 0, cols, by_head(dot(p_low, v, 0, 0)))
        store(slot, 1, cols, by_head(dot(d_low, k, 0, 0)) * 0.125)
        store(slot, 2, cols, dot(d_low, q_wide))
        store(slot, 3, cols, dot(p_low, g_wide))


def place_pair(win, slot, own, halo, own_left):
    def put(left, right):
        for index in range(4):
            both = jnp.concatenate(
                [left[index, 0].astype(F32), right[index, 0].astype(F32)], axis=0
            )
            win[slot, index] = both.astype(BF16)

    @pl.when(own_left)
    def _():
        put(own, halo)

    @pl.when(jnp.logical_not(own_left))
    def _():
        put(halo, own)


def inner_body(core, q0, q1, k0, k1, v0, v1, g0, g1, m0, m1, embed, perm, own, halo, bias, back, *rest):
    outs, token, (win, result, ready, gone), work = rest[:4], rest[4], rest[5:9], rest[9:]
    s = pl.program_id(0)
    for index, pair in enumerate(((q0, q1), (k0, k1), (v0, v1), (g0, g1))):
        first, second = (source[:, 0].astype(F32) for source in pair)
        if index == 1:
            first = keyed_rows(first, m0[0], embed[...])
            second = keyed_rows(second, m1[0], embed[...])
        tokens = jnp.concatenate([first[0], first[1], second[0], second[1]], axis=0)
        packed = dot(perm[...], tokens.astype(BF16))
        if index == 0:
            packed = packed * 0.125
        win[0, index] = packed.astype(BF16)
    place_pair(win, 1, own, halo, core[0] == 0)

    starts = (pl.multiple_of(WIN * core[0], 16), pl.multiple_of(WIN * (1 - core[0]), 16))

    def keep(slot, index, cols, value):
        result[index, pl.ds(starts[slot], WIN), cols] = value.astype(BF16)

    windows(win, 2, bias, *work, keep)

    def leave(slot, step):
        copies = []
        for index, out in enumerate(outs):
            for part in range(2):
                copies.append(
                    pltpu.make_async_copy(
                        ready.at[slot, index, part],
                        out.at[:, 2 * step + 2 - part],
                        gone.at[slot, index, part],
                    )
                )
        return copies

    slot = s % 2

    @pl.when(s >= 2)
    def _():
        for copy in leave(slot, s - 2):
            copy.wait()

    used = pl.ds(pl.multiple_of(64 * core[0], 16), 224)
    for index in range(4):
        full = dot(back[0], result[index, used])
        ready[slot, index] = full.reshape(2, 2, STRIP, 512).astype(BF16)
    for copy in leave(slot, s):
        copy.start()

    @pl.when(s == 6)
    def _():
        token[...] = jnp.zeros_like(token)
        for copy in leave(1, 5) + leave(0, 6):
            copy.wait()


def work_scratch(places):
    return [
        pltpu.VMEM((places, WIN, 576), F32),
        pltpu.VMEM((places, WIN, 576), F32),
        pltpu.VMEM((places, WIN, 576), BF16),
        pltpu.VMEM((places, WIN, 576), BF16),
    ]


def window_cost(count, moved):
    return pl.CostEstimate(
        flops=count * 6 * 2 * WIN * WIN * 512 * 4,
        bytes_accessed=moved,
        transcendentals=count * 8 * WIN * WIN,
    )


def inner(arrays, mask, embed, perm, own, halo, bias, back, core):
    operands, specs = [], []
    block = (2, 1, STRIP, 512)
    for array in arrays:
        array = array.reshape(2, 16, STRIP, 512)
        operands += [array, array]
        specs += [
            pl.BlockSpec(block, lambda s, core: (0, 2 * s + 2, 0, 0)),
            pl.BlockSpec(block, lambda s, core: (0, 2 * s + 1, 0, 0)),
        ]
    anywhere = pl.BlockSpec(memory_space=pl.ANY)
    return pl.pallas_call(
        inner_body,
        grid_spec=pltpu.PrefetchScalarGridSpec(
            num_scalar_prefetch=1,
            grid=(7,),
            in_specs=specs
            + [
                pl.BlockSpec((1, STRIP, 128), lambda s, core: (2 * s + 2, 0, 0)),
                pl.BlockSpec((1, STRIP, 128), lambda s, core: (2 * s + 1, 0, 0)),
                fixed_spec((1, 512)),
                fixed_spec((WIN, 2 * WIN)),
                band_spec(),
                band_spec(),
                fixed_spec((1, 2, WIN, 576)),
                side_spec((2 * WIN, 224)),
            ],
            out_specs=[anywhere] * 4 + [fixed_spec((8, 128))],
            scratch_shapes=[
                pltpu.VMEM((2, 4, WIN, 512), BF16),
                pltpu.VMEM((4, 2 * WIN, 512), BF16),
                pltpu.VMEM((2, 4, 2, 2, STRIP, 512), BF16),
                pltpu.SemaphoreType.DMA((2, 4, 2)),
            ]
            + work_scratch(4),
        ),
        out_shape=[jax.ShapeDtypeStruct((2, 16, STRIP, 512), BF16)] * 4
        + [jax.ShapeDtypeStruct((8, 128), F32)],
        compiler_params=params(),
        cost_estimate=window_cost(14, 24 * MIB),
        name="inner_windows",
    )(core, *operands, mask, mask, embed, perm, own, halo, bias, back)


def band_spec():
    return pl.BlockSpec((4, 1, STRIP, 512), lambda s, core: (0, s, 0, 0))


def outer_body(core, own, halo, bias, back, p0, p1, p2, p3, o0, o1, o2, o3, win, result, tiles, came, gone, *work):
    s = pl.program_id(0)
    tile = 2 * core[0]
    outs = (o0, o1, o2, o3)

    def arrivals():
        return [
            pltpu.make_async_copy(out.at[:, 3:45, tile], tiles.at[index], came.at[index])
            for index, out in enumerate(outs)
        ]

    @pl.when(s == 0)
    def _():
        for copy in arrivals():
            copy.start()

    place_pair(win, 0, own, halo, core[0] == 1)

    def keep(slot, index, cols, value):
        result[index, :, cols] = value.astype(BF16)

    windows(win, 1, bias, *work, keep)

    @pl.when(s == 0)
    def _():
        for copy in arrivals():
            copy.wait()

    used = pl.ds(pl.multiple_of(64 * (1 - core[0]), 16), 80)

    def leave(step, index):
        return pltpu.make_async_copy(
            tiles.at[index, :, pl.ds(6 * step, 6)],
            outs[index].at[:, pl.ds(6 * step + 3, 6), tile],
            gone.at[step, index],
        )

    for index in range(4):
        full = dot(back[0], result[index, used]).reshape(2, 2, 3, 8, 512)
        for part in range(2):
            span = pl.ds(6 * s + 3 * (1 - part), 3)
            total = tiles[index, :, span].astype(F32) + full[part]
            tiles[index, :, span] = total.astype(BF16)
        leave(s, index).start()

    @pl.when(s == 6)
    def _():
        for index in range(4):
            for step in range(7):
                leave(step, index).wait()


def outer(partial, own, halo, bias, back, core):
    anywhere = pl.BlockSpec(memory_space=pl.ANY)
    shape = (2, 48, 3, 8, 512)
    return pl.pallas_call(
        outer_body,
        grid_spec=pltpu.PrefetchScalarGridSpec(
            num_scalar_prefetch=1,
            grid=(7,),
            in_specs=[
                band_spec(),
                band_spec(),
                fixed_spec((1, 2, WIN, 576)),
                side_spec((96, 80)),
            ]
            + [anywhere] * 4,
            out_specs=[anywhere] * 4,
            scratch_shapes=[
                pltpu.VMEM((1, 4, WIN, 512), BF16),
                pltpu.VMEM((4, WIN, 512), BF16),
                pltpu.VMEM((4, 2, 42, 8, 512), BF16),
                pltpu.SemaphoreType.DMA((4,)),
                pltpu.SemaphoreType.DMA((7, 4)),
            ]
            + work_scratch(2),
        ),
        out_shape=[jax.ShapeDtypeStruct(shape, BF16)] * 4,
        input_output_aliases={5 + index: index for index in range(4)},
        compiler_params=params(),
        cost_estimate=window_cost(7, 12 * MIB),
        name="outer_windows",
    )(core, own, halo, bias, back, *[x.reshape(shape) for x in partial])


def corner_body(core, flags, mid, near, near_halo, far, far_halo, bias, back, p0, p1, p2, p3, o0, o1, o2, o3, win, result, cut, *work):
    s = pl.program_id(0)
    left = core[0] == 0
    for index in range(4):
        win[1, index] = mid[index, 0]
    place_pair(win, 0, far, far_halo, jnp.logical_not(left))
    place_pair(win, 2, near, near_halo, left)

    key_part = lax.broadcasted_iota(jnp.int32, (WIN, 576), 0) % STRIP < HALF
    query_part = lax.broadcasted_iota(jnp.int32, (WIN, 576), 1) % STRIP < HALF
    apart = (key_part != query_part) & (flags[s] != 0)
    for group in range(2):
        cut[0, group] = jnp.where(apart, -jnp.inf, bias[0, group])

    starts = (
        pl.multiple_of(2 * WIN * core[0], 16),
        WIN,
        pl.multiple_of(2 * WIN * (1 - core[0]), 16),
    )

    def keep(slot, index, cols, value):
        result[index, pl.ds(starts[slot], WIN), cols] = value.astype(BF16)

    windows(win, 3, cut, *work, keep)
    for index, out in enumerate((o0, o1, o2, o3)):
        full = dot(back[0], result[index, 64:368])
        out[:, 0] = full.reshape(2, STRIP, 512).astype(BF16)


def corners(partial, flags, mid, near, near_halo, far, far_halo, bias, back, core):
    anywhere = pl.BlockSpec(memory_space=pl.ANY)
    shape = (2, 16, STRIP, 512)

    def edge(size):
        return pl.BlockSpec((4, 1, size, 512), lambda s, core, flags: (0, s, 0, 0))

    return pl.pallas_call(
        corner_body,
        grid_spec=pltpu.PrefetchScalarGridSpec(
            num_scalar_prefetch=2,
            grid=(2,),
            in_specs=[
                edge(WIN),
                edge(STRIP),
                edge(STRIP),
                edge(STRIP),
                edge(STRIP),
                pl.BlockSpec((1, 2, WIN, 576), lambda s, core, flags: (0, 0, 0, 0)),
                pl.BlockSpec((1, WIN, 304), lambda s, core, flags: (s, 0, 0)),
            ]
            + [anywhere] * 4,
            out_specs=[
                pl.BlockSpec((2, 1, STRIP, 512), lambda s, core, flags: (0, 15 * s, 0, 0))
            ]
            * 4,
            scratch_shapes=[
                pltpu.VMEM((3, 4, WIN, 512), BF16),
                pltpu.VMEM((4, 3 * WIN, 512), BF16),
                pltpu.VMEM((1, 2, WIN, 576), F32),
            ]
            + work_scratch(6),
        ),
        out_shape=[jax.ShapeDtypeStruct(shape, BF16)] * 4,
        input_output_aliases={9 + index: index for index in range(4)},
        compiler_params=params(),
        cost_estimate=window_cost(6, 8 * MIB),
        name="corner_windows",
    )(
        core, flags, mid, near, near_halo, far, far_halo, bias, back,
        *[x.reshape(shape) for x in partial],
    )


def bias_body(table, hot, squeeze, out, wide, part):
    for head in range(8):
        line = jnp.broadcast_to(table[head : head + 1], (8, 768))
        line = pltpu.roll(line, 0, 1, stride=1, stride_axis=0)
        for run, base in enumerate(run_bases()):
            turn = int(base - 379) % 768
            turned = pltpu.roll(line, turn, 1)
            group, cols = head // 4, slice(384 * (head % 4), 384 * (head % 4) + 384)
            wide[group, 8 * run : 8 * run + 8, cols] = turned[:, :384]
    for group in range(2):
        high = wide[group].astype(BF16)
        part[0, group] = high
        part[1, group] = (wide[group] - high.astype(F32)).astype(BF16)
    for group in range(2):
        total = None
        for order in range(2):
            spread = dot(part[order, group], hot[...]).astype(BF16)
            piece = dot(squeeze[...], spread)
            total = piece if total is None else total + piece
        out[0, group] = total


def window_bias(rel_table):
    tokens = (run_bases()[:, None] + np.arange(6)).reshape(WIN)
    hot = np.zeros((4, 384, 4, WIN), np.float32)
    for head in range(4):
        hot[head, tokens, head, np.arange(WIN)] = 1
    squeeze = np.zeros((24, 6, 24, 8), np.float32)
    for run in range(24):
        squeeze[run, np.arange(6), run, np.arange(6)] = 1
    hot = jnp.asarray(hot.reshape(4 * 384, 4 * WIN), BF16)
    squeeze = jnp.asarray(squeeze.reshape(WIN, 192), BF16)
    table = jnp.pad(rel_table, ((0, 0), (0, 768 - rel_table.shape[1])))
    return pl.pallas_call(
        bias_body,
        out_shape=jax.ShapeDtypeStruct((1, 2, WIN, 576), F32),
        scratch_shapes=[
            pltpu.VMEM((2, 192, 4 * 384), F32),
            pltpu.VMEM((2, 2, 192, 4 * 384), BF16),
        ],
        compiler_params=params(),
        cost_estimate=pl.CostEstimate(
            flops=4 * 2 * 192 * 1536 * 576, bytes_accessed=3 * MIB, transcendentals=0
        ),
        name="window_bias",
    )(table, hot, squeeze)


def side_tables():
    far_strip, near_strip = (0, 3), (3, 0)
    far, near, whole, near_back, far_back = [], [], [], [], []
    for side in range(2):
        far.append(far_matrix(far_strip[side], 2 * side))
        near.append(far_matrix(near_strip[side], 2 - 2 * side))
        whole.append(strip_matrix([far_strip[side], near_strip[side], 1, 2]))
        own = strip_matrix([near_strip[side]]).T
        middle = strip_matrix([1, 2]).T
        pad = np.zeros((2 * WIN, 8), np.float32)
        pad_far = np.zeros((96, 8), np.float32)
        if side == 0:
            near_back.append(np.concatenate([middle, own, pad], axis=1))
            far_back.append(np.concatenate([pad_far, far[0].T], axis=1))
        else:
            near_back.append(np.concatenate([pad, own, middle], axis=1))
            far_back.append(np.concatenate([far[1].T, pad_far], axis=1))
    natural = strip_matrix([0, 1, 2, 3]).T.reshape(2, WIN, 2 * WIN)
    corner_back = np.pad(natural, ((0, 0), (0, 0), (8, 8)))
    stacked = (far, near, whole, near_back, far_back, corner_back)
    return [jnp.asarray(np.stack(table), BF16) for table in stacked]


def after(value, earlier):
    return lax.optimization_barrier((value, earlier))[0]


def shards(queries, key_tokens, value_tokens, out_grad, land_mask, land_embed, rel_table):
    lev, rows, cols, width = queries.shape
    lat = lax.axis_index("lat")
    core = jnp.reshape(lax.axis_index("lon") % 2, (1,))
    bands = lax.axis_size("lat")
    sectors = lax.axis_size("lon")
    arrays = (queries, key_tokens, value_tokens, out_grad)
    mask = jnp.broadcast_to(
        land_mask.astype(F32).reshape(rows // 3, STRIP, 1), (rows // 3, STRIP, 128)
    )
    embed = land_embed.reshape(1, width)
    far_perm, near_perm, all_perm, near_back, far_back, corner_back = side_tables()
    mid_perm = jnp.asarray(strip_matrix([1, 2]), BF16)

    to_far = [((2 * k + 1) % sectors, (2 * k + 2) % sectors) for k in range(sectors // 2)]
    to_far += [(b, a) for a, b in to_far]
    to_near = [(i, i ^ 1) for i in range(sectors)]

    far, near, top, bottom = pack_edges(arrays, mask, embed, far_perm, near_perm, core)
    ends = (4, 2, STRIP, width)
    top, bottom = top.reshape(ends), bottom.reshape(ends)
    far_halo = lax.ppermute(far, "lon", to_far)
    near_halo = lax.ppermute(near, "lon", to_near)
    below = lax.ppermute(top, "lat", [(i, i - 1) for i in range(1, bands)])
    above = lax.ppermute(bottom, "lat", [(i, i + 1) for i in range(bands - 1)])

    bias = window_bias(after(rel_table, far))
    *partial, done = inner(
        arrays, mask, embed, mid_perm, near, near_halo, bias, near_back, core
    )

    far_c, near_c, mid_c = pack_corners(top, bottom, below, above, all_perm, after(core, done))
    far_halo_c = lax.ppermute(far_c, "lon", to_far)
    near_halo_c = lax.ppermute(near_c, "lon", to_near)

    partial = outer(partial, far, far_halo, bias, far_back, core)
    flags = jnp.stack([lat == 0, lat == bands - 1]).astype(jnp.int32)
    final = corners(
        partial, flags, mid_c, near_c, near_halo_c, far_c, far_halo_c, bias, corner_back, core
    )
    return tuple(x.reshape(queries.shape) for x in final)


def solution(mesh):
    tokens = P(None, "lat", "lon", None)
    return jax.shard_map(
        shards,
        mesh=mesh,
        in_specs=(tokens, tokens, tokens, tokens, P("lat", "lon"), P(), P()),
        out_specs=(tokens,) * 4,
        check_vma=False,
    )
```

time: 141 us -> 166 us (1.18)
  starting transfers between devices: 16.8 us -> 36.4 us
  Pallas kernels: 85.6 us -> 96.1 us
  waiting for transfers between devices: 30.5 us -> 24.9 us
    pallas_call x4 -> x3, Pallas kernels: 19.2 us -> 46.6 us  [the longest x1 29.2 us: pack_edges(): pl.pallas_call(edges_body, grid_spec=pltpu.PrefetchScalarGridSpec(num_sca...]
    ppermute x1, waiting for transfers between devices: 29.8 us -> 5.17 us  [shards(): above = lax.ppermute(bottom, 'lat', [(i, i + 1) for i in range(bands - 1)])]
    ppermute x1, starting transfers between devices: 0.01 us -> 20.3 us  [shards(): near_halo_c = lax.ppermute(near_c, 'lon', to_near)]
    ppermute x1, waiting for transfers between devices: 0.69 us -> 19.7 us  [shards(): below = lax.ppermute(top, 'lat', [(i, i - 1) for i in range(1, bands)])]
    pallas_call x1, Pallas kernels: 40.2 us -> 28.4 us  [inner(): pl.pallas_call(inner_body, grid_spec=pltpu.PrefetchScalarGridSpec(num_sca...]
    pallas_call x1, Pallas kernels: 21.7 us -> 16.6 us  [outer(): pl.pallas_call(outer_body, grid_spec=pltpu.PrefetchScalarGridSpec(num_sca...]
    ppermute x1, starting transfers between devices: 4.13 us -> 6.72 us  [shards(): below = lax.ppermute(top, 'lat', [(i, i - 1) for i in range(1, bands)])]
    ppermute x1, starting transfers between devices: 3.82 us -> 1.92 us  [shards(): above = lax.ppermute(bottom, 'lat', [(i, i + 1) for i in range(bands - 1)])]
  transfers between devices with their start and end apart: 6 -> 6, of which waited for: 2 -> 2; matrix products, arithmetic and copies ran while one was open for 1% -> 2% of each run, Pallas kernels for 38% -> 33%
where the time goes in v2:
time: 166 us
  Pallas kernels  96.1 us (58%)
  starting transfers between devices  36.4 us (22%)
  waiting for transfers between devices  24.9 us (15%)
  local copies, waits for them, and re-layouts  6.08 us (4%)
    pallas_call x1, Pallas kernels, pack_edges(): pl.pallas_call(edges_body, grid_spec=pltpu.PrefetchScalarGridSpec(num_sca...  29.2 us
    pallas_call x1, Pallas kernels, inner(): pl.pallas_call(inner_body, grid_spec=pltpu.PrefetchScalarGridSpec(num_sca...  28.4 us
    ppermute x1, starting transfers between devices, shards(): near_halo_c = lax.ppermute(near_c, 'lon', to_near)  20.3 us
    ppermute x1, waiting for transfers between devices, shards(): below = lax.ppermute(top, 'lat', [(i, i - 1) for i in range(1, bands)])  19.7 us
    pallas_call x1, Pallas kernels, outer(): pl.pallas_call(outer_body, grid_spec=pltpu.PrefetchScalarGridSpec(num_sca...  16.6 us
    pallas_call x1, Pallas kernels, corners(): pl.pallas_call(corner_body, grid_spec=pltpu.PrefetchScalarGridSpec(num_sc...  12.1 us
    ppermute x1, starting transfers between devices, shards(): below = lax.ppermute(top, 'lat', [(i, i - 1) for i in range(1, bands)])  6.72 us
    pallas_call x1, Pallas kernels, window_bias(): pl.pallas_call(bias_body, out_shape=jax.ShapeDtypeStruct((1, 2, WIN, 576)...  5.26 us
  transfers between devices with their start and end apart: 6, of which 2 were waited for; matrix products, arithmetic and copies ran while one was open for 2% of the time, Pallas kernels for 33%

profile of v2, /device:TPU:8, one launch (start us, length us, event | category | flops | bytes accessed | tf_op | source)
XLA Modules:
  0.0 165.7 jit_solution(17894085540598278408)
XLA Ops:
  0.6 0.7 fusion
  1.4 0.1 copy.29
  1.5 1.0 broadcast_in_dim.12.mask
  2.5 29.2 %pack_edges.1 = (bf16[4,7,72,512]{3,2,1,0:T(8,128)(2,1)}, bf16[4,7,72,512]{3,2,1,0:T(8,128)(2,1)}, bf16[4,2,3,3,8,512]{5,4,3,2,1,0:T(8,128)(2,1)}, bf16[4,2,3,3,8,512]{5,4,3,2,1,0:T(8,128)(2,1)}) custom-call(s32[1]{0:T(128)} %bitcast.core, bf16[2,48,3,8,512]{4,3,2,1,0:T(8,128)(2,1)} %bitcast.40, bf16[2,48,3,8,512]{4,3,2,1,0:T(8,128)(2,1)} %bitcast.43, ...), custom_call_target="tpu_custom_call" | custom-call | flops 396361728 | bytes 16777216 | tf_op jit(solution)/shard_map/pack_edges/pallas_call | solution.py:143
  31.7 0.1 collective-permute-start.5
  31.8 4.6 %collective-permute-start.4 = (bf16[4,7,72,512]{3,2,1,0:T(8,128)(2,1)}, bf16[4,7,72,512]{3,2,1,0:T(8,128)(2,1)S(1)}, u32[]{:S(2)}, u32[]{:S(2)}) collective-permute-start(bf16[4,7,72,512]{3,2,1,0:T(8,128)(2,1)} %get-tuple-element.29.own), channel_id=1, source_target_pairs={{1,2},{3,4},{5,6},{7,8},{9,10},{11,12},{13,14},{15,0},{2,1},{4,3},... | collective-permute-start | bytes 6193160 | tf_op jit(solution)/shard_map/ppermute | solution.py:642
  36.4 6.7 %collective-permute-start = (bf16[4,2,72,512]{3,2,1,0:T(8,128)(2,1)}, bf16[4,2,72,512]{3,2,1,0:T(8,128)(2,1)S(1)}, u32[]{:S(2)}, u32[]{:S(2)}) collective-permute-start(bf16[4,2,72,512]{3,2,1,0:T(8,128)(2,1)} %bitcast.52), channel_id=1, source_target_pairs={{16,0},{32,16},{48,32},{64,48},{80,64},{96,80},{112,96},{17,1},{33... | collective-permute-start | bytes 1769480 | tf_op jit(solution)/shard_map/ppermute | solution.py:644
  43.2 1.9 %collective-permute-start.1 = (bf16[4,2,72,512]{3,2,1,0:T(8,128)(2,1)}, bf16[4,2,72,512]{3,2,1,0:T(8,128)(2,1)S(1)}, u32[]{:S(2)}, u32[]{:S(2)}) collective-permute-start(bf16[4,2,72,512]{3,2,1,0:T(8,128)(2,1)} %bitcast.54), channel_id=1, source_target_pairs={{0,16},{16,32},{32,48},{48,64},{64,80},{80,96},{96,112},{1,17},{17... | collective-permute-start | bytes 1769480 | tf_op jit(solution)/shard_map/ppermute | solution.py:645
  45.1 0.1 copy.30
  45.2 0.1 broadcast_in_dim.13
  45.2 0.6 pad.4.table
  45.9 0.7 add_convert_fusion.flags
  46.5 5.3 %window_bias.1.bias = f32[1,2,144,576]{3,2,1,0:T(8,128)} custom-call(f32[8,768]{1,0:T(8,128)} %pad.4.table, bf16[1536,576]{1,0:T(8,128)(2,1)} %constant.52.clone.hot, bf16[144,192]{1,0:T(8,128)(2,1)} %constant.53.clone.squeeze), custom_call_target="tpu_custom_call" | custom-call | flops 1358954496 | bytes 3145728 | tf_op jit(solution)/shard_map/window_bias/pallas_call | solution.py:579
  51.8 19.7 %collective-permute-done.below = bf16[4,2,72,512]{3,2,1,0:T(8,128)(2,1)S(1)} collective-permute-done((bf16[4,2,72,512]{3,2,1,0:T(8,128)(2,1)}, bf16[4,2,72,512]{3,2,1,0:T(8,128)(2,1)S(1)}, u32[]{:S(2)}, u32[]{:S(2)}) %collective-permute-start) | collective-permute-done | bytes 589856 | tf_op jit(solution)/shard_map/ppermute | solution.py:644
  71.5 5.2 %collective-permute-done.1.above = bf16[4,2,72,512]{3,2,1,0:T(8,128)(2,1)S(1)} collective-permute-done((bf16[4,2,72,512]{3,2,1,0:T(8,128)(2,1)}, bf16[4,2,72,512]{3,2,1,0:T(8,128)(2,1)S(1)}, u32[]{:S(2)}, u32[]{:S(2)}) %collective-permute-start.1) | collective-permute-done | bytes 589856 | tf_op jit(solution)/shard_map/ppermute | solution.py:645
  76.6 0.0 copy-done.3
  76.6 0.8 copy-done.4
  77.4 4.4 %pack_corners.1 = (bf16[4,2,72,512]{3,2,1,0:T(8,128)(2,1)}, bf16[4,2,72,512]{3,2,1,0:T(8,128)(2,1)}, bf16[4,2,144,512]{3,2,1,0:T(8,128)(2,1)}) custom-call(s32[1]{0:T(128)} %bitcast.core, bf16[4,2,72,512]{3,2,1,0:T(8,128)(2,1)} %bitcast.53, bf16[4,2,72,512]{3,2,1,0:T(8,128)(2,1)} %bitcast.55, bf16[4,2,72,512]{3,2,1,0:T(8,128)(2,1)} %copy-done.3, ...), custom_call_target="tpu_custom_call" | custom-call | flops 679477248 | bytes 5242880 | tf_op jit(solution)/shard_map/pack_corners/pallas_call | solution.py:191
  81.9 20.3 %collective-permute-start.2 = (bf16[4,2,72,512]{3,2,1,0:T(8,128)(2,1)}, bf16[4,2,72,512]{3,2,1,0:T(8,128)(2,1)S(1)}, u32[]{:S(2)}, u32[]{:S(2)}) collective-permute-start(bf16[4,2,72,512]{3,2,1,0:T(8,128)(2,1)} %get-tuple-element.27.near), channel_id=1, source_target_pairs={{0,1},{1,0},{2,3},{3,2},{4,5},{5,4},{6,7},{7,6},{8,9},{9,8},{10,11... | collective-permute-start | bytes 1769480 | tf_op jit(solution)/shard_map/ppermute | solution.py:654
  102.2 2.8 %collective-permute-start.3 = (bf16[4,2,72,512]{3,2,1,0:T(8,128)(2,1)}, bf16[4,2,72,512]{3,2,1,0:T(8,128)(2,1)S(1)}, u32[]{:S(2)}, u32[]{:S(2)}) collective-permute-start(bf16[4,2,72,512]{3,2,1,0:T(8,128)(2,1)} %get-tuple-element.28.far), channel_id=1, source_target_pairs={{1,2},{3,4},{5,6},{7,8},{9,10},{11,12},{13,14},{15,0},{2,1},{4,3},... | collective-permute-start | bytes 1769480 | tf_op jit(solution)/shard_map/ppermute | solution.py:653
  105.0 0.0 collective-permute-done.5.halo
  105.0 1.1 broadcast_in_dim.14.m0.m1
  106.0 28.4 %inner_windows.1 = (bf16[2,16,72,512]{3,2,1,0:T(8,128)(2,1)}, bf16[2,16,72,512]{3,2,1,0:T(8,128)(2,1)}, bf16[2,16,72,512]{3,2,1,0:T(8,128)(2,1)}, bf16[2,16,72,512]{3,2,1,0:T(8,128)(2,1)}, f32[8,128]{1,0:T(8,128)}) custom-call(s32[1]{0:T(128)} %bitcast.core, bf16[2,16,72,512]{3,2,1,0:T(8,128)(2,1)} %bitcast.41, bf16[2,16,72,512]{3,2,1,0:T(8,128)(2,1)} %bitcast.42, ...), custom_call_target="tpu_custom_call" | custom-call | flops 7134511104 | bytes 25165824 | tf_op jit(solution)/shard_map/inner_windows/pallas_call | solution.py:351
  134.4 0.0 collective-permute-done.4.halo
  134.4 1.3 copy-done
  135.7 16.6 %outer_windows.1 = (bf16[2,48,3,8,512]{4,3,2,1,0:T(8,128)(2,1)}, bf16[2,48,3,8,512]{4,3,2,1,0:T(8,128)(2,1)}, bf16[2,48,3,8,512]{4,3,2,1,0:T(8,128)(2,1)}, bf16[2,48,3,8,512]{4,3,2,1,0:T(8,128)(2,1)}) custom-call(s32[1]{0:T(128)} %bitcast.core, ...), custom_call_target="tpu_custom_call", output_to_operand_aliasing={{0}: (5, {}), {1}: (6, {}), {2}: (7, {}), {3}: (8, {})} | custom-call | flops 3567255552 | bytes 12582912 | tf_op jit(solution)/shard_map/outer_windows/pallas_call | solution.py:443
  152.4 0.0 collective-permute-done.2.near_halo
  152.4 0.0 copy-start.1
  152.4 0.0 collective-permute-done.3.far_halo
  152.4 0.8 copy-done.1
  153.2 0.2 copy-done.2
  153.4 12.1 %corner_windows.1 = (bf16[2,16,72,512]{3,2,1,0:T(8,128)(2,1)}, bf16[2,16,72,512]{3,2,1,0:T(8,128)(2,1)}, bf16[2,16,72,512]{3,2,1,0:T(8,128)(2,1)}, bf16[2,16,72,512]{3,2,1,0:T(8,128)(2,1)}) custom-call(s32[1]{0:T(128)} %bitcast.core, s32[2]{0:T(128)} %add_convert_fusion.flags, ...), custom_call_target="tpu_custom_call", output_to_operand_aliasing={{0}: (9, {}), {1}: (10, {}), {2}: (11, {}), {3}: (12, {})} | custom-call | flops 3057647616 | bytes 8388608 | tf_op jit(solution)/shard_map/corner_windows/pallas_call | solution.py:509
  (6 shorter events, 0.0 us)
Async XLA Ops:
  2.5 42.7 %copy-start.5 = (f32[8,759]{1,0:T(8,128)S(1)}, f32[8,759]{1,0:T(8,128)}, u32[]{:S(2)}) copy-start(f32[8,759]{1,0:T(8,128)} %param.22) | copy-start | bytes 72868
  31.7 73.2 %collective-permute-start.5 = (bf16[4,7,72,512]{3,2,1,0:T(8,128)(2,1)}, bf16[4,7,72,512]{3,2,1,0:T(8,128)(2,1)}, u32[]{:S(2)}, u32[]{:S(2)}) collective-permute-start(bf16[4,7,72,512]{3,2,1,0:T(8,128)(2,1)} %get-tuple-element.31.own), channel_id=1, source_target_pairs={{0,1},{1,0},{2,3},{3,2},{4,5},{5,4},{6,7},{7,6},{8,9},{9,8},{10,11... | collective-permute-start | bytes 6193160 | tf_op jit(solution)/shard_map/ppermute | solution.py:643
  31.8 102.6 %collective-permute-start.4 = (bf16[4,7,72,512]{3,2,1,0:T(8,128)(2,1)}, bf16[4,7,72,512]{3,2,1,0:T(8,128)(2,1)S(1)}, u32[]{:S(2)}, u32[]{:S(2)}) collective-permute-start(bf16[4,7,72,512]{3,2,1,0:T(8,128)(2,1)} %get-tuple-element.29.own), channel_id=1, source_target_pairs={{1,2},{3,4},{5,6},{7,8},{9,10},{11,12},{13,14},{15,0},{2,1},{4,3},... | collective-permute-start | bytes 6193160 | tf_op jit(solution)/shard_map/ppermute | solution.py:642
  36.4 35.0 %collective-permute-start = (bf16[4,2,72,512]{3,2,1,0:T(8,128)(2,1)}, bf16[4,2,72,512]{3,2,1,0:T(8,128)(2,1)S(1)}, u32[]{:S(2)}, u32[]{:S(2)}) collective-permute-start(bf16[4,2,72,512]{3,2,1,0:T(8,128)(2,1)} %bitcast.52), channel_id=1, source_target_pairs={{16,0},{32,16},{48,32},{64,48},{80,64},{96,80},{112,96},{17,1},{33... | collective-permute-start | bytes 1769480 | tf_op jit(solution)/shard_map/ppermute | solution.py:644
  43.2 33.5 %collective-permute-start.1 = (bf16[4,2,72,512]{3,2,1,0:T(8,128)(2,1)}, bf16[4,2,72,512]{3,2,1,0:T(8,128)(2,1)S(1)}, u32[]{:S(2)}, u32[]{:S(2)}) collective-permute-start(bf16[4,2,72,512]{3,2,1,0:T(8,128)(2,1)} %bitcast.54), channel_id=1, source_target_pairs={{0,16},{16,32},{32,48},{48,64},{64,80},{80,96},{96,112},{1,17},{17... | collective-permute-start | bytes 1769480 | tf_op jit(solution)/shard_map/ppermute | solution.py:645
  71.4 5.2 %copy-start.3 = (bf16[4,2,72,512]{3,2,1,0:T(8,128)(2,1)}, bf16[4,2,72,512]{3,2,1,0:T(8,128)(2,1)S(1)}, u32[]{:S(2)}) copy-start(bf16[4,2,72,512]{3,2,1,0:T(8,128)(2,1)S(1)} %collective-permute-done.below) | copy-start | bytes 1769476
  76.6 0.8 copy-start.4
  81.9 70.5 %collective-permute-start.2 = (bf16[4,2,72,512]{3,2,1,0:T(8,128)(2,1)}, bf16[4,2,72,512]{3,2,1,0:T(8,128)(2,1)S(1)}, u32[]{:S(2)}, u32[]{:S(2)}) collective-permute-start(bf16[4,2,72,512]{3,2,1,0:T(8,128)(2,1)} %get-tuple-element.27.near), channel_id=1, source_target_pairs={{0,1},{1,0},{2,3},{3,2},{4,5},{5,4},{6,7},{7,6},{8,9},{9,8},{10,11... | collective-permute-start | bytes 1769480 | tf_op jit(solution)/shard_map/ppermute | solution.py:654
  102.2 50.2 %collective-permute-start.3 = (bf16[4,2,72,512]{3,2,1,0:T(8,128)(2,1)}, bf16[4,2,72,512]{3,2,1,0:T(8,128)(2,1)S(1)}, u32[]{:S(2)}, u32[]{:S(2)}) collective-permute-start(bf16[4,2,72,512]{3,2,1,0:T(8,128)(2,1)} %get-tuple-element.28.far), channel_id=1, source_target_pairs={{1,2},{3,4},{5,6},{7,8},{9,10},{11,12},{13,14},{15,0},{2,1},{4,3},... | collective-permute-start | bytes 1769480 | tf_op jit(solution)/shard_map/ppermute | solution.py:653
  134.4 1.3 copy-start
  152.4 0.8 copy-start.1
  152.4 1.0 copy-start.2

commit v3 on v2

--- a/solution.py
+++ b/solution.py
@@ -77,27 +77,24 @@
 
     ends = ((top, 0), (bottom, 45))
 
-    def end_rows(end, index):
-        out, row = ends[end]
-        if index == 1:
-            return pltpu.make_async_copy(rows.at[end], out.at[1], rows_gone.at[end, 1])
+    def rows_in(end, index):
+        row = ends[end][1]
         return pltpu.make_async_copy(
-            sources[index].at[:, row : row + 3], out.at[index], rows_gone.at[end, index]
+            sources[index].at[:, row : row + 3], rows.at[end, index], rows_came.at[end, index]
         )
 
-    def key_rows(end):
-        row = ends[end][1]
-        return pltpu.make_async_copy(k.at[:, row : row + 3], rows.at[end], rows_came.at[end])
+    def rows_out(end, index):
+        return pltpu.make_async_copy(
+            rows.at[end, index], ends[end][0].at[index], rows_gone.at[end, index]
+        )
 
     for index in range(4):
         fetch(0, index).start()
     for end in range(2):
-        key_rows(end).start()
+        for index in range(4):
+            rows_in(end, index).start()
     for index in range(4):
         fetch(1, index).start()
-    for end in range(2):
-        for index in (0, 2, 3):
-            end_rows(end, index).start()
     for side in range(2):
         perm = (far_perm, near_perm)[side]
         for index in range(4):
@@ -123,16 +120,20 @@
             send_off(side, index).start()
         if side == 0:
             for end in range(2):
-                key_rows(end).wait()
                 row = ends[end][1]
-                keyed = keyed_rows(rows[end].astype(F32), mask[row : row + 3], embed[...])
-                rows[end] = keyed.astype(BF16)
-                end_rows(end, 1).start()
+                for index in range(4):
+                    rows_in(end, index).wait()
+                    if index == 1:
+                        keyed = keyed_rows(
+                            rows[end, 1].astype(F32), mask[row : row + 3], embed[...]
+                        )
+                        rows[end, 1] = keyed.astype(BF16)
+                    rows_out(end, index).start()
     for index in range(4):
         for side in range(2):
             send_off(side, index).wait()
         for end in range(2):
-            end_rows(end, index).wait()
+            rows_out(end, index).wait()
 
 
 def pack_edges(arrays, mask, embed, far_perm, near_perm, core):
@@ -156,10 +157,10 @@
             scratch_shapes=[
                 pltpu.VMEM((2, 4, 2, 48, 8, 512), BF16),
                 pltpu.VMEM((2, 4, 7, STRIP, 512), BF16),
-                pltpu.VMEM((2, 2, 3, 3, 8, 512), BF16),
+                pltpu.VMEM((2, 4, 2, 3, 3, 8, 512), BF16),
                 pltpu.SemaphoreType.DMA((2, 4)),
                 pltpu.SemaphoreType.DMA((2, 4)),
-                pltpu.SemaphoreType.DMA((2,)),
+                pltpu.SemaphoreType.DMA((2, 4)),
                 pltpu.SemaphoreType.DMA((2, 4)),
             ],
         ),
@@ -169,10 +170,10 @@
             flops=2 * 56 * STRIP * 96 * 512, bytes_accessed=16 * MIB, transcendentals=0
         ),
         name="pack_edges",
-    )(core, *tiles, mask.reshape(48, 3, 8, 128), embed, far_perm, near_perm)
-
-
-def corners_body(core, top, bottom, below, above, perm, far, near, mid):
+    )(core, *tiles, mask, embed, far_perm, near_perm)
+
+
+def corners_body(core, top, bottom, below, above, perm, done, far, near, mid):
     for index in range(4):
         for place, (first, second) in enumerate(((top, above), (below, bottom))):
             first = first[index].astype(F32)
@@ -186,14 +187,15 @@
             mid[index, place] = strips[2 * STRIP :].astype(BF16)
 
 
-def pack_corners(top, bottom, below, above, perm, core):
+def pack_corners(top, bottom, below, above, perm, core, done):
     sizes = (STRIP, STRIP, WIN)
     return pl.pallas_call(
         corners_body,
         grid_spec=pltpu.PrefetchScalarGridSpec(
             num_scalar_prefetch=1,
             grid=(1,),
-            in_specs=[fixed_spec((4, 2, STRIP, 512))] * 4 + [side_spec((2 * WIN, 2 * WIN))],
+            in_specs=[fixed_spec((4, 2, STRIP, 512))] * 4
+            + [side_spec((2 * WIN, 2 * WIN)), pl.BlockSpec(memory_space=pl.ANY)],
             out_specs=[fixed_spec((4, 2, size, 512)) for size in sizes],
         ),
         out_shape=[jax.ShapeDtypeStruct((4, 2, size, 512), BF16) for size in sizes],
@@ -202,7 +204,7 @@
             flops=2 * 8 * 288 * 288 * 512, bytes_accessed=5 * MIB, transcendentals=0
         ),
         name="pack_corners",
-    )(core, top, bottom, below, above, perm)
+    )(core, top, bottom, below, above, perm, done)
 
 
 def windows(win, slots, bias, scores, grads, low, dlow, store):
@@ -270,8 +272,8 @@
     for index, pair in enumerate(((q0, q1), (k0, k1), (v0, v1), (g0, g1))):
         first, second = (source[:, 0].astype(F32) for source in pair)
         if index == 1:
-            first = keyed_rows(first, m0[0], embed[...])
-            second = keyed_rows(second, m1[0], embed[...])
+            first = keyed_rows(first, m0[...].reshape(STRIP, 128), embed[...])
+            second = keyed_rows(second, m1[...].reshape(STRIP, 128), embed[...])
         tokens = jnp.concatenate([first[0], first[1], second[0], second[1]], axis=0)
         packed = dot(perm[...], tokens.astype(BF16))
         if index == 0:
@@ -355,8 +357,8 @@
             grid=(7,),
             in_specs=specs
             + [
-                pl.BlockSpec((1, STRIP, 128), lambda s, core: (2 * s + 2, 0, 0)),
-                pl.BlockSpec((1, STRIP, 128), lambda s, core: (2 * s + 1, 0, 0)),
+                pl.BlockSpec((3, 3, 8, 128), lambda s, core: (2 * s + 2, 0, 0, 0)),
+                pl.BlockSpec((3, 3, 8, 128), lambda s, core: (2 * s + 1, 0, 0, 0)),
                 fixed_spec((1, 512)),
                 fixed_spec((WIN, 2 * WIN)),
                 band_spec(),
@@ -614,10 +616,6 @@
     return [jnp.asarray(np.stack(table), BF16) for table in stacked]
 
 
-def after(value, earlier):
-    return lax.optimization_barrier((value, earlier))[0]
-
-
 def shards(queries, key_tokens, value_tokens, out_grad, land_mask, land_embed, rel_table):
     lev, rows, cols, width = queries.shape
     lat = lax.axis_index("lat")
@@ -626,7 +624,7 @@
     sectors = lax.axis_size("lon")
     arrays = (queries, key_tokens, value_tokens, out_grad)
     mask = jnp.broadcast_to(
-        land_mask.astype(F32).reshape(rows // 3, STRIP, 1), (rows // 3, STRIP, 128)
+        land_mask.astype(F32).reshape(rows, 3, 8, 1), (rows, 3, 8, 128)
     )
     embed = land_embed.reshape(1, width)
     far_perm, near_perm, all_perm, near_back, far_back, corner_back = side_tables()
@@ -644,12 +642,12 @@
     below = lax.ppermute(top, "lat", [(i, i - 1) for i in range(1, bands)])
     above = lax.ppermute(bottom, "lat", [(i, i + 1) for i in range(bands - 1)])
 
-    bias = window_bias(after(rel_table, far))
+    bias = window_bias(rel_table)
     *partial, done = inner(
         arrays, mask, embed, mid_perm, near, near_halo, bias, near_back, core
     )
 
-    far_c, near_c, mid_c = pack_corners(top, bottom, below, above, all_perm, after(core, done))
+    far_c, near_c, mid_c = pack_corners(top, bottom, below, above, all_perm, core, done)
     far_halo_c = lax.ppermute(far_c, "lon", to_far)
     near_halo_c = lax.ppermute(near_c, "lon", to_near)
 

time: 166 us -> 115 us (0.69)
  waiting for transfers between devices: 24.9 us -> 0.02 us
  Pallas kernels: 96.1 us -> 74.1 us
  starting transfers between devices: 36.4 us -> 33.5 us
    pallas_call x1, Pallas kernels: 29.2 us -> 7.34 us  [pack_edges(): pl.pallas_call(edges_body, grid_spec=pltpu.PrefetchScalarGridSpec(num_sca...]
    ppermute x1, waiting for transfers between devices: 19.7 us -> 0.01 us  [shards(): below = lax.ppermute(top, 'lat', [(i, i - 1) for i in range(1, bands)])]
    ppermute x1, waiting for transfers between devices: 5.17 us -> 0.01 us  [shards(): above = lax.ppermute(bottom, 'lat', [(i, i + 1) for i in range(bands - 1)])]
    ppermute x1, starting transfers between devices: 20.3 us -> 17.4 us  [shards(): near_halo_c = lax.ppermute(near_c, 'lon', to_near)]
  transfers between devices with their start and end apart: 6 -> 6, of which waited for: 2 -> 0; matrix products, arithmetic and copies ran while one was open for 2% -> 1% of each run, Pallas kernels for 33% -> 48%
where the time goes in v3:
time: 115 us
  Pallas kernels  74.1 us (64%)
  starting transfers between devices  33.5 us (29%)
  local copies, waits for them, and re-layouts  5.05 us (4%)
  other arithmetic  1.31 us (1%)
    pallas_call x1, Pallas kernels, inner(): pl.pallas_call(inner_body, grid_spec=pltpu.PrefetchScalarGridSpec(num_sca...  28.4 us
    ppermute x1, starting transfers between devices, shards(): near_halo_c = lax.ppermute(near_c, 'lon', to_near)  17.4 us
    pallas_call x1, Pallas kernels, outer(): pl.pallas_call(outer_body, grid_spec=pltpu.PrefetchScalarGridSpec(num_sca...  16.6 us
    pallas_call x1, Pallas kernels, corners(): pl.pallas_call(corner_body, grid_spec=pltpu.PrefetchScalarGridSpec(num_sc...  12.1 us
    pallas_call x1, Pallas kernels, pack_edges(): pl.pallas_call(edges_body, grid_spec=pltpu.PrefetchScalarGridSpec(num_sca...  7.34 us
    ppermute x1, starting transfers between devices, shards(): below = lax.ppermute(top, 'lat', [(i, i - 1) for i in range(1, bands)])  6.72 us
    pallas_call x1, Pallas kernels, window_bias(): pl.pallas_call(bias_body, out_shape=jax.ShapeDtypeStruct((1, 2, WIN, 576)...  5.23 us
    ppermute x1, starting transfers between devices, shards(): far_halo = lax.ppermute(far, 'lon', to_far)  4.59 us
  transfers between devices with their start and end apart: 6, of which 0 were waited for; matrix products, arithmetic and copies ran while one was open for 1% of the time, Pallas kernels for 48%

profile of v3, /device:TPU:8, one launch (start us, length us, event | category | flops | bytes accessed | tf_op | source)
XLA Modules:
  0.0 114.9 jit_solution(12812045207382066671)
XLA Ops:
  0.6 0.7 convert_bitcast_fusion
  1.3 0.1 copy.28
  1.5 1.0 broadcast_in_dim.8.mask.m0.m1
  2.5 7.3 %pack_edges.1 = (bf16[4,7,72,512]{3,2,1,0:T(8,128)(2,1)}, bf16[4,7,72,512]{3,2,1,0:T(8,128)(2,1)}, bf16[4,2,3,3,8,512]{5,4,3,2,1,0:T(8,128)(2,1)}, bf16[4,2,3,3,8,512]{5,4,3,2,1,0:T(8,128)(2,1)}) custom-call(s32[1]{0:T(128)} %bitcast.core, bf16[2,48,3,8,512]{4,3,2,1,0:T(8,128)(2,1)} %bitcast.40, bf16[2,48,3,8,512]{4,3,2,1,0:T(8,128)(2,1)} %bitcast.43, ...), custom_call_target="tpu_custom_call" | custom-call | flops 396361728 | bytes 16777216 | tf_op jit(solution)/shard_map/pack_edges/pallas_call | solution.py:144
  9.9 0.1 collective-permute-start.2
  9.9 4.6 %collective-permute-start.5 = (bf16[4,7,72,512]{3,2,1,0:T(8,128)(2,1)}, bf16[4,7,72,512]{3,2,1,0:T(8,128)(2,1)S(1)}, u32[]{:S(2)}, u32[]{:S(2)}) collective-permute-start(bf16[4,7,72,512]{3,2,1,0:T(8,128)(2,1)} %get-tuple-element.31.own), channel_id=1, source_target_pairs={{1,2},{3,4},{5,6},{7,8},{9,10},{11,12},{13,14},{15,0},{2,1},{4,3},... | collective-permute-start | bytes 6193160 | tf_op jit(solution)/shard_map/ppermute | solution.py:640
  14.5 6.7 %collective-permute-start = (bf16[4,2,72,512]{3,2,1,0:T(8,128)(2,1)}, bf16[4,2,72,512]{3,2,1,0:T(8,128)(2,1)S(1)}, u32[]{:S(2)}, u32[]{:S(2)}) collective-permute-start(bf16[4,2,72,512]{3,2,1,0:T(8,128)(2,1)} %bitcast.52), channel_id=1, source_target_pairs={{16,0},{32,16},{48,32},{64,48},{80,64},{96,80},{112,96},{17,1},{33... | collective-permute-start | bytes 1769480 | tf_op jit(solution)/shard_map/ppermute | solution.py:642
  21.3 1.9 %collective-permute-start.1 = (bf16[4,2,72,512]{3,2,1,0:T(8,128)(2,1)}, bf16[4,2,72,512]{3,2,1,0:T(8,128)(2,1)S(1)}, u32[]{:S(2)}, u32[]{:S(2)}) collective-permute-start(bf16[4,2,72,512]{3,2,1,0:T(8,128)(2,1)} %bitcast.54), channel_id=1, source_target_pairs={{0,16},{16,32},{32,48},{48,64},{64,80},{80,96},{96,112},{1,17},{17... | collective-permute-start | bytes 1769480 | tf_op jit(solution)/shard_map/ppermute | solution.py:643
  23.2 0.0 copy-done.5
  23.2 0.6 pad.4.table
  23.8 5.2 %window_bias.1.bias = f32[1,2,144,576]{3,2,1,0:T(8,128)} custom-call(f32[8,768]{1,0:T(8,128)} %pad.4.table, bf16[1536,576]{1,0:T(8,128)(2,1)} %constant.52.clone.hot, bf16[144,192]{1,0:T(8,128)(2,1)} %constant.53.clone.squeeze), custom_call_target="tpu_custom_call" | custom-call | flops 1358954496 | bytes 3145728 | tf_op jit(solution)/shard_map/window_bias/pallas_call | solution.py:581
  29.1 0.0 collective-permute-done.2.halo
  29.1 28.4 %inner_windows.1 = (bf16[2,16,72,512]{3,2,1,0:T(8,128)(2,1)}, bf16[2,16,72,512]{3,2,1,0:T(8,128)(2,1)}, bf16[2,16,72,512]{3,2,1,0:T(8,128)(2,1)}, bf16[2,16,72,512]{3,2,1,0:T(8,128)(2,1)}, f32[8,128]{1,0:T(8,128)}) custom-call(s32[1]{0:T(128)} %bitcast.core, bf16[2,16,72,512]{3,2,1,0:T(8,128)(2,1)} %bitcast.41, bf16[2,16,72,512]{3,2,1,0:T(8,128)(2,1)} %bitcast.42, ...), custom_call_target="tpu_custom_call" | custom-call | flops 7134511104 | bytes 25165824 | tf_op jit(solution)/shard_map/inner_windows/pallas_call | solution.py:353
  57.4 0.0 collective-permute-done.below
  57.5 0.0 copy-start.3
  57.5 0.0 collective-permute-done.1.above
  57.5 0.0 copy-start.4
  57.5 0.8 copy-done.3
  58.3 0.2 copy-done.4
  58.5 4.4 %pack_corners.1 = (bf16[4,2,72,512]{3,2,1,0:T(8,128)(2,1)}, bf16[4,2,72,512]{3,2,1,0:T(8,128)(2,1)}, bf16[4,2,144,512]{3,2,1,0:T(8,128)(2,1)}) custom-call(s32[1]{0:T(128)} %bitcast.core, bf16[4,2,72,512]{3,2,1,0:T(8,128)(2,1)} %bitcast.53, bf16[4,2,72,512]{3,2,1,0:T(8,128)(2,1)} %bitcast.55, bf16[4,2,72,512]{3,2,1,0:T(8,128)(2,1)} %copy-done.3, ...), custom_call_target="tpu_custom_call" | custom-call | flops 679477248 | bytes 5242880 | tf_op jit(solution)/shard_map/pack_corners/pallas_call | solution.py:192
  62.8 17.4 %collective-permute-start.3 = (bf16[4,2,72,512]{3,2,1,0:T(8,128)(2,1)}, bf16[4,2,72,512]{3,2,1,0:T(8,128)(2,1)S(1)}, u32[]{:S(2)}, u32[]{:S(2)}) collective-permute-start(bf16[4,2,72,512]{3,2,1,0:T(8,128)(2,1)} %get-tuple-element.29.near), channel_id=1, source_target_pairs={{0,1},{1,0},{2,3},{3,2},{4,5},{5,4},{6,7},{7,6},{8,9},{9,8},{10,11... | collective-permute-start | bytes 1769480 | tf_op jit(solution)/shard_map/ppermute | solution.py:652
  80.2 2.8 %collective-permute-start.4 = (bf16[4,2,72,512]{3,2,1,0:T(8,128)(2,1)}, bf16[4,2,72,512]{3,2,1,0:T(8,128)(2,1)S(1)}, u32[]{:S(2)}, u32[]{:S(2)}) collective-permute-start(bf16[4,2,72,512]{3,2,1,0:T(8,128)(2,1)} %get-tuple-element.30.far), channel_id=1, source_target_pairs={{1,2},{3,4},{5,6},{7,8},{9,10},{11,12},{13,14},{15,0},{2,1},{4,3},... | collective-permute-start | bytes 1769480 | tf_op jit(solution)/shard_map/ppermute | solution.py:651
  83.0 0.6 add_convert_fusion.flags
  83.6 0.0 collective-permute-done.5.halo
  83.6 1.3 %copy-done = bf16[4,7,72,512]{3,2,1,0:T(8,128)(2,1)} copy-done((bf16[4,7,72,512]{3,2,1,0:T(8,128)(2,1)}, bf16[4,7,72,512]{3,2,1,0:T(8,128)(2,1)S(1)}, u32[]{:S(2)}) %copy-start) | copy-done | bytes 2064408
  85.0 16.6 %outer_windows.1 = (bf16[2,48,3,8,512]{4,3,2,1,0:T(8,128)(2,1)}, bf16[2,48,3,8,512]{4,3,2,1,0:T(8,128)(2,1)}, bf16[2,48,3,8,512]{4,3,2,1,0:T(8,128)(2,1)}, bf16[2,48,3,8,512]{4,3,2,1,0:T(8,128)(2,1)}) custom-call(s32[1]{0:T(128)} %bitcast.core, ...), custom_call_target="tpu_custom_call", output_to_operand_aliasing={{0}: (5, {}), {1}: (6, {}), {2}: (7, {}), {3}: (8, {})} | custom-call | flops 3567255552 | bytes 12582912 | tf_op jit(solution)/shard_map/outer_windows/pallas_call | solution.py:445
  101.6 0.0 collective-permute-done.3.near_halo
  101.6 0.0 copy-start.1
  101.6 0.0 collective-permute-done.4.far_halo
  101.6 0.8 copy-done.1
  102.4 0.2 copy-done.2
  102.6 12.1 %corner_windows.1 = (bf16[2,16,72,512]{3,2,1,0:T(8,128)(2,1)}, bf16[2,16,72,512]{3,2,1,0:T(8,128)(2,1)}, bf16[2,16,72,512]{3,2,1,0:T(8,128)(2,1)}, bf16[2,16,72,512]{3,2,1,0:T(8,128)(2,1)}) custom-call(s32[1]{0:T(128)} %bitcast.core, s32[2]{0:T(128)} %add_convert_fusion.flags, ...), custom_call_target="tpu_custom_call", output_to_operand_aliasing={{0}: (9, {}), {1}: (10, {}), {2}: (11, {}), {3}: (12, {})} | custom-call | flops 3057647616 | bytes 8388608 | tf_op jit(solution)/shard_map/corner_windows/pallas_call | solution.py:511
  (3 shorter events, 0.0 us)
Async XLA Ops:
  2.5 20.7 %copy-start.5 = (f32[8,759]{1,0:T(8,128)S(1)}, f32[8,759]{1,0:T(8,128)}, u32[]{:S(2)}) copy-start(f32[8,759]{1,0:T(8,128)} %param.22) | copy-start | bytes 72868
  9.9 19.2 %collective-permute-start.2 = (bf16[4,7,72,512]{3,2,1,0:T(8,128)(2,1)}, bf16[4,7,72,512]{3,2,1,0:T(8,128)(2,1)}, u32[]{:S(2)}, u32[]{:S(2)}) collective-permute-start(bf16[4,7,72,512]{3,2,1,0:T(8,128)(2,1)} %get-tuple-element.26.own), channel_id=1, source_target_pairs={{0,1},{1,0},{2,3},{3,2},{4,5},{5,4},{6,7},{7,6},{8,9},{9,8},{10,11... | collective-permute-start | bytes 6193160 | tf_op jit(solution)/shard_map/ppermute | solution.py:641
  9.9 73.7 %collective-permute-start.5 = (bf16[4,7,72,512]{3,2,1,0:T(8,128)(2,1)}, bf16[4,7,72,512]{3,2,1,0:T(8,128)(2,1)S(1)}, u32[]{:S(2)}, u32[]{:S(2)}) collective-permute-start(bf16[4,7,72,512]{3,2,1,0:T(8,128)(2,1)} %get-tuple-element.31.own), channel_id=1, source_target_pairs={{1,2},{3,4},{5,6},{7,8},{9,10},{11,12},{13,14},{15,0},{2,1},{4,3},... | collective-permute-start | bytes 6193160 | tf_op jit(solution)/shard_map/ppermute | solution.py:640
  14.5 42.9 %collective-permute-start = (bf16[4,2,72,512]{3,2,1,0:T(8,128)(2,1)}, bf16[4,2,72,512]{3,2,1,0:T(8,128)(2,1)S(1)}, u32[]{:S(2)}, u32[]{:S(2)}) collective-permute-start(bf16[4,2,72,512]{3,2,1,0:T(8,128)(2,1)} %bitcast.52), channel_id=1, source_target_pairs={{16,0},{32,16},{48,32},{64,48},{80,64},{96,80},{112,96},{17,1},{33... | collective-permute-start | bytes 1769480 | tf_op jit(solution)/shard_map/ppermute | solution.py:642
  21.3 36.2 %collective-permute-start.1 = (bf16[4,2,72,512]{3,2,1,0:T(8,128)(2,1)}, bf16[4,2,72,512]{3,2,1,0:T(8,128)(2,1)S(1)}, u32[]{:S(2)}, u32[]{:S(2)}) collective-permute-start(bf16[4,2,72,512]{3,2,1,0:T(8,128)(2,1)} %bitcast.54), channel_id=1, source_target_pairs={{0,16},{16,32},{32,48},{48,64},{64,80},{80,96},{96,112},{1,17},{17... | collective-permute-start | bytes 1769480 | tf_op jit(solution)/shard_map/ppermute | solution.py:643
  57.5 0.8 copy-start.3
  57.5 1.0 copy-start.4
  62.8 38.7 %collective-permute-start.3 = (bf16[4,2,72,512]{3,2,1,0:T(8,128)(2,1)}, bf16[4,2,72,512]{3,2,1,0:T(8,128)(2,1)S(1)}, u32[]{:S(2)}, u32[]{:S(2)}) collective-permute-start(bf16[4,2,72,512]{3,2,1,0:T(8,128)(2,1)} %get-tuple-element.29.near), channel_id=1, source_target_pairs={{0,1},{1,0},{2,3},{3,2},{4,5},{5,4},{6,7},{7,6},{8,9},{9,8},{10,11... | collective-permute-start | bytes 1769480 | tf_op jit(solution)/shard_map/ppermute | solution.py:652
  80.2 21.4 %collective-permute-start.4 = (bf16[4,2,72,512]{3,2,1,0:T(8,128)(2,1)}, bf16[4,2,72,512]{3,2,1,0:T(8,128)(2,1)S(1)}, u32[]{:S(2)}, u32[]{:S(2)}) collective-permute-start(bf16[4,2,72,512]{3,2,1,0:T(8,128)(2,1)} %get-tuple-element.30.far), channel_id=1, source_target_pairs={{1,2},{3,4},{5,6},{7,8},{9,10},{11,12},{13,14},{15,0},{2,1},{4,3},... | collective-permute-start | bytes 1769480 | tf_op jit(solution)/shard_map/ppermute | solution.py:651
  83.6 1.3 %copy-start = (bf16[4,7,72,512]{3,2,1,0:T(8,128)(2,1)}, bf16[4,7,72,512]{3,2,1,0:T(8,128)(2,1)S(1)}, u32[]{:S(2)}) copy-start(bf16[4,7,72,512]{3,2,1,0:T(8,128)(2,1)S(1)} %collective-permute-done.5.halo) | copy-start | bytes 6193156
  101.6 0.8 copy-start.1
  101.6 1.0 copy-start.2

commit v4 on v3

--- a/solution.py
+++ b/solution.py
@@ -15,7 +15,7 @@
 WIN = 144
 GROUP = 256
 MIB = 1 << 20
-VMEM_BYTES = 60 * MIB
+VMEM_BYTES = 63 * MIB
 
 
 def strip_matrix(strips):
@@ -267,7 +267,7 @@
 
 
 def inner_body(core, q0, q1, k0, k1, v0, v1, g0, g1, m0, m1, embed, perm, own, halo, bias, back, *rest):
-    outs, token, (win, result, ready, gone), work = rest[:4], rest[4], rest[5:9], rest[9:]
+    outs, beside, token, (win, result, ready, gone), work = rest[:4], rest[4], rest[5], rest[6:10], rest[10:]
     s = pl.program_id(0)
     for index, pair in enumerate(((q0, q1), (k0, k1), (v0, v1), (g0, g1))):
         first, second = (source[:, 0].astype(F32) for source in pair)
@@ -309,7 +309,9 @@
             copy.wait()
 
     used = pl.ds(pl.multiple_of(64 * core[0], 16), 224)
+    near_far = pl.ds(pl.multiple_of(208 * core[0], 16), 80)
     for index in range(4):
+        beside[index, 0] = result[index, near_far]
         full = dot(back[0], result[index, used])
         ready[slot, index] = full.reshape(2, 2, STRIP, 512).astype(BF16)
     for copy in leave(slot, s):
@@ -366,7 +368,11 @@
                 fixed_spec((1, 2, WIN, 576)),
                 side_spec((2 * WIN, 224)),
             ],
-            out_specs=[anywhere] * 4 + [fixed_spec((8, 128))],
+            out_specs=[anywhere] * 4
+            + [
+                pl.BlockSpec((4, 1, 80, 512), lambda s, core: (0, s, 0, 0)),
+                fixed_spec((8, 128)),
+            ],
             scratch_shapes=[
                 pltpu.VMEM((2, 4, WIN, 512), BF16),
                 pltpu.VMEM((4, 2 * WIN, 512), BF16),
@@ -376,100 +382,85 @@
             + work_scratch(4),
         ),
         out_shape=[jax.ShapeDtypeStruct((2, 16, STRIP, 512), BF16)] * 4
-        + [jax.ShapeDtypeStruct((8, 128), F32)],
+        + [jax.ShapeDtypeStruct((4, 7, 80, 512), BF16), jax.ShapeDtypeStruct((8, 128), F32)],
         compiler_params=params(),
         cost_estimate=window_cost(14, 24 * MIB),
         name="inner_windows",
     )(core, *operands, mask, mask, embed, perm, own, halo, bias, back)
 
 
-def band_spec():
-    return pl.BlockSpec((4, 1, STRIP, 512), lambda s, core: (0, s, 0, 0))
-
-
-def outer_body(core, own, halo, bias, back, p0, p1, p2, p3, o0, o1, o2, o3, win, result, tiles, came, gone, *work):
+def band_spec(first=0):
+    return pl.BlockSpec((4, 1, STRIP, 512), lambda s, core: (0, s + first, 0, 0))
+
+
+def outer_body(first, count, core, own, halo, beside, bias, back, p0, p1, p2, p3, o0, o1, o2, o3, token, win, result, tiles, gone, *work):
     s = pl.program_id(0)
     tile = 2 * core[0]
     outs = (o0, o1, o2, o3)
-
-    def arrivals():
-        return [
-            pltpu.make_async_copy(out.at[:, 3:45, tile], tiles.at[index], came.at[index])
-            for index, out in enumerate(outs)
-        ]
-
-    @pl.when(s == 0)
-    def _():
-        for copy in arrivals():
-            copy.start()
-
     place_pair(win, 0, own, halo, core[0] == 1)
 
     def keep(slot, index, cols, value):
-        result[index, :, cols] = value.astype(BF16)
+        result[index, 0:WIN, cols] = value.astype(BF16)
 
     windows(win, 1, bias, *work, keep)
-
-    @pl.when(s == 0)
-    def _():
-        for copy in arrivals():
-            copy.wait()
-
-    used = pl.ds(pl.multiple_of(64 * (1 - core[0]), 16), 80)
 
     def leave(step, index):
         return pltpu.make_async_copy(
             tiles.at[index, :, pl.ds(6 * step, 6)],
-            outs[index].at[:, pl.ds(6 * step + 3, 6), tile],
+            outs[index].at[:, pl.ds(6 * (step + first) + 3, 6), tile],
             gone.at[step, index],
         )
 
+    used = pl.ds(pl.multiple_of(64 * (1 - core[0]), 16), 160)
+    beside_at = pl.ds(pl.multiple_of(WIN - 64 * core[0], 16), 80)
     for index in range(4):
+        result[index, beside_at] = beside[index, 0]
         full = dot(back[0], result[index, used]).reshape(2, 2, 3, 8, 512)
         for part in range(2):
             span = pl.ds(6 * s + 3 * (1 - part), 3)
-            total = tiles[index, :, span].astype(F32) + full[part]
-            tiles[index, :, span] = total.astype(BF16)
+            tiles[index, :, span] = full[part].astype(BF16)
         leave(s, index).start()
 
-    @pl.when(s == 6)
+    @pl.when(s == count - 1)
     def _():
+        token[...] = jnp.zeros_like(token)
         for index in range(4):
-            for step in range(7):
+            for step in range(count):
                 leave(step, index).wait()
 
 
-def outer(partial, own, halo, bias, back, core):
+def outer(partial, own, halo, beside, bias, back, core, first, count):
     anywhere = pl.BlockSpec(memory_space=pl.ANY)
     shape = (2, 48, 3, 8, 512)
     return pl.pallas_call(
-        outer_body,
+        functools.partial(outer_body, first, count),
         grid_spec=pltpu.PrefetchScalarGridSpec(
             num_scalar_prefetch=1,
-            grid=(7,),
+            grid=(count,),
             in_specs=[
-                band_spec(),
-                band_spec(),
+                band_spec(first),
+                band_spec(first),
+                pl.BlockSpec((4, 1, 80, 512), lambda s, core: (0, s + first, 0, 0)),
                 fixed_spec((1, 2, WIN, 576)),
-                side_spec((96, 80)),
+                side_spec((96, 160)),
             ]
             + [anywhere] * 4,
-            out_specs=[anywhere] * 4,
+            out_specs=[anywhere] * 4 + [fixed_spec((8, 128))],
             scratch_shapes=[
                 pltpu.VMEM((1, 4, WIN, 512), BF16),
-                pltpu.VMEM((4, WIN, 512), BF16),
-                pltpu.VMEM((4, 2, 42, 8, 512), BF16),
-                pltpu.SemaphoreType.DMA((4,)),
-                pltpu.SemaphoreType.DMA((7, 4)),
+                pltpu.VMEM((4, WIN + 80, 512), BF16),
+                pltpu.VMEM((4, 2, 6 * count, 8, 512), BF16),
+                pltpu.SemaphoreType.DMA((count, 4)),
             ]
             + work_scratch(2),
         ),
-        out_shape=[jax.ShapeDtypeStruct(shape, BF16)] * 4,
-        input_output_aliases={5 + index: index for index in range(4)},
+        out_shape=[jax.ShapeDtypeStruct(shape, BF16)] * 4
+        + [jax.ShapeDtypeStruct((8, 128), F32)],
+        input_output_aliases={6 + index: index for index in range(4)},
         compiler_params=params(),
-        cost_estimate=window_cost(7, 12 * MIB),
+        cost_estimate=window_cost(count, count * 2 * MIB),
         name="outer_windows",
-    )(core, own, halo, bias, back, *[x.reshape(shape) for x in partial])
+    )(core, own, halo, beside, bias, back, *[x.reshape(shape) for x in partial])
 
 
 def corner_body(core, flags, mid, near, near_halo, far, far_halo, bias, back, p0, p1, p2, p3, o0, o1, o2, o3, win, result, cut, *work):
@@ -604,12 +595,13 @@
         middle = strip_matrix([1, 2]).T
         pad = np.zeros((2 * WIN, 8), np.float32)
         pad_far = np.zeros((96, 8), np.float32)
+        inside = far_matrix(1 + side, 2 * side).T
         if side == 0:
             near_back.append(np.concatenate([middle, own, pad], axis=1))
-            far_back.append(np.concatenate([pad_far, far[0].T], axis=1))
+            far_back.append(np.concatenate([pad_far, far[0].T, inside, pad_far], axis=1))
         else:
             near_back.append(np.concatenate([pad, own, middle], axis=1))
-            far_back.append(np.concatenate([far[1].T, pad_far], axis=1))
+            far_back.append(np.concatenate([far[1].T, pad_far, pad_far, inside], axis=1))
     natural = strip_matrix([0, 1, 2, 3]).T.reshape(2, WIN, 2 * WIN)
     corner_back = np.pad(natural, ((0, 0), (0, 0), (8, 8)))
     stacked = (far, near, whole, near_back, far_back, corner_back)
@@ -643,15 +635,15 @@
     above = lax.ppermute(bottom, "lat", [(i, i + 1) for i in range(bands - 1)])
 
     bias = window_bias(rel_table)
-    *partial, done = inner(
+    *partial, beside, _ = inner(
         arrays, mask, embed, mid_perm, near, near_halo, bias, near_back, core
     )
+    *partial, done = outer(partial, far, far_halo, beside, bias, far_back, core, 0, 4)
 
     far_c, near_c, mid_c = pack_corners(top, bottom, below, above, all_perm, core, done)
     far_halo_c = lax.ppermute(far_c, "lon", to_far)
     near_halo_c = lax.ppermute(near_c, "lon", to_near)
-
-    partial = outer(partial, far, far_halo, bias, far_back, core)
+    *partial, _ = outer(partial, far, far_halo, beside, bias, far_back, core, 4, 3)
     flags = jnp.stack([lat == 0, lat == bands - 1]).astype(jnp.int32)
     final = corners(
         partial, flags, mid_c, near_c, near_halo_c, far_c, far_halo_c, bias, corner_back, core

time: 115 us -> 112 us (0.974)
  the two profiles are of different devices: /device:TPU:8 before, /device:TPU:13 now
where the time goes in v4:
time: 112 us
  Pallas kernels  77.6 us (69%)
  waiting for transfers between devices  16.2 us (14%)
  starting transfers between devices  13.1 us (12%)
  local copies, waits for them, and re-layouts  2.62 us (2%)
  other arithmetic  1.38 us (1%)
    pallas_call x1, Pallas kernels, inner(): pl.pallas_call(inner_body, grid_spec=pltpu.PrefetchScalarGridSpec(num_sca...  28.9 us
    pallas_call x2, Pallas kernels, outer(): pl.pallas_call(functools.partial(outer_body, first, count), grid_spec=plt...  19.6 us
    pallas_call x1, Pallas kernels, corners(): pl.pallas_call(corner_body, grid_spec=pltpu.PrefetchScalarGridSpec(num_sc...  12.1 us
    ppermute x1, waiting for transfers between devices, shards(): far_halo = lax.ppermute(far, 'lon', to_far)  10.2 us
    pallas_call x1, Pallas kernels, pack_edges(): pl.pallas_call(edges_body, grid_spec=pltpu.PrefetchScalarGridSpec(num_sca...  7.39 us
    ppermute x1, starting transfers between devices, shards(): below = lax.ppermute(top, 'lat', [(i, i - 1) for i in range(1, bands)])  6.44 us
    ppermute x1, waiting for transfers between devices, shards(): far_halo_c = lax.ppermute(far_c, 'lon', to_far)  6.01 us
    pallas_call x1, Pallas kernels, window_bias(): pl.pallas_call(bias_body, out_shape=jax.ShapeDtypeStruct((1, 2, WIN, 576)...  5.24 us
  transfers between devices with their start and end apart: 6, of which 2 were waited for; matrix products, arithmetic and copies ran while one was open for 1% of the time, Pallas kernels for 48%

profile of v4, /device:TPU:13, one launch (start us, length us, event | category | flops | bytes accessed | tf_op | source)
XLA Modules:
  0.0 111.9 jit_solution(11610572764988252)
XLA Ops:
  0.6 0.7 convert_bitcast_fusion
  1.3 0.1 copy.32
  1.5 1.0 broadcast_in_dim.8.mask.m0.m1
  2.5 0.0 copy-start.2
  2.5 7.4 %pack_edges.1 = (bf16[4,7,72,512]{3,2,1,0:T(8,128)(2,1)}, bf16[4,7,72,512]{3,2,1,0:T(8,128)(2,1)}, bf16[4,2,3,3,8,512]{5,4,3,2,1,0:T(8,128)(2,1)}, bf16[4,2,3,3,8,512]{5,4,3,2,1,0:T(8,128)(2,1)}) custom-call(s32[1]{0:T(128)} %bitcast.core, bf16[2,48,3,8,512]{4,3,2,1,0:T(8,128)(2,1)} %bitcast.40, bf16[2,48,3,8,512]{4,3,2,1,0:T(8,128)(2,1)} %bitcast.43, ...), custom_call_target="tpu_custom_call" | custom-call | flops 396361728 | bytes 16777216 | tf_op jit(solution)/shard_map/pack_edges/pallas_call | solution.py:144
  9.9 0.8 collective-permute-start.3
  10.7 2.0 %collective-permute-start.2 = (bf16[4,7,72,512]{3,2,1,0:T(8,128)(2,1)}, bf16[4,7,72,512]{3,2,1,0:T(8,128)(2,1)}, u32[]{:S(2)}, u32[]{:S(2)}) collective-permute-start(bf16[4,7,72,512]{3,2,1,0:T(8,128)(2,1)} %get-tuple-element.31.own), channel_id=1, source_target_pairs={{1,2},{3,4},{5,6},{7,8},{9,10},{11,12},{13,14},{15,0},{2,1},{4,3},... | collective-permute-start | bytes 6193160 | tf_op jit(solution)/shard_map/ppermute | solution.py:632
  12.7 6.4 %collective-permute-start = (bf16[4,2,72,512]{3,2,1,0:T(8,128)(2,1)}, bf16[4,2,72,512]{3,2,1,0:T(8,128)(2,1)S(1)}, u32[]{:S(2)}, u32[]{:S(2)}) collective-permute-start(bf16[4,2,72,512]{3,2,1,0:T(8,128)(2,1)} %bitcast.52), channel_id=1, source_target_pairs={{16,0},{32,16},{48,32},{64,48},{80,64},{96,80},{112,96},{17,1},{33... | collective-permute-start | bytes 1769480 | tf_op jit(solution)/shard_map/ppermute | solution.py:634
  19.1 1.9 %collective-permute-start.1 = (bf16[4,2,72,512]{3,2,1,0:T(8,128)(2,1)}, bf16[4,2,72,512]{3,2,1,0:T(8,128)(2,1)}, u32[]{:S(2)}, u32[]{:S(2)}) collective-permute-start(bf16[4,2,72,512]{3,2,1,0:T(8,128)(2,1)} %bitcast.54), channel_id=1, source_target_pairs={{0,16},{16,32},{32,48},{48,64},{64,80},{80,96},{96,112},{1,17},{17... | collective-permute-start | bytes 1769480 | tf_op jit(solution)/shard_map/ppermute | solution.py:635
  21.0 0.0 copy-done.2
  21.0 0.6 pad.4.table
  21.7 5.2 %window_bias.1.bias = f32[1,2,144,576]{3,2,1,0:T(8,128)} custom-call(f32[8,768]{1,0:T(8,128)} %pad.4.table, bf16[1536,576]{1,0:T(8,128)(2,1)} %constant.52.clone.hot, bf16[144,192]{1,0:T(8,128)(2,1)} %constant.53.clone.squeeze), custom_call_target="tpu_custom_call" | custom-call | flops 1358954496 | bytes 3145728 | tf_op jit(solution)/shard_map/window_bias/pallas_call | solution.py:572
  26.9 0.0 collective-permute-done.3.halo
  26.9 28.9 %inner_windows.1 = (bf16[2,16,72,512]{3,2,1,0:T(8,128)(2,1)}, bf16[2,16,72,512]{3,2,1,0:T(8,128)(2,1)}, bf16[2,16,72,512]{3,2,1,0:T(8,128)(2,1)}, bf16[2,16,72,5...) custom-call(s32[1]{0:T(128)} %bitcast.core, bf16[2,16,72,512]{3,2,1,0:T(8,128)(2,1)} %bitcast.41, ...), custom_call_target="tpu_custom_call" | custom-call | flops 7134511104 | bytes 25165824 | tf_op jit(solution)/shard_map/inner_windows/pallas_call | solution.py:355
  55.8 10.2 %collective-permute-done.2.halo = bf16[4,7,72,512]{3,2,1,0:T(8,128)(2,1)} collective-permute-done((bf16[4,7,72,512]{3,2,1,0:T(8,128)(2,1)}, bf16[4,7,72,512]{3,2,1,0:T(8,128)(2,1)}, u32[]{:S(2)}, u32[]{:S(2)}) %collective-permute-start.2) | collective-permute-done | bytes 2064416 | tf_op jit(solution)/shard_map/ppermute | solution.py:632
  66.0 10.8 %outer_windows.2 = (bf16[2,48,3,8,512]{4,3,2,1,0:T(8,128)(2,1)}, bf16[2,48,3,8,512]{4,3,2,1,0:T(8,128)(2,1)}, bf16[2,48,3,8,512]{4,3,2,1,0:T(8,128)(2,1)}, bf16[2,48,3,8,512]{4,3,2,1,0:T(8,128)(2,1)}, f32[8,128]{1,0:T(8,128)}) custom-call(s32[1]{0:T(128)} %bitcast.core, ...), custom_call_target="tpu_custom_call", output_to_operand_aliasing={{0}: (6, {}), {1}: (7, {}), {2}: (8, {}), {3}: (9, {})} | custom-call | flops 2038431744 | bytes 8388608 | tf_op jit(solution)/shard_map/outer_windows/pallas_call | solution.py:435
  76.9 0.0 collective-permute-done.below
  76.9 0.0 copy-start.1
  76.9 0.0 collective-permute-done.1.above
  76.9 0.9 copy-done.1
  77.8 4.4 %pack_corners.1 = (bf16[4,2,72,512]{3,2,1,0:T(8,128)(2,1)}, bf16[4,2,72,512]{3,2,1,0:T(8,128)(2,1)}, bf16[4,2,144,512]{3,2,1,0:T(8,128)(2,1)}) custom-call(s32[1]{0:T(128)} %bitcast.core, bf16[4,2,72,512]{3,2,1,0:T(8,128)(2,1)} %bitcast.53, bf16[4,2,72,512]{3,2,1,0:T(8,128)(2,1)} %bitcast.55, bf16[4,2,72,512]{3,2,1,0:T(8,128)(2,1)} %copy-done.1, ...), custom_call_target="tpu_custom_call" | custom-call | flops 679477248 | bytes 5242880 | tf_op jit(solution)/shard_map/pack_corners/pallas_call | solution.py:192
  82.2 0.0 collective-permute-start.4
  82.2 2.0 %collective-permute-start.5 = (bf16[4,2,72,512]{3,2,1,0:T(8,128)(2,1)}, bf16[4,2,72,512]{3,2,1,0:T(8,128)(2,1)}, u32[]{:S(2)}, u32[]{:S(2)}) collective-permute-start(bf16[4,2,72,512]{3,2,1,0:T(8,128)(2,1)} %get-tuple-element.41.far), channel_id=1, source_target_pairs={{1,2},{3,4},{5,6},{7,8},{9,10},{11,12},{13,14},{15,0},{2,1},{4,3},... | collective-permute-start | bytes 1769480 | tf_op jit(solution)/shard_map/ppermute | solution.py:644
  84.2 0.7 add_convert_fusion.flags
  84.8 8.8 %outer_windows.3 = (bf16[2,48,3,8,512]{4,3,2,1,0:T(8,128)(2,1)}, bf16[2,48,3,8,512]{4,3,2,1,0:T(8,128)(2,1)}, bf16[2,48,3,8,512]{4,3,2,1,0:T(8,128)(2,1)}, bf16[2,48,3,8,512]{4,3,2,1,0:T(8,128)(2,1)}, f32[8,128]{1,0:T(8,128)}) custom-call(s32[1]{0:T(128)} %bitcast.core, ...), custom_call_target="tpu_custom_call", output_to_operand_aliasing={{0}: (6, {}), {1}: (7, {}), {2}: (8, {}), {3}: (9, {})} | custom-call | flops 1528823808 | bytes 6291456 | tf_op jit(solution)/shard_map/outer_windows/pallas_call | solution.py:435
  93.6 0.0 collective-permute-done.4.near_halo
  93.6 0.0 copy-start
  93.6 6.0 %collective-permute-done.5.far_halo = bf16[4,2,72,512]{3,2,1,0:T(8,128)(2,1)} collective-permute-done((bf16[4,2,72,512]{3,2,1,0:T(8,128)(2,1)}, bf16[4,2,72,512]{3,2,1,0:T(8,128)(2,1)}, u32[]{:S(2)}, u32[]{:S(2)}) %collective-permute-start.5) | collective-permute-done | bytes 589856 | tf_op jit(solution)/shard_map/ppermute | solution.py:644
  99.6 0.0 copy-done
  99.6 12.1 %corner_windows.1 = (bf16[2,16,72,512]{3,2,1,0:T(8,128)(2,1)}, bf16[2,16,72,512]{3,2,1,0:T(8,128)(2,1)}, bf16[2,16,72,512]{3,2,1,0:T(8,128)(2,1)}, bf16[2,16,72,512]{3,2,1,0:T(8,128)(2,1)}) custom-call(s32[1]{0:T(128)} %bitcast.core, s32[2]{0:T(128)} %add_convert_fusion.flags, ...), custom_call_target="tpu_custom_call", output_to_operand_aliasing={{0}: (9, {}), {1}: (10, {}), {2}: (11, {}), {3}: (12, {})} | custom-call | flops 3057647616 | bytes 8388608 | tf_op jit(solution)/shard_map/corner_windows/pallas_call | solution.py:502
Async XLA Ops:
  2.5 18.5 %copy-start.2 = (f32[8,759]{1,0:T(8,128)S(1)}, f32[8,759]{1,0:T(8,128)}, u32[]{:S(2)}) copy-start(f32[8,759]{1,0:T(8,128)} %param.22) | copy-start | bytes 72868
  9.9 17.0 %collective-permute-start.3 = (bf16[4,7,72,512]{3,2,1,0:T(8,128)(2,1)}, bf16[4,7,72,512]{3,2,1,0:T(8,128)(2,1)}, u32[]{:S(2)}, u32[]{:S(2)}) collective-permute-start(bf16[4,7,72,512]{3,2,1,0:T(8,128)(2,1)} %get-tuple-element.32.own), channel_id=1, source_target_pairs={{0,1},{1,0},{2,3},{3,2},{4,5},{5,4},{6,7},{7,6},{8,9},{9,8},{10,11... | collective-permute-start | bytes 6193160 | tf_op jit(solution)/shard_map/ppermute | solution.py:633
  10.7 55.4 %collective-permute-start.2 = (bf16[4,7,72,512]{3,2,1,0:T(8,128)(2,1)}, bf16[4,7,72,512]{3,2,1,0:T(8,128)(2,1)}, u32[]{:S(2)}, u32[]{:S(2)}) collective-permute-start(bf16[4,7,72,512]{3,2,1,0:T(8,128)(2,1)} %get-tuple-element.31.own), channel_id=1, source_target_pairs={{1,2},{3,4},{5,6},{7,8},{9,10},{11,12},{13,14},{15,0},{2,1},{4,3},... | collective-permute-start | bytes 6193160 | tf_op jit(solution)/shard_map/ppermute | solution.py:632
  12.7 64.2 %collective-permute-start = (bf16[4,2,72,512]{3,2,1,0:T(8,128)(2,1)}, bf16[4,2,72,512]{3,2,1,0:T(8,128)(2,1)S(1)}, u32[]{:S(2)}, u32[]{:S(2)}) collective-permute-start(bf16[4,2,72,512]{3,2,1,0:T(8,128)(2,1)} %bitcast.52), channel_id=1, source_target_pairs={{16,0},{32,16},{48,32},{64,48},{80,64},{96,80},{112,96},{17,1},{33... | collective-permute-start | bytes 1769480 | tf_op jit(solution)/shard_map/ppermute | solution.py:634
  19.1 57.8 %collective-permute-start.1 = (bf16[4,2,72,512]{3,2,1,0:T(8,128)(2,1)}, bf16[4,2,72,512]{3,2,1,0:T(8,128)(2,1)}, u32[]{:S(2)}, u32[]{:S(2)}) collective-permute-start(bf16[4,2,72,512]{3,2,1,0:T(8,128)(2,1)} %bitcast.54), channel_id=1, source_target_pairs={{0,16},{16,32},{32,48},{48,64},{64,80},{80,96},{96,112},{1,17},{17... | collective-permute-start | bytes 1769480 | tf_op jit(solution)/shard_map/ppermute | solution.py:635
  76.9 0.9 copy-start.1
  82.2 11.4 %collective-permute-start.4 = (bf16[4,2,72,512]{3,2,1,0:T(8,128)(2,1)}, bf16[4,2,72,512]{3,2,1,0:T(8,128)(2,1)S(1)}, u32[]{:S(2)}, u32[]{:S(2)}) collective-permute-start(bf16[4,2,72,512]{3,2,1,0:T(8,128)(2,1)} %get-tuple-element.40.near), channel_id=1, source_target_pairs={{0,1},{1,0},{2,3},{3,2},{4,5},{5,4},{6,7},{7,6},{8,9},{9,8},{10,11... | collective-permute-start | bytes 1769480 | tf_op jit(solution)/shard_map/ppermute | solution.py:645
  82.2 17.4 %collective-permute-start.5 = (bf16[4,2,72,512]{3,2,1,0:T(8,128)(2,1)}, bf16[4,2,72,512]{3,2,1,0:T(8,128)(2,1)}, u32[]{:S(2)}, u32[]{:S(2)}) collective-permute-start(bf16[4,2,72,512]{3,2,1,0:T(8,128)(2,1)} %get-tuple-element.41.far), channel_id=1, source_target_pairs={{1,2},{3,4},{5,6},{7,8},{9,10},{11,12},{13,14},{15,0},{2,1},{4,3},... | collective-permute-start | bytes 1769480 | tf_op jit(solution)/shard_map/ppermute | solution.py:644
  93.6 6.0 %copy-start = (bf16[4,2,72,512]{3,2,1,0:T(8,128)(2,1)}, bf16[4,2,72,512]{3,2,1,0:T(8,128)(2,1)S(1)}, u32[]{:S(2)}) copy-start(bf16[4,2,72,512]{3,2,1,0:T(8,128)(2,1)S(1)} %collective-permute-done.4.near_halo) | copy-start | bytes 1769476

commit v5 on v4

--- a/solution.py
+++ b/solution.py
@@ -61,20 +61,17 @@
     return pltpu.CompilerParams(vmem_limit_bytes=VMEM_BYTES)
 
 
-def edges_body(core, q, k, v, g, mask, embed, far_perm, near_perm, far, near, top, bottom, held, packed, rows, came, gone, rows_came, rows_gone):
+def edges_body(bands, q, k, v, g, mask, embed, far_perm, near_perm, far_a, far_b, near, top, bottom, below, above, held, packed, rows, came, gone, rows_came, rows_gone, sent, received):
+    core = lax.axis_index("lon") % 2
+    lat, lon = lax.axis_index("lat"), lax.axis_index("lon")
+    neighbours = ((lat + bands - 1) % bands, (lat + 1) % bands)
+    barrier = pltpu.get_barrier_semaphore()
+    for neighbour in neighbours:
+        pl.semaphore_signal(
+            barrier, inc=1, device_id=(neighbour, lon), device_id_type=pl.DeviceIdType.MESH
+        )
     sources = (q, k, v, g)
-    tiles = (2 * core[0], 2 - 2 * core[0])
-
-    def fetch(side, index):
-        return pltpu.make_async_copy(
-            sources[index].at[:, :, tiles[side]], held.at[side, index], came.at[side, index]
-        )
-
-    def send_off(side, index):
-        return pltpu.make_async_copy(
-            packed.at[side, index], (far, near)[side].at[index], gone.at[side, index]
-        )
-
+    tiles = (2 * core, 2 - 2 * core)
     ends = ((top, 0), (bottom, 45))
 
     def rows_in(end, index):
@@ -88,92 +85,117 @@
             rows.at[end, index], ends[end][0].at[index], rows_gone.at[end, index]
         )
 
-    for index in range(4):
-        fetch(0, index).start()
+    def rows_over(end, index):
+        return pltpu.make_async_remote_copy(
+            src_ref=rows.at[end, index],
+            dst_ref=(below, above)[end].at[index],
+            send_sem=sent.at[end, index],
+            recv_sem=received.at[end, index],
+            device_id=(neighbours[end], lon),
+            device_id_type=pl.DeviceIdType.MESH,
+        )
+
+    def fetch(side, index):
+        return pltpu.make_async_copy(
+            sources[index].at[:, :, tiles[side]], held.at[side, index], came.at[side, index]
+        )
+
+    def send_off(side, index):
+        if side == 0:
+            return [
+                pltpu.make_async_copy(
+                    packed.at[0, index, 0:4], far_a.at[index], gone.at[0, index]
+                ),
+                pltpu.make_async_copy(
+                    packed.at[0, index, 4:7], far_b.at[index], gone.at[2, index]
+                ),
+            ]
+        return [pltpu.make_async_copy(packed.at[1, index], near.at[index], gone.at[1, index])]
+
     for end in range(2):
         for index in range(4):
             rows_in(end, index).start()
-    for index in range(4):
-        fetch(1, index).start()
+    for side in range(2):
+        for index in range(4):
+            fetch(side, index).start()
+    pl.semaphore_wait(barrier, 2)
+    for end in range(2):
+        row = ends[end][1]
+        for index in (0, 2, 3, 1):
+            rows_in(end, index).wait()
+            if index == 1:
+                keyed = keyed_rows(rows[end, 1].astype(F32), mask[row : row + 3], embed[...])
+                rows[end, 1] = keyed.astype(BF16)
+            rows_over(end, index).start()
+            rows_out(end, index).start()
     for side in range(2):
         perm = (far_perm, near_perm)[side]
         for index in range(4):
             fetch(side, index).wait()
-            for band in range(1, 8):
-                lower, upper = 6 * band, 6 * band - 3
-                opening = held[side, index, :, lower : lower + 3].astype(F32)
-                closing = held[side, index, :, upper : upper + 3].astype(F32)
+
+            def pack_band(step, carry, side=side, index=index, perm=perm):
+                lower, upper = pl.ds(6 * step + 6, 3), pl.ds(6 * step + 3, 3)
+                opening = held[side, index, :, lower].astype(F32)
+                closing = held[side, index, :, upper].astype(F32)
                 if index == 1:
-                    opening = keyed_rows(
-                        opening, mask[lower : lower + 3, pl.ds(tiles[side], 1)][:, 0], embed[...]
-                    )
-                    closing = keyed_rows(
-                        closing, mask[upper : upper + 3, pl.ds(tiles[side], 1)][:, 0], embed[...]
-                    )
+                    column = pl.ds(tiles[side], 1)
+                    opening = keyed_rows(opening, mask[lower, column][:, 0], embed[...])
+                    closing = keyed_rows(closing, mask[upper, column][:, 0], embed[...])
                 tokens = jnp.concatenate(
                     [opening.reshape(48, 512), closing.reshape(48, 512)], axis=0
                 )
-                strip = dot(perm[0], tokens.astype(BF16))
+                strip = dot(perm[core], tokens.astype(BF16))
                 if index == 0:
                     strip = strip * 0.125
-                packed[side, index, band - 1] = strip.astype(BF16)
-            send_off(side, index).start()
-        if side == 0:
-            for end in range(2):
-                row = ends[end][1]
-                for index in range(4):
-                    rows_in(end, index).wait()
-                    if index == 1:
-                        keyed = keyed_rows(
-                            rows[end, 1].astype(F32), mask[row : row + 3], embed[...]
-                        )
-                        rows[end, 1] = keyed.astype(BF16)
-                    rows_out(end, index).start()
+                packed[side, index, step] = strip.astype(BF16)
+                return carry
+
+            lax.fori_loop(0, 7, pack_band, 0)
+            for copy in send_off(side, index):
+                copy.start()
     for index in range(4):
-        for side in range(2):
-            send_off(side, index).wait()
+        for copy in send_off(0, index) + send_off(1, index):
+            copy.wait()
         for end in range(2):
             rows_out(end, index).wait()
-
-
-def pack_edges(arrays, mask, embed, far_perm, near_perm, core):
+            rows_over(end, index).wait()
+
+
+def pack_edges(arrays, mask, embed, far_perm, near_perm, bands):
     tiles = [array.reshape(2, 48, 3, 8, 512) for array in arrays]
     anywhere = pl.BlockSpec(memory_space=pl.ANY)
-    strips = jax.ShapeDtypeStruct((4, 7, STRIP, 512), BF16)
+    local = pl.BlockSpec(memory_space=pltpu.VMEM)
+    far_a, far_b, near = (
+        jax.ShapeDtypeStruct((4, count, STRIP, 512), BF16) for count in (4, 3, 7)
+    )
     ends = jax.ShapeDtypeStruct((4, 2, 3, 3, 8, 512), BF16)
     return pl.pallas_call(
-        edges_body,
-        grid_spec=pltpu.PrefetchScalarGridSpec(
-            num_scalar_prefetch=1,
-            grid=(1,),
-            in_specs=[anywhere] * 4
-            + [
-                fixed_spec((48, 3, 8, 128)),
-                fixed_spec((1, 512)),
-                side_spec((STRIP, 96)),
-                side_spec((STRIP, 96)),
-            ],
-            out_specs=[anywhere] * 4,
-            scratch_shapes=[
-                pltpu.VMEM((2, 4, 2, 48, 8, 512), BF16),
-                pltpu.VMEM((2, 4, 7, STRIP, 512), BF16),
-                pltpu.VMEM((2, 4, 2, 3, 3, 8, 512), BF16),
-                pltpu.SemaphoreType.DMA((2, 4)),
-                pltpu.SemaphoreType.DMA((2, 4)),
-                pltpu.SemaphoreType.DMA((2, 4)),
-                pltpu.SemaphoreType.DMA((2, 4)),
-            ],
-        ),
-        out_shape=[strips, strips, ends, ends],
-        compiler_params=params(),
+        functools.partial(edges_body, bands),
+        in_specs=[anywhere] * 4 + [local] * 4,
+        out_specs=[anywhere] * 7,
+        scratch_shapes=[
+            pltpu.VMEM((2, 4, 2, 48, 8, 512), BF16),
+            pltpu.VMEM((2, 4, 7, STRIP, 512), BF16),
+            pltpu.VMEM((2, 4, 2, 3, 3, 8, 512), BF16),
+            pltpu.SemaphoreType.DMA((2, 4)),
+            pltpu.SemaphoreType.DMA((3, 4)),
+            pltpu.SemaphoreType.DMA((2, 4)),
+            pltpu.SemaphoreType.DMA((2, 4)),
+            pltpu.SemaphoreType.DMA((2, 4)),
+            pltpu.SemaphoreType.DMA((2, 4)),
+        ],
+        out_shape=[far_a, far_b, near, ends, ends, ends, ends],
+        compiler_params=pltpu.CompilerParams(
+            vmem_limit_bytes=VMEM_BYTES, collective_id=0, has_side_effects=True
+        ),
         cost_estimate=pl.CostEstimate(
             flops=2 * 56 * STRIP * 96 * 512, bytes_accessed=16 * MIB, transcendentals=0
         ),
         name="pack_edges",
-    )(core, *tiles, mask, embed, far_perm, near_perm)
-
-
-def corners_body(core, top, bottom, below, above, perm, done, far, near, mid):
+    )(*tiles, mask, embed, far_perm, near_perm)
+
+
+def corners_body(core, top, bottom, below, above, perm, far, near, mid):
     for index in range(4):
         for place, (first, second) in enumerate(((top, above), (below, bottom))):
             first = first[index].astype(F32)
@@ -187,15 +209,14 @@
             mid[index, place] = strips[2 * STRIP :].astype(BF16)
 
 
-def pack_corners(top, bottom, below, above, perm, core, done):
+def pack_corners(top, bottom, below, above, perm, core):
     sizes = (STRIP, STRIP, WIN)
     return pl.pallas_call(
         corners_body,
         grid_spec=pltpu.PrefetchScalarGridSpec(
             num_scalar_prefetch=1,
             grid=(1,),
-            in_specs=[fixed_spec((4, 2, STRIP, 512))] * 4
-            + [side_spec((2 * WIN, 2 * WIN)), pl.BlockSpec(memory_space=pl.ANY)],
+            in_specs=[fixed_spec((4, 2, STRIP, 512))] * 4 + [side_spec((2 * WIN, 2 * WIN))],
             out_specs=[fixed_spec((4, 2, size, 512)) for size in sizes],
         ),
         out_shape=[jax.ShapeDtypeStruct((4, 2, size, 512), BF16) for size in sizes],
@@ -204,7 +225,7 @@
             flops=2 * 8 * 288 * 288 * 512, bytes_accessed=5 * MIB, transcendentals=0
         ),
         name="pack_corners",
-    )(core, top, bottom, below, above, perm, done)
+    )(core, top, bottom, below, above, perm)
 
 
 def windows(win, slots, bias, scores, grads, low, dlow, store):
@@ -389,8 +410,8 @@
     )(core, *operands, mask, mask, embed, perm, own, halo, bias, back)
 
 
-def band_spec(first=0):
-    return pl.BlockSpec((4, 1, STRIP, 512), lambda s, core: (0, s + first, 0, 0))
+def band_spec():
+    return pl.BlockSpec((4, 1, STRIP, 512), lambda s, core: (0, s, 0, 0))
 
 
 def outer_body(first, count, core, own, halo, beside, bias, back, p0, p1, p2, p3, o0, o1, o2, o3, token, win, result, tiles, gone, *work):
@@ -438,8 +459,8 @@
             num_scalar_prefetch=1,
             grid=(count,),
             in_specs=[
-                band_spec(first),
-                band_spec(first),
+                band_spec(),
+                band_spec(),
                 pl.BlockSpec((4, 1, 80, 512), lambda s, core: (0, s + first, 0, 0)),
                 fixed_spec((1, 2, WIN, 576)),
                 side_spec((96, 160)),
@@ -626,24 +647,22 @@
     to_far += [(b, a) for a, b in to_far]
     to_near = [(i, i ^ 1) for i in range(sectors)]
 
-    far, near, top, bottom = pack_edges(arrays, mask, embed, far_perm, near_perm, core)
-    ends = (4, 2, STRIP, width)
-    top, bottom = top.reshape(ends), bottom.reshape(ends)
-    far_halo = lax.ppermute(far, "lon", to_far)
+    far_a, far_b, near, *edge_rows = pack_edges(arrays, mask, embed, far_perm, near_perm, bands)
+    top, bottom, below, above = (x.reshape(4, 2, STRIP, width) for x in edge_rows)
+    far_halo_a = lax.ppermute(far_a, "lon", to_far)
+    far_halo_b = lax.ppermute(far_b, "lon", to_far)
     near_halo = lax.ppermute(near, "lon", to_near)
-    below = lax.ppermute(top, "lat", [(i, i - 1) for i in range(1, bands)])
-    above = lax.ppermute(bottom, "lat", [(i, i + 1) for i in range(bands - 1)])
+
+    far_c, near_c, mid_c = pack_corners(top, bottom, below, above, all_perm, core)
+    far_halo_c = lax.ppermute(far_c, "lon", to_far)
+    near_halo_c = lax.ppermute(near_c, "lon", to_near)
 
     bias = window_bias(rel_table)
     *partial, beside, _ = inner(
         arrays, mask, embed, mid_perm, near, near_halo, bias, near_back, core
     )
-    *partial, done = outer(partial, far, far_halo, beside, bias, far_back, core, 0, 4)
-
-    far_c, near_c, mid_c = pack_corners(top, bottom, below, above, all_perm, core, done)
-    far_halo_c = lax.ppermute(far_c, "lon", to_far)
-    near_halo_c = lax.ppermute(near_c, "lon", to_near)
-    *partial, _ = outer(partial, far, far_halo, beside, bias, far_back, core, 4, 3)
+    *partial, _ = outer(partial, far_a, far_halo_a, beside, bias, far_back, core, 0, 4)
+    *partial, _ = outer(partial, far_b, far_halo_b, beside, bias, far_back, core, 4, 3)
     flags = jnp.stack([lat == 0, lat == bands - 1]).astype(jnp.int32)
     final = corners(
         partial, flags, mid_c, near_c, near_halo_c, far_c, far_halo_c, bias, corner_back, core

time: 112 us -> 109 us (0.973)
  the two profiles are of different devices: /device:TPU:13 before, /device:TPU:8 now
where the time goes in v5:
time: 109 us; the launch traced here: 107 us
  Pallas kernels  91.5 us (84%)
  starting transfers between devices  10.3 us (9%)
  local copies, waits for them, and re-layouts  2.77 us (3%)
  other arithmetic  1.37 us (1%)
    pallas_call x1, Pallas kernels, inner(): pl.pallas_call(inner_body, grid_spec=pltpu.PrefetchScalarGridSpec(num_sca...  29 us
    pallas_call x1, Pallas kernels, pack_edges(): pl.pallas_call(functools.partial(edges_body, bands), in_specs=[anywhere]...  21.1 us
    pallas_call x2, Pallas kernels, outer(): pl.pallas_call(functools.partial(outer_body, first, count), grid_spec=plt...  19.6 us
    pallas_call x1, Pallas kernels, corners(): pl.pallas_call(corner_body, grid_spec=pltpu.PrefetchScalarGridSpec(num_sc...  12.1 us
    pallas_call x1, Pallas kernels, window_bias(): pl.pallas_call(bias_body, out_shape=jax.ShapeDtypeStruct((1, 2, WIN, 576)...  5.25 us
    ppermute x1, starting transfers between devices, shards(): far_halo_a = lax.ppermute(far_a, 'lon', to_far)  4.88 us
    ppermute x1, starting transfers between devices, shards(): far_halo_c = lax.ppermute(far_c, 'lon', to_far)  4.8 us
    pallas_call x1, Pallas kernels, pack_corners(): pl.pallas_call(corners_body, grid_spec=pltpu.PrefetchScalarGridSpec(num_s...  4.41 us
  transfers between devices with their start and end apart: 5, of which 0 were waited for; matrix products, arithmetic and copies ran while one was open for 1% of the time, Pallas kernels for 55%

profile of v5, /device:TPU:8, one launch (start us, length us, event | category | flops | bytes accessed | tf_op | source)
XLA Modules:
  0.0 106.8 jit_solution(8841622271263639916)
XLA Ops:
  0.6 0.7 convert_bitcast_fusion
  1.3 0.1 copy.32
  1.4 1.1 %broadcast_in_dim.8.mask.m0.m1 = f32[48,3,8,128]{3,2,1,0:T(8,128)} broadcast(f32[48,3,8]{2,1,0:T(4,128)S(1)} %copy.32), dimensions={0,1,2} | broadcast | bytes 594432 | tf_op jit(solution)/shard_map/broadcast_in_dim | solution.py:639
  2.5 21.1 %pack_edges.1 = (bf16[4,4,72,512]{3,2,1,0:T(8,128)(2,1)}, bf16[4,3,72,512]{3,2,1,0:T(8,128)(2,1)}, bf16[4,7,72,512]{3,2,1,0:T(8,128)(2,1)}, bf16[4,2,3,3,8,512]{...) custom-call(bf16[2,48,3,8,512]{4,3,2,1,0:T(8,128)(2,1)} %bitcast.42,, ...), custom_call_target="tpu_custom_call" | custom-call | flops 396361728 | bytes 16777216 | tf_op jit(solution)/shard_map/pack_edges/pallas_call | solution.py:172
  23.6 0.0 copy-start.1
  23.6 0.1 collective-permute-start.3
  23.7 4.9 %collective-permute-start.4 = (bf16[4,4,72,512]{3,2,1,0:T(8,128)(2,1)}, bf16[4,4,72,512]{3,2,1,0:T(8,128)(2,1)}, u32[]{:S(2)}, u32[]{:S(2)}) collective-permute-start(bf16[4,4,72,512]{3,2,1,0:T(8,128)(2,1)} %get-tuple-element.41.own), channel_id=1, source_target_pairs={{1,2},{3,4},{5,6},{7,8},{9,10},{11,12},{13,14},{15,0},{2,1},{4,3},... | collective-permute-start | bytes 3538952 | tf_op jit(solution)/shard_map/ppermute | solution.py:652
  28.6 0.6 collective-permute-start.2
  29.2 4.4 %pack_corners.1 = (bf16[4,2,72,512]{3,2,1,0:T(8,128)(2,1)}, bf16[4,2,72,512]{3,2,1,0:T(8,128)(2,1)}, bf16[4,2,144,512]{3,2,1,0:T(8,128)(2,1)}) custom-call(s32[1]{0:T(128)} %bitcast.core, bf16[4,2,72,512]{3,2,1,0:T(8,128)(2,1)} %bitcast.54, bf16[4,2,72,512]{3,2,1,0:T(8,128)(2,1)} %bitcast.55, bf16[4,2,72,512]{3,2,1,0:T(8,128)(2,1)} %bitcast.56, ...), custom_call_target="tpu_custom_call" | custom-call | flops 679477248 | bytes 5242880 | tf_op jit(solution)/shard_map/pack_corners/pallas_call | solution.py:214
  33.6 0.0 collective-permute-start
  33.6 4.8 %collective-permute-start.1 = (bf16[4,2,72,512]{3,2,1,0:T(8,128)(2,1)}, bf16[4,2,72,512]{3,2,1,0:T(8,128)(2,1)}, u32[]{:S(2)}, u32[]{:S(2)}) collective-permute-start(bf16[4,2,72,512]{3,2,1,0:T(8,128)(2,1)} %get-tuple-element.37.far), channel_id=1, source_target_pairs={{1,2},{3,4},{5,6},{7,8},{9,10},{11,12},{13,14},{15,0},{2,1},{4,3},... | collective-permute-start | bytes 1769480 | tf_op jit(solution)/shard_map/ppermute | solution.py:657
  38.4 0.0 copy-done.1
  38.4 0.6 pad.4.table
  39.0 5.3 %window_bias.1.bias = f32[1,2,144,576]{3,2,1,0:T(8,128)} custom-call(f32[8,768]{1,0:T(8,128)} %pad.4.table, bf16[1536,576]{1,0:T(8,128)(2,1)} %constant.52.clone.hot, bf16[144,192]{1,0:T(8,128)(2,1)} %constant.53.clone.squeeze), custom_call_target="tpu_custom_call" | custom-call | flops 1358954496 | bytes 3145728 | tf_op jit(solution)/shard_map/window_bias/pallas_call | solution.py:593
  44.2 0.7 add_convert_fusion.flags
  44.9 0.0 collective-permute-done.3.halo
  44.9 29.0 %inner_windows.1 = (bf16[2,16,72,512]{3,2,1,0:T(8,128)(2,1)}, bf16[2,16,72,512]{3,2,1,0:T(8,128)(2,1)}, bf16[2,16,72,512]{3,2,1,0:T(8,128)(2,1)}, bf16[2,16,72,5...) custom-call(s32[1]{0:T(128)} %bitcast.core, bf16[2,16,72,512]{3,2,1,0:T(8,128)(2,1)} %bitcast.43, ...), custom_call_target="tpu_custom_call" | custom-call | flops 7134511104 | bytes 25165824 | tf_op jit(solution)/shard_map/inner_windows/pallas_call | solution.py:376
  73.9 0.0 collective-permute-done.4.halo
  73.9 10.9 %outer_windows.2 = (bf16[2,48,3,8,512]{4,3,2,1,0:T(8,128)(2,1)}, bf16[2,48,3,8,512]{4,3,2,1,0:T(8,128)(2,1)}, bf16[2,48,3,8,512]{4,3,2,1,0:T(8,128)(2,1)}, bf16[2,48,3,8,512]{4,3,2,1,0:T(8,128)(2,1)}, f32[8,128]{1,0:T(8,128)}) custom-call(s32[1]{0:T(128)} %bitcast.core, ...), custom_call_target="tpu_custom_call", output_to_operand_aliasing={{0}: (6, {}), {1}: (7, {}), {2}: (8, {}), {3}: (9, {})} | custom-call | flops 2038431744 | bytes 8388608 | tf_op jit(solution)/shard_map/outer_windows/pallas_call | solution.py:456
  84.8 0.0 collective-permute-done.2.halo
  84.8 0.0 copy-start
  84.8 1.0 copy-done
  85.8 8.8 %outer_windows.3 = (bf16[2,48,3,8,512]{4,3,2,1,0:T(8,128)(2,1)}, bf16[2,48,3,8,512]{4,3,2,1,0:T(8,128)(2,1)}, bf16[2,48,3,8,512]{4,3,2,1,0:T(8,128)(2,1)}, bf16[2,48,3,8,512]{4,3,2,1,0:T(8,128)(2,1)}, f32[8,128]{1,0:T(8,128)}) custom-call(s32[1]{0:T(128)} %bitcast.core, ...), custom_call_target="tpu_custom_call", output_to_operand_aliasing={{0}: (6, {}), {1}: (7, {}), {2}: (8, {}), {3}: (9, {})} | custom-call | flops 1528823808 | bytes 6291456 | tf_op jit(solution)/shard_map/outer_windows/pallas_call | solution.py:456
  94.5 0.0 collective-permute-done.near_halo
  94.5 0.0 collective-permute-done.1.far_halo
  94.6 12.1 %corner_windows.1 = (bf16[2,16,72,512]{3,2,1,0:T(8,128)(2,1)}, bf16[2,16,72,512]{3,2,1,0:T(8,128)(2,1)}, bf16[2,16,72,512]{3,2,1,0:T(8,128)(2,1)}, bf16[2,16,72,512]{3,2,1,0:T(8,128)(2,1)}) custom-call(s32[1]{0:T(128)} %bitcast.core, s32[2]{0:T(128)} %add_convert_fusion.flags, ...), custom_call_target="tpu_custom_call", output_to_operand_aliasing={{0}: (9, {}), {1}: (10, {}), {2}: (11, {}), {3}: (12, {})} | custom-call | flops 3057647616 | bytes 8388608 | tf_op jit(solution)/shard_map/corner_windows/pallas_call | solution.py:523
Async XLA Ops:
  23.6 14.8 %copy-start.1 = (f32[8,759]{1,0:T(8,128)S(1)}, f32[8,759]{1,0:T(8,128)}, u32[]{:S(2)}) copy-start(f32[8,759]{1,0:T(8,128)} %param.22) | copy-start | bytes 72868
  23.6 21.3 %collective-permute-start.3 = (bf16[4,7,72,512]{3,2,1,0:T(8,128)(2,1)}, bf16[4,7,72,512]{3,2,1,0:T(8,128)(2,1)}, u32[]{:S(2)}, u32[]{:S(2)}) collective-permute-start(bf16[4,7,72,512]{3,2,1,0:T(8,128)(2,1)} %get-tuple-element.39.own), channel_id=1, source_target_pairs={{0,1},{1,0},{2,3},{3,2},{4,5},{5,4},{6,7},{7,6},{8,9},{9,8},{10,11... | collective-permute-start | bytes 6193160 | tf_op jit(solution)/shard_map/ppermute | solution.py:654
  23.7 50.2 %collective-permute-start.4 = (bf16[4,4,72,512]{3,2,1,0:T(8,128)(2,1)}, bf16[4,4,72,512]{3,2,1,0:T(8,128)(2,1)}, u32[]{:S(2)}, u32[]{:S(2)}) collective-permute-start(bf16[4,4,72,512]{3,2,1,0:T(8,128)(2,1)} %get-tuple-element.41.own), channel_id=1, source_target_pairs={{1,2},{3,4},{5,6},{7,8},{9,10},{11,12},{13,14},{15,0},{2,1},{4,3},... | collective-permute-start | bytes 3538952 | tf_op jit(solution)/shard_map/ppermute | solution.py:652
  28.6 56.2 %collective-permute-start.2 = (bf16[4,3,72,512]{3,2,1,0:T(8,128)(2,1)}, bf16[4,3,72,512]{3,2,1,0:T(8,128)(2,1)S(1)}, u32[]{:S(2)}, u32[]{:S(2)}) collective-permute-start(bf16[4,3,72,512]{3,2,1,0:T(8,128)(2,1)} %get-tuple-element.38.own), channel_id=1, source_target_pairs={{1,2},{3,4},{5,6},{7,8},{9,10},{11,12},{13,14},{15,0},{2,1},{4,3},... | collective-permute-start | bytes 2654216 | tf_op jit(solution)/shard_map/ppermute | solution.py:653
  33.6 61.0 %collective-permute-start = (bf16[4,2,72,512]{3,2,1,0:T(8,128)(2,1)}, bf16[4,2,72,512]{3,2,1,0:T(8,128)(2,1)}, u32[]{:S(2)}, u32[]{:S(2)}) collective-permute-start(bf16[4,2,72,512]{3,2,1,0:T(8,128)(2,1)} %get-tuple-element.36.near), channel_id=1, source_target_pairs={{0,1},{1,0},{2,3},{3,2},{4,5},{5,4},{6,7},{7,6},{8,9},{9,8},{10,11... | collective-permute-start | bytes 1769480 | tf_op jit(solution)/shard_map/ppermute | solution.py:658
  33.6 61.0 %collective-permute-start.1 = (bf16[4,2,72,512]{3,2,1,0:T(8,128)(2,1)}, bf16[4,2,72,512]{3,2,1,0:T(8,128)(2,1)}, u32[]{:S(2)}, u32[]{:S(2)}) collective-permute-start(bf16[4,2,72,512]{3,2,1,0:T(8,128)(2,1)} %get-tuple-element.37.far), channel_id=1, source_target_pairs={{1,2},{3,4},{5,6},{7,8},{9,10},{11,12},{13,14},{15,0},{2,1},{4,3},... | collective-permute-start | bytes 1769480 | tf_op jit(solution)/shard_map/ppermute | solution.py:657
  84.8 1.0 copy-start

commit v6 on v5

--- a/solution.py
+++ b/solution.py
@@ -61,7 +61,7 @@
     return pltpu.CompilerParams(vmem_limit_bytes=VMEM_BYTES)
 
 
-def edges_body(bands, q, k, v, g, mask, embed, far_perm, near_perm, far_a, far_b, near, top, bottom, below, above, held, packed, rows, came, gone, rows_came, rows_gone, sent, received):
+def edges_body(bands, q, k, v, g, mask, embed, perm, table, hot, squeeze, far_a, far_b, near, mid, top, bottom, below, above, bias, held, packed, interior, rows, came, gone, rows_came, rows_gone, sent, received, wide, part):
     core = lax.axis_index("lon") % 2
     lat, lon = lax.axis_index("lat"), lax.axis_index("lon")
     neighbours = ((lat + bands - 1) % bands, (lat + 1) % bands)
@@ -71,7 +71,7 @@
             barrier, inc=1, device_id=(neighbour, lon), device_id_type=pl.DeviceIdType.MESH
         )
     sources = (q, k, v, g)
-    tiles = (2 * core, 2 - 2 * core)
+    tiles = (2 * core, 2 - 2 * core, 1)
     ends = ((top, 0), (bottom, 45))
 
     def rows_in(end, index):
@@ -110,13 +110,15 @@
                     packed.at[0, index, 4:7], far_b.at[index], gone.at[2, index]
                 ),
             ]
-        return [pltpu.make_async_copy(packed.at[1, index], near.at[index], gone.at[1, index])]
+        if side == 1:
+            return [pltpu.make_async_copy(packed.at[1, index], near.at[index], gone.at[1, index])]
+        return [pltpu.make_async_copy(interior.at[index], mid.at[index], gone.at[3, index])]
 
     for end in range(2):
         for index in range(4):
             rows_in(end, index).start()
-    for side in range(2):
-        for index in range(4):
+    for index in range(4):
+        for side in range(3):
             fetch(side, index).start()
     pl.semaphore_wait(barrier, 2)
     for end in range(2):
@@ -128,40 +130,43 @@
                 rows[end, 1] = keyed.astype(BF16)
             rows_over(end, index).start()
             rows_out(end, index).start()
-    for side in range(2):
-        perm = (far_perm, near_perm)[side]
-        for index in range(4):
+    for index in range(4):
+        for side in range(3):
             fetch(side, index).wait()
 
-            def pack_band(step, carry, side=side, index=index, perm=perm):
-                lower, upper = pl.ds(6 * step + 6, 3), pl.ds(6 * step + 3, 3)
-                opening = held[side, index, :, lower].astype(F32)
-                closing = held[side, index, :, upper].astype(F32)
-                if index == 1:
-                    column = pl.ds(tiles[side], 1)
-                    opening = keyed_rows(opening, mask[lower, column][:, 0], embed[...])
-                    closing = keyed_rows(closing, mask[upper, column][:, 0], embed[...])
-                tokens = jnp.concatenate(
-                    [opening.reshape(48, 512), closing.reshape(48, 512)], axis=0
-                )
-                strip = dot(perm[core], tokens.astype(BF16))
-                if index == 0:
-                    strip = strip * 0.125
-                packed[side, index, step] = strip.astype(BF16)
-                return carry
-
-            lax.fori_loop(0, 7, pack_band, 0)
+        def pack_band(step, carry, index=index):
+            lower, upper = pl.ds(6 * step + 6, 3), pl.ds(6 * step + 3, 3)
+            pieces = []
+            for side in range(3):
+                for span in (lower, upper):
+                    piece = held[side, index, :, span].astype(F32)
+                    if index == 1:
+                        column = mask[span, pl.ds(tiles[side], 1)][:, 0]
+                        piece = keyed_rows(piece, column, embed[...])
+                    pieces.append(piece.reshape(48, 512))
+            strips = dot(perm[core], jnp.concatenate(pieces, axis=0).astype(BF16))
+            if index == 0:
+                strips = strips * 0.125
+            packed[0, index, step] = strips[:STRIP].astype(BF16)
+            packed[1, index, step] = strips[STRIP : 2 * STRIP].astype(BF16)
+            interior[index, step] = strips[2 * STRIP :].astype(BF16)
+            return carry
+
+        lax.fori_loop(0, 7, pack_band, 0)
+        for side in range(3):
             for copy in send_off(side, index):
                 copy.start()
-    for index in range(4):
-        for copy in send_off(0, index) + send_off(1, index):
-            copy.wait()
+    bias_body(table, hot, squeeze, bias, wide, part)
+    for index in range(4):
+        for side in range(3):
+            for copy in send_off(side, index):
+                copy.wait()
         for end in range(2):
             rows_out(end, index).wait()
             rows_over(end, index).wait()
 
 
-def pack_edges(arrays, mask, embed, far_perm, near_perm, bands):
+def pack_edges(arrays, mask, embed, perm, bias_operands, bands):
     tiles = [array.reshape(2, 48, 3, 8, 512) for array in arrays]
     anywhere = pl.BlockSpec(memory_space=pl.ANY)
     local = pl.BlockSpec(memory_space=pltpu.VMEM)
@@ -169,30 +174,35 @@
         jax.ShapeDtypeStruct((4, count, STRIP, 512), BF16) for count in (4, 3, 7)
     )
     ends = jax.ShapeDtypeStruct((4, 2, 3, 3, 8, 512), BF16)
+    interior = jax.ShapeDtypeStruct((4, 7, WIN, 512), BF16)
     return pl.pallas_call(
         functools.partial(edges_body, bands),
-        in_specs=[anywhere] * 4 + [local] * 4,
-        out_specs=[anywhere] * 7,
+        in_specs=[anywhere] * 4 + [local] * 6,
+        out_specs=[anywhere] * 8 + [local],
         scratch_shapes=[
-            pltpu.VMEM((2, 4, 2, 48, 8, 512), BF16),
+            pltpu.VMEM((3, 4, 2, 48, 8, 512), BF16),
             pltpu.VMEM((2, 4, 7, STRIP, 512), BF16),
+            pltpu.VMEM((4, 7, WIN, 512), BF16),
             pltpu.VMEM((2, 4, 2, 3, 3, 8, 512), BF16),
-            pltpu.SemaphoreType.DMA((2, 4)),
             pltpu.SemaphoreType.DMA((3, 4)),
+            pltpu.SemaphoreType.DMA((4, 4)),
             pltpu.SemaphoreType.DMA((2, 4)),
             pltpu.SemaphoreType.DMA((2, 4)),
             pltpu.SemaphoreType.DMA((2, 4)),
             pltpu.SemaphoreType.DMA((2, 4)),
+            pltpu.VMEM((2, 192, 4 * 384), F32),
+            pltpu.VMEM((2, 2, 192, 4 * 384), BF16),
         ],
-        out_shape=[far_a, far_b, near, ends, ends, ends, ends],
+        out_shape=[far_a, far_b, near, interior, ends, ends, ends, ends]
+        + [jax.ShapeDtypeStruct((1, 2, WIN, 576), F32)],
         compiler_params=pltpu.CompilerParams(
             vmem_limit_bytes=VMEM_BYTES, collective_id=0, has_side_effects=True
         ),
         cost_estimate=pl.CostEstimate(
-            flops=2 * 56 * STRIP * 96 * 512, bytes_accessed=16 * MIB, transcendentals=0
+            flops=2 * 28 * 288 * 288 * 512, bytes_accessed=24 * MIB, transcendentals=0
         ),
         name="pack_edges",
-    )(*tiles, mask, embed, far_perm, near_perm)
+    )(*tiles, mask, embed, perm, *bias_operands)
 
 
 def corners_body(core, top, bottom, below, above, perm, far, near, mid):
@@ -287,19 +297,11 @@
         put(halo, own)
 
 
-def inner_body(core, q0, q1, k0, k1, v0, v1, g0, g1, m0, m1, embed, perm, own, halo, bias, back, *rest):
+def inner_body(core, mid, own, halo, bias, back, *rest):
     outs, beside, token, (win, result, ready, gone), work = rest[:4], rest[4], rest[5], rest[6:10], rest[10:]
     s = pl.program_id(0)
-    for index, pair in enumerate(((q0, q1), (k0, k1), (v0, v1), (g0, g1))):
-        first, second = (source[:, 0].astype(F32) for source in pair)
-        if index == 1:
-            first = keyed_rows(first, m0[...].reshape(STRIP, 128), embed[...])
-            second = keyed_rows(second, m1[...].reshape(STRIP, 128), embed[...])
-        tokens = jnp.concatenate([first[0], first[1], second[0], second[1]], axis=0)
-        packed = dot(perm[...], tokens.astype(BF16))
-        if index == 0:
-            packed = packed * 0.125
-        win[0, index] = packed.astype(BF16)
+    for index in range(4):
+        win[0, index] = mid[index, 0]
     place_pair(win, 1, own, halo, core[0] == 0)
 
     starts = (pl.multiple_of(WIN * core[0], 16), pl.multiple_of(WIN * (1 - core[0]), 16))
@@ -362,28 +364,15 @@
     )
 
 
-def inner(arrays, mask, embed, perm, own, halo, bias, back, core):
-    operands, specs = [], []
-    block = (2, 1, STRIP, 512)
-    for array in arrays:
-        array = array.reshape(2, 16, STRIP, 512)
-        operands += [array, array]
-        specs += [
-            pl.BlockSpec(block, lambda s, core: (0, 2 * s + 2, 0, 0)),
-            pl.BlockSpec(block, lambda s, core: (0, 2 * s + 1, 0, 0)),
-        ]
+def inner(mid, own, halo, bias, back, core):
     anywhere = pl.BlockSpec(memory_space=pl.ANY)
     return pl.pallas_call(
         inner_body,
         grid_spec=pltpu.PrefetchScalarGridSpec(
             num_scalar_prefetch=1,
             grid=(7,),
-            in_specs=specs
-            + [
-                pl.BlockSpec((3, 3, 8, 128), lambda s, core: (2 * s + 2, 0, 0, 0)),
-                pl.BlockSpec((3, 3, 8, 128), lambda s, core: (2 * s + 1, 0, 0, 0)),
-                fixed_spec((1, 512)),
-                fixed_spec((WIN, 2 * WIN)),
+            in_specs=[
+                pl.BlockSpec((4, 1, WIN, 512), lambda s, core: (0, s, 0, 0)),
                 band_spec(),
                 band_spec(),
                 fixed_spec((1, 2, WIN, 576)),
@@ -407,14 +396,22 @@
         compiler_params=params(),
         cost_estimate=window_cost(14, 24 * MIB),
         name="inner_windows",
-    )(core, *operands, mask, mask, embed, perm, own, halo, bias, back)
+    )(core, mid, own, halo, bias, back)
 
 
 def band_spec():
     return pl.BlockSpec((4, 1, STRIP, 512), lambda s, core: (0, s, 0, 0))
 
 
-def outer_body(first, count, core, own, halo, beside, bias, back, p0, p1, p2, p3, o0, o1, o2, o3, token, win, result, tiles, gone, *work):
+def cut_bias(cut, bias, flag):
+    key_part = lax.broadcasted_iota(jnp.int32, (WIN, 576), 0) % STRIP < HALF
+    query_part = lax.broadcasted_iota(jnp.int32, (WIN, 576), 1) % STRIP < HALF
+    apart = (key_part != query_part) & (flag != 0)
+    for group in range(2):
+        cut[0, group] = jnp.where(apart, -jnp.inf, bias[0, group])
+
+
+def outer_body(first, count, edge, core, flags, own, halo, beside, bias, back, p0, p1, p2, p3, o0, o1, o2, o3, win, result, tiles, gone, cut, *work):
     s = pl.program_id(0)
     tile = 2 * core[0]
     outs = (o0, o1, o2, o3)
@@ -423,12 +420,15 @@
     def keep(slot, index, cols, value):
         result[index, 0:WIN, cols] = value.astype(BF16)
 
-    windows(win, 1, bias, *work, keep)
+    if edge:
+        cut_bias(cut, bias, flags[s])
+    windows(win, 1, cut if edge else bias, *work, keep)
 
     def leave(step, index):
+        size, row = (3, 45 * step) if edge else (6, 6 * (step + first) + 3)
         return pltpu.make_async_copy(
-            tiles.at[index, :, pl.ds(6 * step, 6)],
-            outs[index].at[:, pl.ds(6 * (step + first) + 3, 6), tile],
+            tiles.at[index, :, pl.ds(6 * step, size)],
+            outs[index].at[:, pl.ds(row, size), tile],
             gone.at[step, index],
         )
 
@@ -438,82 +438,79 @@
         result[index, beside_at] = beside[index, 0]
         full = dot(back[0], result[index, used]).reshape(2, 2, 3, 8, 512)
         for part in range(2):
+            if edge:
+
+                @pl.when(s == part)
+                def _(part=part, full=full, index=index):
+                    tiles[index, :, 6 * part : 6 * part + 3] = full[part].astype(BF16)
+
+                continue
             span = pl.ds(6 * s + 3 * (1 - part), 3)
             tiles[index, :, span] = full[part].astype(BF16)
         leave(s, index).start()
 
     @pl.when(s == count - 1)
     def _():
-        token[...] = jnp.zeros_like(token)
         for index in range(4):
             for step in range(count):
                 leave(step, index).wait()
 
 
-def outer(partial, own, halo, beside, bias, back, core, first, count):
+def outer(partial, own, halo, beside, bias, back, core, flags, first, count, edge=False):
     anywhere = pl.BlockSpec(memory_space=pl.ANY)
     shape = (2, 48, 3, 8, 512)
     return pl.pallas_call(
-        functools.partial(outer_body, first, count),
+        functools.partial(outer_body, first, count, edge),
         grid_spec=pltpu.PrefetchScalarGridSpec(
-            num_scalar_prefetch=1,
+            num_scalar_prefetch=2,
             grid=(count,),
             in_specs=[
-                band_spec(),
-                band_spec(),
-                pl.BlockSpec((4, 1, 80, 512), lambda s, core: (0, s + first, 0, 0)),
-                fixed_spec((1, 2, WIN, 576)),
-                side_spec((96, 160)),
+                pl.BlockSpec((4, 1, STRIP, 512), lambda s, core, flags: (0, s, 0, 0)),
+                pl.BlockSpec((4, 1, STRIP, 512), lambda s, core, flags: (0, s, 0, 0)),
+                pl.BlockSpec((4, 1, 80, 512), lambda s, core, flags: (0, s + first, 0, 0)),
+                pl.BlockSpec((1, 2, WIN, 576), lambda s, core, flags: (0, 0, 0, 0)),
+                pl.BlockSpec((1, 96, 160), lambda s, core, flags: (core[0], 0, 0)),
             ]
             + [anywhere] * 4,
-            out_specs=[anywhere] * 4 + [fixed_spec((8, 128))],
+            out_specs=[anywhere] * 4,
             scratch_shapes=[
                 pltpu.VMEM((1, 4, WIN, 512), BF16),
                 pltpu.VMEM((4, WIN + 80, 512), BF16),
                 pltpu.VMEM((4, 2, 6 * count, 8, 512), BF16),
                 pltpu.SemaphoreType.DMA((count, 4)),
+                pltpu.VMEM((1, 2, WIN, 576), F32),
             ]
             + work_scratch(2),
         ),
-        out_shape=[jax.ShapeDtypeStruct(shape, BF16)] * 4
-        + [jax.ShapeDtypeStruct((8, 128), F32)],
-        input_output_aliases={6 + index: index for index in range(4)},
+        out_shape=[jax.ShapeDtypeStruct(shape, BF16)] * 4,
+        input_output_aliases={7 + index: index for index in range(4)},
         compiler_params=params(),
         cost_estimate=window_cost(count, count * 2 * MIB),
         name="outer_windows",
-    )(core, own, halo, beside, bias, back, *[x.reshape(shape) for x in partial])
-
-
-def corner_body(core, flags, mid, near, near_halo, far, far_halo, bias, back, p0, p1, p2, p3, o0, o1, o2, o3, win, result, cut, *work):
+    )(core, flags, own, halo, beside, bias, back, *[x.reshape(shape) for x in partial])
+
+
+def corner_body(core, flags, mid, near, near_halo, bias, back, p0, p1, p2, p3, o0, o1, o2, o3, beside, win, result, cut, *work):
     s = pl.program_id(0)
-    left = core[0] == 0
-    for index in range(4):
-        win[1, index] = mid[index, 0]
-    place_pair(win, 0, far, far_halo, jnp.logical_not(left))
-    place_pair(win, 2, near, near_halo, left)
-
-    key_part = lax.broadcasted_iota(jnp.int32, (WIN, 576), 0) % STRIP < HALF
-    query_part = lax.broadcasted_iota(jnp.int32, (WIN, 576), 1) % STRIP < HALF
-    apart = (key_part != query_part) & (flags[s] != 0)
-    for group in range(2):
-        cut[0, group] = jnp.where(apart, -jnp.inf, bias[0, group])
-
-    starts = (
-        pl.multiple_of(2 * WIN * core[0], 16),
-        WIN,
-        pl.multiple_of(2 * WIN * (1 - core[0]), 16),
-    )
+    for index in range(4):
+        win[0, index] = mid[index, 0]
+    place_pair(win, 1, near, near_halo, core[0] == 0)
+    cut_bias(cut, bias, flags[s])
+    starts = (pl.multiple_of(WIN * core[0], 16), pl.multiple_of(WIN * (1 - core[0]), 16))
 
     def keep(slot, index, cols, value):
         result[index, pl.ds(starts[slot], WIN), cols] = value.astype(BF16)
 
-    windows(win, 3, cut, *work, keep)
+    windows(win, 2, cut, *work, keep)
+    used = pl.ds(pl.multiple_of(64 * core[0], 16), 224)
+    near_far = pl.ds(pl.multiple_of(208 * core[0], 16), 80)
     for index, out in enumerate((o0, o1, o2, o3)):
-        full = dot(back[0], result[index, 64:368])
+        beside[index, 0] = result[index, near_far]
+        full = dot(back[0], result[index, used])
         out[:, 0] = full.reshape(2, STRIP, 512).astype(BF16)
 
 
-def corners(partial, flags, mid, near, near_halo, far, far_halo, bias, back, core):
+def corners(partial, flags, mid, near, near_halo, bias, back, core):
     anywhere = pl.BlockSpec(memory_space=pl.ANY)
     shape = (2, 16, STRIP, 512)
 
@@ -529,32 +526,29 @@
                 edge(WIN),
                 edge(STRIP),
                 edge(STRIP),
-                edge(STRIP),
-                edge(STRIP),
                 pl.BlockSpec((1, 2, WIN, 576), lambda s, core, flags: (0, 0, 0, 0)),
-                pl.BlockSpec((1, WIN, 304), lambda s, core, flags: (s, 0, 0)),
+                pl.BlockSpec((1, WIN, 224), lambda s, core, flags: (core[0], s, 0)),
             ]
             + [anywhere] * 4,
             out_specs=[
                 pl.BlockSpec((2, 1, STRIP, 512), lambda s, core, flags: (0, 15 * s, 0, 0))
             ]
-            * 4,
+            * 4
+            + [edge(80)],
             scratch_shapes=[
-                pltpu.VMEM((3, 4, WIN, 512), BF16),
-                pltpu.VMEM((4, 3 * WIN, 512), BF16),
+                pltpu.VMEM((2, 4, WIN, 512), BF16),
+                pltpu.VMEM((4, 2 * WIN, 512), BF16),
                 pltpu.VMEM((1, 2, WIN, 576), F32),
             ]
-            + work_scratch(6),
+            + work_scratch(4),
         ),
-        out_shape=[jax.ShapeDtypeStruct(shape, BF16)] * 4,
-        input_output_aliases={9 + index: index for index in range(4)},
+        out_shape=[jax.ShapeDtypeStruct(shape, BF16)] * 4
+        + [jax.ShapeDtypeStruct((4, 2, 80, 512), BF16)],
+        input_output_aliases={7 + index: index for index in range(4)},
         compiler_params=params(),
-        cost_estimate=window_cost(6, 8 * MIB),
+        cost_estimate=window_cost(4, 8 * MIB),
         name="corner_windows",
-    )(
-        core, flags, mid, near, near_halo, far, far_halo, bias, back,
-        *[x.reshape(shape) for x in partial],
-    )
+    )(core, flags, mid, near, near_halo, bias, back, *[x.reshape(shape) for x in partial])
 
 
 def bias_body(table, hot, squeeze, out, wide, part):
@@ -579,7 +573,7 @@
         out[0, group] = total
 
 
-def window_bias(rel_table):
+def bias_operands(rel_table):
     tokens = (run_bases()[:, None] + np.arange(6)).reshape(WIN)
     hot = np.zeros((4, 384, 4, WIN), np.float32)
     for head in range(4):
@@ -590,28 +584,17 @@
     hot = jnp.asarray(hot.reshape(4 * 384, 4 * WIN), BF16)
     squeeze = jnp.asarray(squeeze.reshape(WIN, 192), BF16)
     table = jnp.pad(rel_table, ((0, 0), (0, 768 - rel_table.shape[1])))
-    return pl.pallas_call(
-        bias_body,
-        out_shape=jax.ShapeDtypeStruct((1, 2, WIN, 576), F32),
-        scratch_shapes=[
-            pltpu.VMEM((2, 192, 4 * 384), F32),
-            pltpu.VMEM((2, 2, 192, 4 * 384), BF16),
-        ],
-        compiler_params=params(),
-        cost_estimate=pl.CostEstimate(
-            flops=4 * 2 * 192 * 1536 * 576, bytes_accessed=3 * MIB, transcendentals=0
-        ),
-        name="window_bias",
-    )(table, hot, squeeze)
+    return table, hot, squeeze
 
 
 def side_tables():
     far_strip, near_strip = (0, 3), (3, 0)
-    far, near, whole, near_back, far_back = [], [], [], [], []
+    far, tiled, whole, near_back, far_back = [], [], [], [], []
     for side in range(2):
         far.append(far_matrix(far_strip[side], 2 * side))
-        near.append(far_matrix(near_strip[side], 2 - 2 * side))
         whole.append(strip_matrix([far_strip[side], near_strip[side], 1, 2]))
+        by_tile = whole[side].reshape(2 * WIN, 12, 3, 8)[:, :, [2 * side, 2 - 2 * side, 1]]
+        tiled.append(by_tile.transpose(0, 2, 1, 3).reshape(2 * WIN, 2 * WIN))
         own = strip_matrix([near_strip[side]]).T
         middle = strip_matrix([1, 2]).T
         pad = np.zeros((2 * WIN, 8), np.float32)
@@ -623,9 +606,7 @@
         else:
             near_back.append(np.concatenate([pad, own, middle], axis=1))
             far_back.append(np.concatenate([far[1].T, pad_far, pad_far, inside], axis=1))
-    natural = strip_matrix([0, 1, 2, 3]).T.reshape(2, WIN, 2 * WIN)
-    corner_back = np.pad(natural, ((0, 0), (0, 0), (8, 8)))
-    stacked = (far, near, whole, near_back, far_back, corner_back)
+    stacked = (tiled, whole, near_back, far_back)
     return [jnp.asarray(np.stack(table), BF16) for table in stacked]
 
 
@@ -640,14 +621,15 @@
         land_mask.astype(F32).reshape(rows, 3, 8, 1), (rows, 3, 8, 128)
     )
     embed = land_embed.reshape(1, width)
-    far_perm, near_perm, all_perm, near_back, far_back, corner_back = side_tables()
-    mid_perm = jnp.asarray(strip_matrix([1, 2]), BF16)
+    edge_perm, all_perm, near_back, far_back = side_tables()
 
     to_far = [((2 * k + 1) % sectors, (2 * k + 2) % sectors) for k in range(sectors // 2)]
     to_far += [(b, a) for a, b in to_far]
     to_near = [(i, i ^ 1) for i in range(sectors)]
 
-    far_a, far_b, near, *edge_rows = pack_edges(arrays, mask, embed, far_perm, near_perm, bands)
+    far_a, far_b, near, mid, *edge_rows, bias = pack_edges(
+        arrays, mask, embed, edge_perm, bias_operands(rel_table), bands
+    )
     top, bottom, below, above = (x.reshape(4, 2, STRIP, width) for x in edge_rows)
     far_halo_a = lax.ppermute(far_a, "lon", to_far)
     far_halo_b = lax.ppermute(far_b, "lon", to_far)
@@ -657,15 +639,15 @@
     far_halo_c = lax.ppermute(far_c, "lon", to_far)
     near_halo_c = lax.ppermute(near_c, "lon", to_near)
 
-    bias = window_bias(rel_table)
-    *partial, beside, _ = inner(
-        arrays, mask, embed, mid_perm, near, near_halo, bias, near_back, core
+    *partial, beside, _ = inner(mid, near, near_halo, bias, near_back, core)
+    flags = jnp.stack([lat == 0, lat == bands - 1]).astype(jnp.int32)
+    *partial, beside_c = corners(
+        partial, flags, mid_c, near_c, near_halo_c, bias, near_back, core
     )
-    *partial, _ = outer(partial, far_a, far_halo_a, beside, bias, far_back, core, 0, 4)
-    *partial, _ = outer(partial, far_b, far_halo_b, beside, bias, far_back, core, 4, 3)
-    flags = jnp.stack([lat == 0, lat == bands - 1]).astype(jnp.int32)
-    final = corners(
-        partial, flags, mid_c, near_c, near_halo_c, far_c, far_halo_c, bias, corner_back, core
+    partial = outer(partial, far_a, far_halo_a, beside, bias, far_back, core, flags, 0, 4)
+    partial = outer(partial, far_b, far_halo_b, beside, bias, far_back, core, flags, 4, 3)
+    final = outer(
+        partial, far_c, far_halo_c, beside_c, bias, far_back, core, flags, 0, 2, edge=True
     )
     return tuple(x.reshape(queries.shape) for x in final)
 

time: 109 us -> 106 us (0.972)
  Pallas kernels: 91.5 us -> 89.3 us
    pallas_call x1, Pallas kernels: 29 us -> 24.9 us  [inner(): pl.pallas_call(inner_body, grid_spec=pltpu.PrefetchScalarGridSpec(num_sca...]
    pallas_call x1, Pallas kernels: 12.1 us -> 9.31 us  [corners(): pl.pallas_call(corner_body, grid_spec=pltpu.PrefetchScalarGridSpec(num_sc...]
    pallas_call x1, Pallas kernels: 21.1 us -> 23.7 us  [pack_edges(): pl.pallas_call(functools.partial(edges_body, bands), in_specs=[anywhere]...]
    pallas_call x3, Pallas kernels: 24.9 us -> 26.9 us  [outer(): pl.pallas_call(functools.partial(outer_body, first, count, edge), grid_sp...]
  transfers between devices with their start and end apart: 5 -> 5, of which waited for: 0 -> 0; matrix products, arithmetic and copies ran while one was open for 1% -> 1% of each run, Pallas kernels for 55% -> 56%
where the time goes in v6:
time: 106 us; the launch traced here: 104 us
  Pallas kernels  89.3 us (84%)
  starting transfers between devices  10.4 us (10%)
  local copies, waits for them, and re-layouts  2.48 us (2%)
  other arithmetic  1.29 us (1%)
    pallas_call x3, Pallas kernels, outer(): pl.pallas_call(functools.partial(outer_body, first, count, edge), grid_sp...  26.9 us
    pallas_call x1, Pallas kernels, inner(): pl.pallas_call(inner_body, grid_spec=pltpu.PrefetchScalarGridSpec(num_sca...  24.9 us
    pallas_call x1, Pallas kernels, pack_edges(): pl.pallas_call(functools.partial(edges_body, bands), in_specs=[anywhere]...  23.7 us
    pallas_call x1, Pallas kernels, corners(): pl.pallas_call(corner_body, grid_spec=pltpu.PrefetchScalarGridSpec(num_sc...  9.31 us
    ppermute x1, starting transfers between devices, shards(): far_halo_a = lax.ppermute(far_a, 'lon', to_far)  4.88 us
    pallas_call x1, Pallas kernels, pack_corners(): pl.pallas_call(corners_body, grid_spec=pltpu.PrefetchScalarGridSpec(num_s...  4.44 us
    ppermute x1, starting transfers between devices, shards(): far_halo_c = lax.ppermute(far_c, 'lon', to_far)  4.38 us
  transfers between devices with their start and end apart: 5, of which 0 were waited for; matrix products, arithmetic and copies ran while one was open for 1% of the time, Pallas kernels for 56%

profile of v6, /device:TPU:8, one launch (start us, length us, event | category | flops | bytes accessed | tf_op | source)
XLA Modules:
  0.0 104.4 jit_solution(8524932579412295337)
XLA Ops:
  0.6 0.7 convert_bitcast_fusion
  1.3 0.1 copy.33
  1.4 1.4 %pad.4.table = f32[8,768]{1,0:T(8,128)} pad(f32[8,759]{1,0:T(8,128)} %param.19, f32[]{:T(128)} %constant.38.clone.1), padding=0_0x0_9 | pad | bytes 48868 | tf_op jit(solution)/shard_map/jit(_pad)/pad | solution.py:586
  2.8 1.0 broadcast_in_dim.8.mask
  3.8 23.7 %pack_edges.1 = (bf16[4,4,72,512]{3,2,1,0:T(8,128)(2,1)}, bf16[4,3,72,512]{3,2,1,0:T(8,128)(2,1)}, bf16[4,7,72,512]{3,2,1,0:T(8,128)(2,1)}, bf16[4,7,144,512]{3,...) custom-call(bf16[2,48,3,8,512]{4,3,2,1,0:T(8,128)(2,1)} %bitcast.30,, ...), custom_call_target="tpu_custom_call" | custom-call | flops 2378170368 | bytes 25165824 | tf_op jit(solution)/shard_map/pack_edges/pallas_call | solution.py:178
  27.6 0.0 copy-start
  27.6 0.1 collective-permute-start.2
  27.7 4.9 %collective-permute-start.4 = (bf16[4,4,72,512]{3,2,1,0:T(8,128)(2,1)}, bf16[4,4,72,512]{3,2,1,0:T(8,128)(2,1)}, u32[]{:S(2)}, u32[]{:S(2)}) collective-permute-start(bf16[4,4,72,512]{3,2,1,0:T(8,128)(2,1)} %get-tuple-element.55.own), channel_id=1, source_target_pairs={{1,2},{3,4},{5,6},{7,8},{9,10},{11,12},{13,14},{15,0},{2,1},{4,3},... | collective-permute-start | bytes 3538952 | tf_op jit(solution)/shard_map/ppermute | solution.py:634
  32.6 4.4 %pack_corners.1 = (bf16[4,2,72,512]{3,2,1,0:T(8,128)(2,1)}, bf16[4,2,72,512]{3,2,1,0:T(8,128)(2,1)}, bf16[4,2,144,512]{3,2,1,0:T(8,128)(2,1)}) custom-call(s32[1]{0:T(128)} %bitcast.core, bf16[4,2,72,512]{3,2,1,0:T(8,128)(2,1)} %bitcast.34, bf16[4,2,72,512]{3,2,1,0:T(8,128)(2,1)} %bitcast.35, bf16[4,2,72,512]{3,2,1,0:T(8,128)(2,1)} %bitcast.36, ...), custom_call_target="tpu_custom_call" | custom-call | flops 679477248 | bytes 5242880 | tf_op jit(solution)/shard_map/pack_corners/pallas_call | solution.py:224
  37.0 0.0 collective-permute-start.1
  37.0 0.0 copy-done
  37.0 1.1 %collective-permute-start.3 = (bf16[4,3,72,512]{3,2,1,0:T(8,128)(2,1)S(1)}, bf16[4,3,72,512]{3,2,1,0:T(8,128)(2,1)}, u32[]{:S(2)}, u32[]{:S(2)}) collective-permute-start(bf16[4,3,72,512]{3,2,1,0:T(8,128)(2,1)S(1)} %copy-done), channel_id=1, source_target_pairs={{1,2},{3,4},{5,6},{7,8},{9,10},{11,12},{13,14},{15,0},{2,1},{4,3},... | collective-permute-start | bytes 2654216 | tf_op jit(solution)/shard_map/ppermute | solution.py:635
  38.1 4.4 %collective-permute-start = (bf16[4,2,72,512]{3,2,1,0:T(8,128)(2,1)}, bf16[4,2,72,512]{3,2,1,0:T(8,128)(2,1)}, u32[]{:S(2)}, u32[]{:S(2)}) collective-permute-start(bf16[4,2,72,512]{3,2,1,0:T(8,128)(2,1)} %get-tuple-element.42.own), channel_id=1, source_target_pairs={{1,2},{3,4},{5,6},{7,8},{9,10},{11,12},{13,14},{15,0},{2,1},{4,3},... | collective-permute-start | bytes 1769480 | tf_op jit(solution)/shard_map/ppermute | solution.py:639
  42.5 0.6 add_convert_fusion.flags
  43.0 0.0 collective-permute-done.2.halo
  43.0 24.9 %inner_windows.1 = (bf16[2,16,72,512]{3,2,1,0:T(8,128)(2,1)}, bf16[2,16,72,512]{3,2,1,0:T(8,128)(2,1)}, bf16[2,16,72,512]{3,2,1,0:T(8,128)(2,1)}, bf16[2,16,72,5...) custom-call(s32[1]{0:T(128)} %bitcast.core, ...), custom_call_target="tpu_custom_call" | custom-call | flops 7134511104 | bytes 25165824 | tf_op jit(solution)/shard_map/inner_windows/pallas_call | solution.py:369
  68.0 0.0 collective-permute-done.1.near_halo
  68.0 9.3 %corner_windows.1 = (bf16[2,16,72,512]{3,2,1,0:T(8,128)(2,1)}, bf16[2,16,72,512]{3,2,1,0:T(8,128)(2,1)}, bf16[2,16,72,512]{3,2,1,0:T(8,128)(2,1)}, bf16[2,16,72,...) custom-call(s32[1]{0:T(128)} %bitcast.core, ...), custom_call_target="tpu_custom_call", output_to_operand_aliasing={{0}: (7, {}), {1}: (8, {}), {2}: (9, {}), {3}: (10, {})} | custom-call | flops 2038431744 | bytes 8388608 | tf_op jit(solution)/shard_map/corner_windows/pallas_call | solution.py:520
  77.3 0.0 collective-permute-done.4.halo
  77.3 11.0 %outer_windows.3 = (bf16[2,48,3,8,512]{4,3,2,1,0:T(8,128)(2,1)}, bf16[2,48,3,8,512]{4,3,2,1,0:T(8,128)(2,1)}, bf16[2,48,3,8,512]{4,3,2,1,0:T(8,128)(2,1)}, bf16[2,48,3,8,512]{4,3,2,1,0:T(8,128)(2,1)}) custom-call(s32[1]{0:T(128)} %bitcast.core, s32[2]{0:T(128)} %add_convert_fusion.flags, ...), custom_call_target="tpu_custom_call", output_to_operand_aliasing={{0}: (7, {}), {1}: (8, {}), {2}: (9, {}), {3}: (10, {})} | custom-call | flops 2038431744 | bytes 8388608 | tf_op jit(solution)/shard_map/outer_windows/pallas_call | solution.py:462
  88.3 0.0 collective-permute-done.3.halo
  88.3 8.9 %outer_windows.4 = (bf16[2,48,3,8,512]{4,3,2,1,0:T(8,128)(2,1)}, bf16[2,48,3,8,512]{4,3,2,1,0:T(8,128)(2,1)}, bf16[2,48,3,8,512]{4,3,2,1,0:T(8,128)(2,1)}, bf16[2,48,3,8,512]{4,3,2,1,0:T(8,128)(2,1)}) custom-call(s32[1]{0:T(128)} %bitcast.core, s32[2]{0:T(128)} %add_convert_fusion.flags, ...), custom_call_target="tpu_custom_call", output_to_operand_aliasing={{0}: (7, {}), {1}: (8, {}), {2}: (9, {}), {3}: (10, {})} | custom-call | flops 1528823808 | bytes 6291456 | tf_op jit(solution)/shard_map/outer_windows/pallas_call | solution.py:462
  97.2 0.0 collective-permute-done.halo
  97.2 7.0 %outer_windows.5 = (bf16[2,48,3,8,512]{4,3,2,1,0:T(8,128)(2,1)}, bf16[2,48,3,8,512]{4,3,2,1,0:T(8,128)(2,1)}, bf16[2,48,3,8,512]{4,3,2,1,0:T(8,128)(2,1)}, bf16[2,48,3,8,512]{4,3,2,1,0:T(8,128)(2,1)}) custom-call(s32[1]{0:T(128)} %bitcast.core, s32[2]{0:T(128)} %add_convert_fusion.flags, ...), custom_call_target="tpu_custom_call", output_to_operand_aliasing={{0}: (7, {}), {1}: (8, {}), {2}: (9, {}), {3}: (10, {})} | custom-call | flops 1019215872 | bytes 4194304 | tf_op jit(solution)/shard_map/outer_windows/pallas_call | solution.py:462
Async XLA Ops:
  27.6 9.4 %copy-start = (bf16[4,3,72,512]{3,2,1,0:T(8,128)(2,1)S(1)}, bf16[4,3,72,512]{3,2,1,0:T(8,128)(2,1)}, u32[]{:S(2)}) copy-start(bf16[4,3,72,512]{3,2,1,0:T(8,128)(2,1)} %get-tuple-element.53.own) | copy-start | bytes 2654212
  27.6 15.4 %collective-permute-start.2 = (bf16[4,7,72,512]{3,2,1,0:T(8,128)(2,1)}, bf16[4,7,72,512]{3,2,1,0:T(8,128)(2,1)}, u32[]{:S(2)}, u32[]{:S(2)}) collective-permute-start(bf16[4,7,72,512]{3,2,1,0:T(8,128)(2,1)} %get-tuple-element.47.own), channel_id=1, source_target_pairs={{0,1},{1,0},{2,3},{3,2},{4,5},{5,4},{6,7},{7,6},{8,9},{9,8},{10,11... | collective-permute-start | bytes 6193160 | tf_op jit(solution)/shard_map/ppermute | solution.py:636
  27.7 49.6 %collective-permute-start.4 = (bf16[4,4,72,512]{3,2,1,0:T(8,128)(2,1)}, bf16[4,4,72,512]{3,2,1,0:T(8,128)(2,1)}, u32[]{:S(2)}, u32[]{:S(2)}) collective-permute-start(bf16[4,4,72,512]{3,2,1,0:T(8,128)(2,1)} %get-tuple-element.55.own), channel_id=1, source_target_pairs={{1,2},{3,4},{5,6},{7,8},{9,10},{11,12},{13,14},{15,0},{2,1},{4,3},... | collective-permute-start | bytes 3538952 | tf_op jit(solution)/shard_map/ppermute | solution.py:634
  37.0 31.0 %collective-permute-start.1 = (bf16[4,2,72,512]{3,2,1,0:T(8,128)(2,1)}, bf16[4,2,72,512]{3,2,1,0:T(8,128)(2,1)}, u32[]{:S(2)}, u32[]{:S(2)}) collective-permute-start(bf16[4,2,72,512]{3,2,1,0:T(8,128)(2,1)} %get-tuple-element.44.near), channel_id=1, source_target_pairs={{0,1},{1,0},{2,3},{3,2},{4,5},{5,4},{6,7},{7,6},{8,9},{9,8},{10,11... | collective-permute-start | bytes 1769480 | tf_op jit(solution)/shard_map/ppermute | solution.py:640
  37.0 51.3 %collective-permute-start.3 = (bf16[4,3,72,512]{3,2,1,0:T(8,128)(2,1)S(1)}, bf16[4,3,72,512]{3,2,1,0:T(8,128)(2,1)}, u32[]{:S(2)}, u32[]{:S(2)}) collective-permute-start(bf16[4,3,72,512]{3,2,1,0:T(8,128)(2,1)S(1)} %copy-done), channel_id=1, source_target_pairs={{1,2},{3,4},{5,6},{7,8},{9,10},{11,12},{13,14},{15,0},{2,1},{4,3},... | collective-permute-start | bytes 2654216 | tf_op jit(solution)/shard_map/ppermute | solution.py:635
  38.1 59.1 %collective-permute-start = (bf16[4,2,72,512]{3,2,1,0:T(8,128)(2,1)}, bf16[4,2,72,512]{3,2,1,0:T(8,128)(2,1)}, u32[]{:S(2)}, u32[]{:S(2)}) collective-permute-start(bf16[4,2,72,512]{3,2,1,0:T(8,128)(2,1)} %get-tuple-element.42.own), channel_id=1, source_target_pairs={{1,2},{3,4},{5,6},{7,8},{9,10},{11,12},{13,14},{15,0},{2,1},{4,3},... | collective-permute-start | bytes 1769480 | tf_op jit(solution)/shard_map/ppermute | solution.py:639

commit v7 on v6

--- a/solution.py
+++ b/solution.py
@@ -411,63 +411,124 @@
         cut[0, group] = jnp.where(apart, -jnp.inf, bias[0, group])
 
 
-def outer_body(first, count, edge, core, flags, own, halo, beside, bias, back, p0, p1, p2, p3, o0, o1, o2, o3, win, result, tiles, gone, cut, *work):
+def outer_body(first, count, edge, core, flags, *refs):
+    inputs = 6 if edge else 3
+    strips, (bias, back) = refs[:inputs], refs[inputs : inputs + 2]
+    outs = refs[inputs + 6 : inputs + 10]
+    win, result, tiles, gone, cut, *work = refs[inputs + 10 :]
     s = pl.program_id(0)
     tile = 2 * core[0]
-    outs = (o0, o1, o2, o3)
-    place_pair(win, 0, own, halo, core[0] == 1)
+    left = core[0] == 1
+    whole = s < count
+    if edge:
+
+        @pl.when(whole)
+        def _():
+            place_pair(win, 0, strips[0], strips[1], left)
+
+        @pl.when(s == 0)
+        def _():
+            cut[...] = bias[...]
+
+        @pl.when(jnp.logical_not(whole))
+        def _():
+            place_pair(win, 0, strips[3], strips[4], left)
+            cut_bias(cut, bias, flags[jnp.maximum(s - count, 0)])
+    else:
+        place_pair(win, 0, strips[0], strips[1], left)
 
     def keep(slot, index, cols, value):
         result[index, 0:WIN, cols] = value.astype(BF16)
 
-    if edge:
-        cut_bias(cut, bias, flags[s])
     windows(win, 1, cut if edge else bias, *work, keep)
 
     def leave(step, index):
-        size, row = (3, 45 * step) if edge else (6, 6 * (step + first) + 3)
         return pltpu.make_async_copy(
-            tiles.at[index, :, pl.ds(6 * step, size)],
-            outs[index].at[:, pl.ds(row, size), tile],
+            tiles.at[index, :, pl.ds(6 * step, 6)],
+            outs[index].at[:, pl.ds(6 * (step + first) + 3, 6), tile],
             gone.at[step, index],
+        )
+
+    def leave_edge(part, index):
+        return pltpu.make_async_copy(
+            tiles.at[index, :, 6 * count + 3 * part : 6 * count + 3 * part + 3],
+            outs[index].at[:, 45 * part : 45 * part + 3, tile],
+            gone.at[count + part, index],
         )
 
     used = pl.ds(pl.multiple_of(64 * (1 - core[0]), 16), 160)
     beside_at = pl.ds(pl.multiple_of(WIN - 64 * core[0], 16), 80)
+    if edge:
+
+        @pl.when(whole)
+        def _():
+            for index in range(4):
+                result[index, beside_at] = strips[2][index, 0]
+
+        @pl.when(jnp.logical_not(whole))
+        def _():
+            for index in range(4):
+                result[index, beside_at] = strips[5][index, 0]
+    else:
+        for index in range(4):
+            result[index, beside_at] = strips[2][index, 0]
+
     for index in range(4):
-        result[index, beside_at] = beside[index, 0]
-        full = dot(back[0], result[index, used]).reshape(2, 2, 3, 8, 512)
+        full = dot(back[0], result[index, used]).reshape(2, 2, 3, 8, 512).astype(BF16)
+
+        def put_band(index=index, full=full):
+            for part in range(2):
+                tiles[index, :, pl.ds(6 * s + 3 * (1 - part), 3)] = full[part]
+            leave(s, index).start()
+
+        if not edge:
+            put_band()
+            continue
+        pl.when(whole)(put_band)
         for part in range(2):
-            if edge:
-
-                @pl.when(s == part)
-                def _(part=part, full=full, index=index):
-                    tiles[index, :, 6 * part : 6 * part + 3] = full[part].astype(BF16)
-
-                continue
-            span = pl.ds(6 * s + 3 * (1 - part), 3)
-            tiles[index, :, span] = full[part].astype(BF16)
-        leave(s, index).start()
-
-    @pl.when(s == count - 1)
+
+            @pl.when(s == count + part)
+            def _(part=part, index=index, full=full):
+                row = 6 * count + 3 * part
+                tiles[index, :, row : row + 3] = full[part]
+                leave_edge(part, index).start()
+
+    @pl.when(s == count + (2 if edge else 0) - 1)
     def _():
         for index in range(4):
             for step in range(count):
                 leave(step, index).wait()
-
-
-def outer(partial, own, halo, beside, bias, back, core, flags, first, count, edge=False):
+            if edge:
+                for part in range(2):
+                    leave_edge(part, index).wait()
+
+
+def outer(partial, strips, bias, back, core, flags, first, count):
+    edge = len(strips) == 6
+    steps = count + (2 if edge else 0)
     anywhere = pl.BlockSpec(memory_space=pl.ANY)
     shape = (2, 48, 3, 8, 512)
+
+    def band(size, shift=0):
+        return pl.BlockSpec(
+            (4, 1, size, 512), lambda s, core, flags: (0, jnp.minimum(s, count - 1) + shift, 0, 0)
+        )
+
+    def corner(size):
+        return pl.BlockSpec(
+            (4, 1, size, 512), lambda s, core, flags: (0, jnp.maximum(s - count, 0), 0, 0)
+        )
+
+    specs = [band(STRIP), band(STRIP), band(80, first)]
+    if edge:
+        specs += [corner(STRIP), corner(STRIP), corner(80)]
     return pl.pallas_call(
         functools.partial(outer_body, first, count, edge),
         grid_spec=pltpu.PrefetchScalarGridSpec(
             num_scalar_prefetch=2,
-            grid=(count,),
-            in_specs=[
-                pl.BlockSpec((4, 1, STRIP, 512), lambda s, core, flags: (0, s, 0, 0)),
-                pl.BlockSpec((4, 1, STRIP, 512), lambda s, core, flags: (0, s, 0, 0)),
-                pl.BlockSpec((4, 1, 80, 512), lambda s, core, flags: (0, s + first, 0, 0)),
+            grid=(steps,),
+            in_specs=specs
+            + [
                 pl.BlockSpec((1, 2, WIN, 576), lambda s, core, flags: (0, 0, 0, 0)),
                 pl.BlockSpec((1, 96, 160), lambda s, core, flags: (core[0], 0, 0)),
             ]
@@ -476,18 +537,18 @@
             scratch_shapes=[
                 pltpu.VMEM((1, 4, WIN, 512), BF16),
                 pltpu.VMEM((4, WIN + 80, 512), BF16),
-                pltpu.VMEM((4, 2, 6 * count, 8, 512), BF16),
-                pltpu.SemaphoreType.DMA((count, 4)),
+                pltpu.VMEM((4, 2, 6 * steps, 8, 512), BF16),
+                pltpu.SemaphoreType.DMA((steps, 4)),
                 pltpu.VMEM((1, 2, WIN, 576), F32),
             ]
             + work_scratch(2),
         ),
         out_shape=[jax.ShapeDtypeStruct(shape, BF16)] * 4,
-        input_output_aliases={7 + index: index for index in range(4)},
+        input_output_aliases={len(strips) + 4 + index: index for index in range(4)},
         compiler_params=params(),
-        cost_estimate=window_cost(count, count * 2 * MIB),
+        cost_estimate=window_cost(steps, steps * 2 * MIB),
         name="outer_windows",
-    )(core, flags, own, halo, beside, bias, back, *[x.reshape(shape) for x in partial])
+    )(core, flags, *strips, bias, back, *[x.reshape(shape) for x in partial])
 
 
 def corner_body(core, flags, mid, near, near_halo, bias, back, p0, p1, p2, p3, o0, o1, o2, o3, beside, win, result, cut, *work):
@@ -644,11 +705,11 @@
     *partial, beside_c = corners(
         partial, flags, mid_c, near_c, near_halo_c, bias, near_back, core
     )
-    partial = outer(partial, far_a, far_halo_a, beside, bias, far_back, core, flags, 0, 4)
-    partial = outer(partial, far_b, far_halo_b, beside, bias, far_back, core, flags, 4, 3)
-    final = outer(
-        partial, far_c, far_halo_c, beside_c, bias, far_back, core, flags, 0, 2, edge=True
+    partial = outer(
+        partial, (far_a, far_halo_a, beside), bias, far_back, core, flags, 0, 4
     )
+    late = (far_b, far_halo_b, beside, far_c, far_halo_c, beside_c)
+    final = outer(partial, late, bias, far_back, core, flags, 4, 3)
     return tuple(x.reshape(queries.shape) for x in final)
 
 

time: 106 us -> 106 us (level)
  the two profiles are of different devices: /device:TPU:8 before, /device:TPU:1 now
where the time goes in v7:
time: 106 us
  Pallas kernels  88.7 us (84%)
  starting transfers between devices  9.77 us (9%)
  waiting for transfers between devices  2.92 us (3%)
  local copies, waits for them, and re-layouts  2.48 us (2%)
  other arithmetic  1.38 us (1%)
    pallas_call x1, Pallas kernels, pack_edges(): pl.pallas_call(functools.partial(edges_body, bands), in_specs=[anywhere]...  25.2 us
    pallas_call x1, Pallas kernels, inner(): pl.pallas_call(inner_body, grid_spec=pltpu.PrefetchScalarGridSpec(num_sca...  24.9 us
    pallas_call x2, Pallas kernels, outer(): pl.pallas_call(functools.partial(outer_body, first, count, edge), grid_sp...  24.9 us
    pallas_call x1, Pallas kernels, corners(): pl.pallas_call(corner_body, grid_spec=pltpu.PrefetchScalarGridSpec(num_sc...  9.29 us
    pallas_call x1, Pallas kernels, pack_corners(): pl.pallas_call(corners_body, grid_spec=pltpu.PrefetchScalarGridSpec(num_s...  4.44 us
    ppermute x1, starting transfers between devices, shards(): far_halo_b = lax.ppermute(far_b, 'lon', to_far)  3.25 us
    ppermute x1, waiting for transfers between devices, shards(): far_halo_b = lax.ppermute(far_b, 'lon', to_far)  2.91 us
    ppermute x1, starting transfers between devices, shards(): near_halo_c = lax.ppermute(near_c, 'lon', to_near)  2.61 us
  transfers between devices with their start and end apart: 5, of which 1 were waited for; matrix products, arithmetic and copies ran while one was open for 1% of the time, Pallas kernels for 47%

profile of v7, /device:TPU:1, one launch (start us, length us, event | category | flops | bytes accessed | tf_op | source)
XLA Modules:
  0.0 106.1 jit_solution(17707480426747862562)
XLA Ops:
  0.6 0.7 convert_bitcast_fusion
  1.3 0.1 copy.29
  1.4 1.4 %pad.4.table = f32[8,768]{1,0:T(8,128)} pad(f32[8,759]{1,0:T(8,128)} %param.19, f32[]{:T(128)} %constant.38.clone.1), padding=0_0x0_9 | pad | bytes 48868 | tf_op jit(solution)/shard_map/jit(_pad)/pad | solution.py:647
  2.8 1.0 broadcast_in_dim.8.mask
  3.8 25.2 %pack_edges.1 = (bf16[4,4,72,512]{3,2,1,0:T(8,128)(2,1)}, bf16[4,3,72,512]{3,2,1,0:T(8,128)(2,1)}, bf16[4,7,72,512]{3,2,1,0:T(8,128)(2,1)}, bf16[4,7,144,512]{3,...) custom-call(bf16[2,48,3,8,512]{4,3,2,1,0:T(8,128)(2,1)} %bitcast.30,, ...), custom_call_target="tpu_custom_call" | custom-call | flops 2378170368 | bytes 25165824 | tf_op jit(solution)/shard_map/pack_edges/pallas_call | solution.py:178
  29.0 0.0 copy-start
  29.0 1.3 %collective-permute-start.1 = (bf16[4,7,72,512]{3,2,1,0:T(8,128)(2,1)}, bf16[4,7,72,512]{3,2,1,0:T(8,128)(2,1)}, u32[]{:S(2)}, u32[]{:S(2)}) collective-permute-start(bf16[4,7,72,512]{3,2,1,0:T(8,128)(2,1)} %get-tuple-element.36.own), channel_id=1, source_target_pairs={{0,1},{1,0},{2,3},{3,2},{4,5},{5,4},{6,7},{7,6},{8,9},{9,8},{10,11... | collective-permute-start | bytes 6193160 | tf_op jit(solution)/shard_map/ppermute | solution.py:697
  30.3 2.6 %collective-permute-start.4 = (bf16[4,4,72,512]{3,2,1,0:T(8,128)(2,1)}, bf16[4,4,72,512]{3,2,1,0:T(8,128)(2,1)}, u32[]{:S(2)}, u32[]{:S(2)}) collective-permute-start(bf16[4,4,72,512]{3,2,1,0:T(8,128)(2,1)} %get-tuple-element.51.refs_0_), channel_id=1, source_target_pairs={{1,2},{3,4},{5,6},{7,8},{9,10},{11,12},{13,14},{15,0},{2,1},{4,3},... | collective-permute-start | bytes 3538952 | tf_op jit(solution)/shard_map/ppermute | solution.py:695
  32.9 4.4 %pack_corners.1 = (bf16[4,2,72,512]{3,2,1,0:T(8,128)(2,1)}, bf16[4,2,72,512]{3,2,1,0:T(8,128)(2,1)}, bf16[4,2,144,512]{3,2,1,0:T(8,128)(2,1)}) custom-call(s32[1]{0:T(128)} %bitcast.core, bf16[4,2,72,512]{3,2,1,0:T(8,128)(2,1)} %bitcast.34, bf16[4,2,72,512]{3,2,1,0:T(8,128)(2,1)} %bitcast.35, bf16[4,2,72,512]{3,2,1,0:T(8,128)(2,1)} %bitcast.36, ...), custom_call_target="tpu_custom_call" | custom-call | flops 679477248 | bytes 5242880 | tf_op jit(solution)/shard_map/pack_corners/pallas_call | solution.py:224
  37.4 2.6 %collective-permute-start.3 = (bf16[4,2,72,512]{3,2,1,0:T(8,128)(2,1)}, bf16[4,2,72,512]{3,2,1,0:T(8,128)(2,1)}, u32[]{:S(2)}, u32[]{:S(2)}) collective-permute-start(bf16[4,2,72,512]{3,2,1,0:T(8,128)(2,1)} %get-tuple-element.45.near), channel_id=1, source_target_pairs={{0,1},{1,0},{2,3},{3,2},{4,5},{5,4},{6,7},{7,6},{8,9},{9,8},{10,11... | collective-permute-start | bytes 1769480 | tf_op jit(solution)/shard_map/ppermute | solution.py:701
  40.0 0.0 collective-permute-start.2
  40.0 0.0 copy-done
  40.0 3.2 %collective-permute-start = (bf16[4,3,72,512]{3,2,1,0:T(8,128)(2,1)S(1)}, bf16[4,3,72,512]{3,2,1,0:T(8,128)(2,1)}, u32[]{:S(2)}, u32[]{:S(2)}) collective-permute-start(bf16[4,3,72,512]{3,2,1,0:T(8,128)(2,1)S(1)} %copy-done), channel_id=1, source_target_pairs={{1,2},{3,4},{5,6},{7,8},{9,10},{11,12},{13,14},{15,0},{2,1},{4,3},... | collective-permute-start | bytes 2654216 | tf_op jit(solution)/shard_map/ppermute | solution.py:696
  43.2 0.7 add_convert_fusion.flags
  43.9 0.0 collective-permute-done.1.halo
  43.9 24.9 %inner_windows.1 = (bf16[2,16,72,512]{3,2,1,0:T(8,128)(2,1)}, bf16[2,16,72,512]{3,2,1,0:T(8,128)(2,1)}, bf16[2,16,72,512]{3,2,1,0:T(8,128)(2,1)}, bf16[2,16,72,5...) custom-call(s32[1]{0:T(128)} %bitcast.core, ...), custom_call_target="tpu_custom_call" | custom-call | flops 7134511104 | bytes 25165824 | tf_op jit(solution)/shard_map/inner_windows/pallas_call | solution.py:369
  68.8 0.0 collective-permute-done.3.near_halo
  68.8 9.3 %corner_windows.1 = (bf16[2,16,72,512]{3,2,1,0:T(8,128)(2,1)}, bf16[2,16,72,512]{3,2,1,0:T(8,128)(2,1)}, bf16[2,16,72,512]{3,2,1,0:T(8,128)(2,1)}, bf16[2,16,72,...) custom-call(s32[1]{0:T(128)} %bitcast.core, ...), custom_call_target="tpu_custom_call", output_to_operand_aliasing={{0}: (7, {}), {1}: (8, {}), {2}: (9, {}), {3}: (10, {})} | custom-call | flops 2038431744 | bytes 8388608 | tf_op jit(solution)/shard_map/corner_windows/pallas_call | solution.py:581
  78.1 0.0 collective-permute-done.4.refs_1_
  78.1 10.9 %outer_windows.2 = (bf16[2,48,3,8,512]{4,3,2,1,0:T(8,128)(2,1)}, bf16[2,48,3,8,512]{4,3,2,1,0:T(8,128)(2,1)}, bf16[2,48,3,8,512]{4,3,2,1,0:T(8,128)(2,1)}, bf16[2,48,3,8,512]{4,3,2,1,0:T(8,128)(2,1)}) custom-call(s32[1]{0:T(128)} %bitcast.core, s32[2]{0:T(128)} %add_convert_fusion.flags, ...), custom_call_target="tpu_custom_call", output_to_operand_aliasing={{0}: (7, {}), {1}: (8, {}), {2}: (9, {}), {3}: (10, {})} | custom-call | flops 2038431744 | bytes 8388608 | tf_op jit(solution)/shard_map/outer_windows/pallas_call | solution.py:525
  89.1 0.0 collective-permute-done.2.refs_4_
  89.1 2.9 %collective-permute-done.refs_1_ = bf16[4,3,72,512]{3,2,1,0:T(8,128)(2,1)} collective-permute-done((bf16[4,3,72,512]{3,2,1,0:T(8,128)(2,1)S(1)}, bf16[4,3,72,512]{3,2,1,0:T(8,128)(2,1)}, u32[]{:S(2)}, u32[]{:S(2)}) %collective-permute-start) | collective-permute-done | bytes 884768 | tf_op jit(solution)/shard_map/ppermute | solution.py:696
  92.0 13.9 %outer_windows.3 = (bf16[2,48,3,8,512]{4,3,2,1,0:T(8,128)(2,1)}, bf16[2,48,3,8,512]{4,3,2,1,0:T(8,128)(2,1)}, bf16[2,48,3,8,512]{4,3,2,1,0:T(8,128)(2,1)}, bf16[2,48,3,8,512]{4,3,2,1,0:T(8,128)(2,1)}) custom-call(s32[1]{0:T(128)} %bitcast.core, s32[2]{0:T(128)} %add_convert_fusion.flags, ...), custom_call_target="tpu_custom_call", output_to_operand_aliasing={{0}: (10, {}), {1}: (11, {}), {2}: (12, {}), {3}: (13, {})} | custom-call | flops 2548039680 | bytes 10485760 | tf_op jit(solution)/shard_map/outer_windows/pallas_call | solution.py:525
Async XLA Ops:
  29.0 11.0 %copy-start = (bf16[4,3,72,512]{3,2,1,0:T(8,128)(2,1)S(1)}, bf16[4,3,72,512]{3,2,1,0:T(8,128)(2,1)}, u32[]{:S(2)}) copy-start(bf16[4,3,72,512]{3,2,1,0:T(8,128)(2,1)} %get-tuple-element.34.refs_0_) | copy-start | bytes 2654212
  29.0 14.9 %collective-permute-start.1 = (bf16[4,7,72,512]{3,2,1,0:T(8,128)(2,1)}, bf16[4,7,72,512]{3,2,1,0:T(8,128)(2,1)}, u32[]{:S(2)}, u32[]{:S(2)}) collective-permute-start(bf16[4,7,72,512]{3,2,1,0:T(8,128)(2,1)} %get-tuple-element.36.own), channel_id=1, source_target_pairs={{0,1},{1,0},{2,3},{3,2},{4,5},{5,4},{6,7},{7,6},{8,9},{9,8},{10,11... | collective-permute-start | bytes 6193160 | tf_op jit(solution)/shard_map/ppermute | solution.py:697
  30.3 47.8 %collective-permute-start.4 = (bf16[4,4,72,512]{3,2,1,0:T(8,128)(2,1)}, bf16[4,4,72,512]{3,2,1,0:T(8,128)(2,1)}, u32[]{:S(2)}, u32[]{:S(2)}) collective-permute-start(bf16[4,4,72,512]{3,2,1,0:T(8,128)(2,1)} %get-tuple-element.51.refs_0_), channel_id=1, source_target_pairs={{1,2},{3,4},{5,6},{7,8},{9,10},{11,12},{13,14},{15,0},{2,1},{4,3},... | collective-permute-start | bytes 3538952 | tf_op jit(solution)/shard_map/ppermute | solution.py:695
  37.4 31.5 %collective-permute-start.3 = (bf16[4,2,72,512]{3,2,1,0:T(8,128)(2,1)}, bf16[4,2,72,512]{3,2,1,0:T(8,128)(2,1)}, u32[]{:S(2)}, u32[]{:S(2)}) collective-permute-start(bf16[4,2,72,512]{3,2,1,0:T(8,128)(2,1)} %get-tuple-element.45.near), channel_id=1, source_target_pairs={{0,1},{1,0},{2,3},{3,2},{4,5},{5,4},{6,7},{7,6},{8,9},{9,8},{10,11... | collective-permute-start | bytes 1769480 | tf_op jit(solution)/shard_map/ppermute | solution.py:701
  40.0 49.1 %collective-permute-start.2 = (bf16[4,2,72,512]{3,2,1,0:T(8,128)(2,1)}, bf16[4,2,72,512]{3,2,1,0:T(8,128)(2,1)}, u32[]{:S(2)}, u32[]{:S(2)}) collective-permute-start(bf16[4,2,72,512]{3,2,1,0:T(8,128)(2,1)} %get-tuple-element.43.refs_3_), channel_id=1, source_target_pairs={{1,2},{3,4},{5,6},{7,8},{9,10},{11,12},{13,14},{15,0},{2,1},{4,3},... | collective-permute-start | bytes 1769480 | tf_op jit(solution)/shard_map/ppermute | solution.py:700
  40.0 52.0 %collective-permute-start = (bf16[4,3,72,512]{3,2,1,0:T(8,128)(2,1)S(1)}, bf16[4,3,72,512]{3,2,1,0:T(8,128)(2,1)}, u32[]{:S(2)}, u32[]{:S(2)}) collective-permute-start(bf16[4,3,72,512]{3,2,1,0:T(8,128)(2,1)S(1)} %copy-done), channel_id=1, source_target_pairs={{1,2},{3,4},{5,6},{7,8},{9,10},{11,12},{13,14},{15,0},{2,1},{4,3},... | collective-permute-start | bytes 2654216 | tf_op jit(solution)/shard_map/ppermute | solution.py:696
